TPU v7x, 128 devices: a whole 4x4x4 slice. The times are simulated.
128 devices in a mesh: tile: 16 (over z, y), seq: 8 (over x, core).
Axes of the slice: x: 4, y: 4, z: 4, core: 2. Of those that a mesh axis runs over, the one named last changes fastest.
Arguments:
- cls_tokens: bfloat16 [16384, 1536], P(('tile', 'seq')), may hold values from -6 to 6
- norm_gain: float32 [1536], replicated, may hold values from 0.5 to 1.5
- w_gate: bfloat16 [1536, 4096], P(None, 'tile'), may hold values from -0.15625 to 0.15625
- w_up: bfloat16 [1536, 4096], P(None, 'tile'), may hold values from -0.15625 to 0.15625
- w_down: bfloat16 [4096, 1536], P('tile'), may hold values from -0.09375 to 0.09375
- layer_scale: float32 [1536], replicated, may hold values from 0.25 to 1.75
- final_gain: float32 [1536], replicated, may hold values from 0.5 to 1.5
- w_embed: bfloat16 [1536, 768], replicated, may hold values from -0.15625 to 0.15625
- dest_pos: int32 [16384], P(('tile', 'seq')), may hold values from 0 to 16383, as said below
- tile_coords: int32 [2, 16384], P(None, ('tile', 'seq')), may hold values from 0 to 999
- attn_gain: float32 [768], replicated, may hold values from 0.5 to 1.5
- w_qkv: bfloat16 [768, 2304], replicated, may hold values from -4 to 4
- offsets: int32 [12], replicated, may hold values from 0 to 15
- w_out: bfloat16 [768, 768], replicated, may hold values from -0.21875 to 0.21875
Outputs:
- slide_out: bfloat16 [16384, 768], P(('tile', 'seq'))
Inputs may be any that keep to these rules, and one draw needn't show every extreme that they name: dest_pos holds each number of 0 to 16383 once; the 128 rows of one device go to the devices of the slide order in groups of 0, 1 or 2 rows a device, some pair carrying 2; every device receives 128 rows, 2 of them from the device 128 / 2 places before it in the slide order, counted round.
All inputs are finite; a program needn't handle non-finite values.
Results may differ from a plain program's by a relative error of at most 0.018.
Values may be sent and summed in bfloat16 or wider, within the bound.
No kernel may reach another device: no remote copies, remote signals or barrier semaphores. Data moves between devices by JAX's collectives and lax.ppermute only.
A program may use at most 128 MiB of HBM per device.

v0:
```python
import jax
import jax.numpy as jnp
from jax import lax
from jax.sharding import PartitionSpec as P

HEAD_COUNT = 12
HEAD_WIDTH = 64
SEGMENT_SPACING = 16


def layer_norm(sender_rows, gain):
    average = jnp.mean(sender_rows, axis=-1, keepdims=True)
    centered = sender_rows - average
    variance = jnp.mean(centered * centered, axis=-1, keepdims=True)
    return centered * lax.rsqrt(variance + 1e-06) * gain


def position_table(coords, hidden_width):
    quarter = hidden_width // 4
    frequency = 1.0 / 10000.0 ** (jnp.arange(quarter).astype(jnp.float32) / quarter)
    along_x = coords[:, 0:1].astype(jnp.float32) * frequency[None, :]
    along_y = coords[:, 1:2].astype(jnp.float32) * frequency[None, :]
    return jnp.concatenate(
        [jnp.sin(along_x), jnp.cos(along_x), jnp.sin(along_y), jnp.cos(along_y)], axis=1
    )


def attend(queries, key_rows, values):
    score_scale = queries.shape[-1] ** (-0.5)
    scores = (
        jnp.einsum("qhd,khd->hqk", queries, key_rows, preferred_element_type=jnp.float32)
        * score_scale
    )
    highest = jnp.max(scores, axis=-1, keepdims=True)
    weights = jnp.exp(scores - highest)
    totals = jnp.sum(weights, axis=-1, keepdims=True)
    mixed_rows = jnp.einsum(
        "hqk,khd->qhd", weights.astype(jnp.bfloat16), values, preferred_element_type=jnp.float32
    )
    result = mixed_rows / jnp.transpose(totals, (1, 0, 2))
    logsum = jnp.transpose((highest + jnp.log(totals))[:, :, 0])
    return (result, logsum)


def body(
    cls_tokens,
    norm_gain,
    w_gate,
    w_up,
    w_down,
    layer_scale,
    final_gain,
    w_embed,
    dest_pos,
    tile_coords,
    attn_gain,
    w_qkv,
    offsets,
    w_out,
):
    resident_rows = cls_tokens.shape[0]
    tokens = cls_tokens.astype(jnp.float32)
    normed = layer_norm(tokens, norm_gain).astype(jnp.bfloat16)
    shard_rows = lax.all_gather(normed, "tile", axis=0, tiled=True)
    gate_proj = jnp.dot(shard_rows, w_gate, preferred_element_type=jnp.float32)
    upward = jnp.dot(shard_rows, w_up, preferred_element_type=jnp.float32)
    hidden = (jax.nn.silu(gate_proj) * upward).astype(jnp.bfloat16)
    projected = lax.psum_scatter(
        jnp.dot(hidden, w_down, preferred_element_type=jnp.float32),
        "tile",
        scatter_dimension=0,
        tiled=True,
    )
    mixed_rows = tokens + layer_scale * projected
    final_rows = layer_norm(mixed_rows, final_gain).astype(jnp.bfloat16)
    embedded = jnp.dot(final_rows, w_embed, preferred_element_type=jnp.float32).astype(jnp.bfloat16)
    hidden_width = embedded.shape[1]
    tile_count = lax.axis_size("tile")
    seq_count = lax.axis_size("seq")
    devices = tile_count * seq_count
    capacity = 2 * max(1, resident_rows // devices)
    target = dest_pos // resident_rows
    row_ids = jnp.arange(resident_rows)
    earlier = (target[:, None] == target[None, :]) & (row_ids[None, :] < row_ids[:, None])
    slot_index = jnp.sum(earlier.astype(jnp.int32), axis=1)
    where_to = target * capacity + slot_index
    payload = jnp.zeros((devices * capacity, hidden_width), jnp.bfloat16).at[where_to].set(embedded)
    meta_rows = jnp.stack([dest_pos, tile_coords[0], tile_coords[1]], axis=1)
    meta_table = jnp.full((devices * capacity, 3), -1, jnp.int32).at[where_to].set(meta_rows)
    received, received_meta = (
        lax.all_to_all(
            payload.reshape(devices, capacity, hidden_width),
            ("tile", "seq"),
            split_axis=0,
            concat_axis=0,
            tiled=True,
        ),
        lax.all_to_all(
            meta_table.reshape(devices, capacity, 3),
            ("tile", "seq"),
            split_axis=0,
            concat_axis=0,
            tiled=True,
        ),
    )
    flat_rows = received.reshape(-1, hidden_width)
    flat_meta = received_meta.reshape(-1, 3)
    is_live = flat_meta[:, 0] >= 0
    local_slot = jnp.where(is_live, flat_meta[:, 0] % resident_rows, resident_rows)
    placed = (
        jnp.zeros((resident_rows, hidden_width), jnp.bfloat16)
        .at[local_slot]
        .set(flat_rows, mode="drop")
    )
    coords = (
        jnp.zeros((resident_rows, 2), jnp.int32).at[local_slot].set(flat_meta[:, 1:], mode="drop")
    )
    seq_in = placed.astype(jnp.float32) + position_table(coords, hidden_width)
    normed_seq = layer_norm(seq_in, attn_gain).astype(jnp.bfloat16)
    qkv = jnp.dot(normed_seq, w_qkv, preferred_element_type=jnp.float32).astype(jnp.bfloat16)
    queries = qkv[:, :hidden_width]
    keys_values = qkv[:, hidden_width:]
    segment_kv = lax.all_gather(keys_values, "seq", axis=0, tiled=True)
    near_out, nearby_logsumexp = attend(
        queries.reshape(resident_rows, HEAD_COUNT, HEAD_WIDTH),
        segment_kv[:, :hidden_width].reshape(-1, HEAD_COUNT, HEAD_WIDTH),
        segment_kv[:, hidden_width:].reshape(-1, HEAD_COUNT, HEAD_WIDTH),
    )
    kept_rows = jnp.arange(SEGMENT_SPACING, dtype=jnp.int32)[:, None] == offsets[None, :]

    def select(sender_rows, stacked_rows):
        head_grouped = sender_rows.reshape(
            resident_rows // SEGMENT_SPACING, SEGMENT_SPACING, stacked_rows, HEAD_COUNT, HEAD_WIDTH
        )
        sampled_rows = jnp.sum(
            jnp.where(
                kept_rows[None, :, None, :, None], head_grouped, jnp.zeros((), sender_rows.dtype)
            ),
            axis=1,
        )
        return sampled_rows.reshape(resident_rows // SEGMENT_SPACING, stacked_rows * hidden_width)

    far_kv = lax.all_gather(select(keys_values, 2), ("tile", "seq"), axis=0, tiled=True)
    far_out, far_lse = attend(
        select(queries, 1).reshape(-1, HEAD_COUNT, HEAD_WIDTH),
        far_kv[:, :hidden_width].reshape(-1, HEAD_COUNT, HEAD_WIDTH),
        far_kv[:, hidden_width:].reshape(-1, HEAD_COUNT, HEAD_WIDTH),
    )
    far_full = jnp.where(kept_rows[None, :, :, None], far_out[:, None], 0.0).reshape(
        resident_rows, HEAD_COUNT, HEAD_WIDTH
    )
    nearby_grouped = nearby_logsumexp.reshape(
        resident_rows // SEGMENT_SPACING, SEGMENT_SPACING, HEAD_COUNT
    )
    far_share = jnp.where(
        kept_rows[None], 1.0 / (1.0 + jnp.exp(nearby_grouped - far_lse[:, None])), 0.0
    ).reshape(resident_rows, HEAD_COUNT)
    combined = (1.0 - far_share)[:, :, None] * near_out + far_share[:, :, None] * far_full
    attn_rows = combined.reshape(resident_rows, hidden_width).astype(jnp.bfloat16)
    return (seq_in + jnp.dot(attn_rows, w_out, preferred_element_type=jnp.float32)).astype(
        jnp.bfloat16
    )


def solution(mesh):
    in_specs = (
        P(("tile", "seq"), None),
        P(),
        P(None, "tile"),
        P(None, "tile"),
        P("tile", None),
        P(),
        P(),
        P(),
        P(("tile", "seq")),
        P(None, ("tile", "seq")),
        P(),
        P(),
        P(),
        P(),
    )
    out_specs = P(("tile", "seq"), None)
    return jax.shard_map(body, mesh=mesh, in_specs=in_specs, out_specs=out_specs, check_vma=False)
```

profile of v0, /device:TPU:1, one launch (start us, length us, event | category | flops | bytes accessed | tf_op | source)
XLA Modules:
  0.0 357.2 jit_solution(11485548192163310712)
XLA Ops:
  9.1 2.0 fusion.33
  11.2 64.7 %all-gather.4.cloned.1.call-done = bf16[2048,1536]{1,0:T(8,128)(2,1)} async-done(((bf16[128,1536]{1,0:T(8,128)(2,1)}), bf16[2048,1536]{1,0:T(8,128)(2,1)}) %all-gather.4.cloned.1.call-update) | async-done | bytes 6291472 | tf_op jit(solution)/shard_map/all_gather | solution.py:64
  75.9 6.1 %fusion.70 = f32[2048,256]{1,0:T(8,128)} fusion(bf16[2048,1536]{1,0:T(8,128)(2,1)} %all-gather.4.cloned.1.call-done, bf16[1536,256]{1,0:T(8,128)(2,1)} %param.16), kind=kOutput, calls=%fused_computation.112 | convolution fusion | flops 1610612736 | bytes 9175040 | tf_op jit(solution)/shard_map/dot_general | solution.py:65
  82.0 14.6 %fusion.7 = f32[2048,1536]{1,0:T(8,128)} fusion(bf16[256,1536]{1,0:T(8,128)(2,1)} %param.18, bf16[2048,1536]{1,0:T(8,128)(2,1)} %all-gather.4.cloned.1.call-done, bf16[1536,256]{1,0:T(8,128)(2,1)} %param.17, f32[2048,256]{1,0:T(8,128)} %fusion.70), kind=kOutput, calls=%fused_computation.14 | convolution fusion | flops 3224371200 | bytes 22544384 | tf_op jit(solution)/shard_map/dot_general | solution.py:69
  103.8 8.3 %all-to-all-start = ((s32[128,2,3]{2,1,0:T(2,128)}), s32[128,2,3]{2,1,0:T(2,128)}, u32[]{:S(2)}, u32[]{:S(2)}) async-start(s32[128,2,3]{2,1,0:T(2,128)} %bitcast.76), calls=%async_computation | async-start | bytes 262144 | tf_op jit(solution)/shard_map/all_to_all | solution.py:98
  112.8 9.2 %all-to-all-done = s32[128,2,3]{2,1,0:T(2,128)} async-done(((s32[128,2,3]{2,1,0:T(2,128)}), s32[128,2,3]{2,1,0:T(2,128)}, u32[]{:S(2)}, u32[]{:S(2)}) %all-to-all-start) | async-done | bytes 3104 | tf_op jit(solution)/shard_map/all_to_all | solution.py:98
  123.5 68.9 %reduce-scatter.2.cloned.1.call-done = f32[128,1536]{1,0:T(8,128)} async-done(((f32[2048,1536]{1,0:T(8,128)}), f32[128,1536]{1,0:T(8,128)}) %reduce-scatter.2.cloned.1.call-update) | async-done | bytes 786448 | tf_op jit(solution)/shard_map/reduce_scatter | solution.py:68
  195.4 2.9 convolution_convert_fusion.1
  198.3 2.3 scatter_custom_fusion.1
  200.6 1.9 reshape.194
  202.5 7.8 %all-to-all-start.1 = ((bf16[128,2,768]{2,1,0:T(2,128)(2,1)}), bf16[128,2,768]{2,1,0:T(2,128)(2,1)}, u32[]{:S(2)}, u32[]{:S(2)}) async-start(bf16[128,2,768]{2,1,0:T(2,128)(2,1)} %reshape.194), calls=%async_computation.2 | async-start | bytes 786432 | tf_op jit(solution)/shard_map/all_to_all | solution.py:91
  211.0 2.2 scatter_custom_fusion.3
  214.3 2.5 multiply_sine_fusion.1
  216.7 5.6 %all-to-all-done.1 = bf16[128,2,768]{2,1,0:T(2,128)(2,1)} async-done(((bf16[128,2,768]{2,1,0:T(2,128)(2,1)}), bf16[128,2,768]{2,1,0:T(2,128)(2,1)}, u32[]{:S(2)}, u32[]{:S(2)}) %all-to-all-start.1) | async-done | bytes 393248 | tf_op jit(solution)/shard_map/all_to_all | solution.py:91
  222.3 1.9 reshape.224
  224.2 2.7 scatter_custom_fusion.2
  231.0 2.6 reshape.199
  233.5 2.2 select_reduce_fusion
  242.8 2.1 reshape.198
  246.8 8.7 %all-gather.6.cloned.1.call-done = bf16[1024,1536]{1,0:T(8,128)(2,1)} async-done(((bf16[128,1536]{1,0:T(8,128)(2,1)}), bf16[1024,1536]{1,0:T(8,128)(2,1)}) %all-gather.6.cloned.1.call-update) | async-done | bytes 3145744 | tf_op jit(solution)/shard_map/all_gather | solution.py:123
  255.4 3.8 %fusion.68 = (bf16[1024,768]{1,0:T(8,128)(2,1)}, bf16[1024,768]{1,0:T(8,128)(2,1)}) fusion(bf16[1024,1536]{1,0:T(8,128)(2,1)} %all-gather.6.cloned.1.call-done), kind=kLoop, calls=%fused_computation.110 | loop fusion | bytes 6291456 | tf_op jit(solution)/shard_map/slice | solution.py:126
  259.2 2.6 copy.82
  261.9 2.6 copy.85
  264.5 2.6 multiply_reduce_fusion
  267.1 2.7 copy-done.1
  271.7 52.7 %all-gather.8.cloned.1.call-done = bf16[1024,1536]{1,0:T(8,128)(2,1)} async-done(((bf16[8,1536]{1,0:T(8,128)(2,1)}), bf16[1024,1536]{1,0:T(8,128)(2,1)}) %all-gather.8.cloned.1.call-update) | async-done | bytes 3145744 | tf_op jit(solution)/shard_map/all_gather | solution.py:143
  324.3 3.8 %fusion.67 = (bf16[1024,768]{1,0:T(8,128)(2,1)}, bf16[1024,768]{1,0:T(8,128)(2,1)}) fusion(bf16[1024,1536]{1,0:T(8,128)(2,1)} %all-gather.8.cloned.1.call-done), kind=kLoop, calls=%fused_computation.109 | loop fusion | bytes 6291456 | tf_op jit(solution)/shard_map/slice | solution.py:146
  328.1 2.6 copy.83
  336.2 2.6 copy.86
  338.8 2.1 fusion.15
  341.9 2.1 copy.89
  344.8 4.8 %fusion.26 = bf16[128,12,64]{0,2,1:T(8,128)(2,1)S(1)} fusion(bf16[1024,12,64]{0,2,1:T(8,128)(2,1)} %bitcast.74, f32[12,128,1024]{2,1,0:T(8,128)} %copy-done.1, f32[12,128]{1,0:T(8,128)S(1)} %get-tuple-element.23, f32[128,12,64]{0,2,1:T(8,128)} %copy.89, f32[128,12]{0,1:T(8,128)S(1)} %get-tuple-element.8, f32[128,12]{0,1:T(8,128)} %bitcast.79, ...), kind=kOutput, calls=%fused_computation.33 | convolution fusion | flops 206635008 | bytes 8480256 | tf_op jit(solution)/shard_map/hqk,khd->qhd/dot_general | solution.py:37
  (77 shorter events, 39.8 us)
Async XLA Ops:
  6.5 222.0 %copy-start = (bf16[768,2304]{1,0:T(8,128)(2,1)S(1)}, bf16[768,2304]{1,0:T(8,128)(2,1)}, u32[]{:S(2)}) copy-start(bf16[768,2304]{1,0:T(8,128)(2,1)} %param.25) | copy-start | bytes 10616836
  6.5 69.4 %all-gather.4.cloned.1.call-start = ((), (), s32[]{:S(2)}) async-start(), calls=%async_computation.3 | async-start | bytes 6684672 | tf_op jit(solution)/shard_map/all_gather | solution.py:64
  11.1 181.2 %reduce-scatter.2.cloned.1.call-start = ((), (), s32[]{:S(2)}) async-start(), calls=%async_computation.4 | async-start | bytes 13369344 | tf_op jit(solution)/shard_map/reduce_scatter | solution.py:68
  96.6 95.8 %copy-start.9 = (f32[1536]{0:T(1024)S(1)}, f32[1536]{0:T(1024)}, u32[]{:S(2)}) copy-start(f32[1536]{0:T(1024)} %param.19) | copy-start | bytes 18436
  96.6 98.8 %copy-start.11 = (f32[1536]{0:T(1024)S(1)}, f32[1536]{0:T(1024)}, u32[]{:S(2)}) copy-start(f32[1536]{0:T(1024)} %param.20) | copy-start | bytes 18436
  103.8 18.1 %all-to-all-start = ((s32[128,2,3]{2,1,0:T(2,128)}), s32[128,2,3]{2,1,0:T(2,128)}, u32[]{:S(2)}, u32[]{:S(2)}) async-start(s32[128,2,3]{2,1,0:T(2,128)} %bitcast.76), calls=%async_computation | async-start | bytes 262144 | tf_op jit(solution)/shard_map/all_to_all | solution.py:98
  192.4 3.0 copy-start.2
  192.4 3.0 copy-start.3
  200.6 28.0 %copy-start.12 = (f32[768]{0:T(1024)S(1)}, f32[768]{0:T(1024)}, u32[]{:S(2)}) copy-start(f32[768]{0:T(1024)} %param.24) | copy-start | bytes 9220
  202.5 19.8 %all-to-all-start.1 = ((bf16[128,2,768]{2,1,0:T(2,128)(2,1)}), bf16[128,2,768]{2,1,0:T(2,128)(2,1)}, u32[]{:S(2)}, u32[]{:S(2)}) async-start(bf16[128,2,768]{2,1,0:T(2,128)(2,1)} %reshape.194), calls=%async_computation.2 | async-start | bytes 786432 | tf_op jit(solution)/shard_map/all_to_all | solution.py:91
  210.3 45.2 %all-gather.6.cloned.1.call-start = ((), (), s32[]{:S(2)}) async-start(), calls=%async_computation.5 | async-start | bytes 3538944 | tf_op jit(solution)/shard_map/all_gather | solution.py:123
  228.3 0.9 copy-start.4
  228.5 2.4 copy-start.13
  229.2 0.8 copy-start.7
  230.9 93.4 %all-gather.8.cloned.1.call-start = ((), (), s32[]{:S(2)}) async-start(), calls=%async_computation.6 | async-start | bytes 3170304 | tf_op jit(solution)/shard_map/all_gather | solution.py:143
  267.1 2.7 copy-start.1
  332.5 0.7 copy-start.6
  333.5 0.6 copy-start.10
  344.8 4.8 %copy-start.5 = (f32[128,768]{1,0:T(8,128)S(1)}, f32[128,768]{1,0:T(8,128)}, u32[]{:S(2)}) copy-start(f32[128,768]{1,0:T(8,128)} %copy-done.4) | copy-start | bytes 1179652
  344.8 4.8 %copy-start.8 = (bf16[768,768]{1,0:T(8,128)(2,1)S(1)}, bf16[768,768]{1,0:T(8,128)(2,1)}, u32[]{:S(2)}) copy-start(bf16[768,768]{1,0:T(8,128)(2,1)} %param.27) | copy-start | bytes 3538948
Sparse Core Ops, SparseCore 0:
  11.3 64.6 all-gather.3
  96.7 95.5 reduce-scatter.1
  231.0 24.3 all-gather.5
  258.4 65.8 all-gather.7
where the time goes:
time: 358 us; the launch traced here: 357 us
  waiting for transfers between devices  210 us (59%)
  local copies, waits for them, and re-layouts  56.9 us (16%)
  matrix products  36.7 us (10%)
  other arithmetic  24.2 us (7%)
  starting transfers between devices  16.2 us (5%)
  between operations  13.4 us (4%)
    reduce_scatter x1, waiting for transfers between devices, body(): lax.psum_scatter(jnp.dot(hidden, w_down, preferred_element_type=jnp.float...  68.9 us
    all_gather x1, waiting for transfers between devices, body(): shard_rows = lax.all_gather(normed, 'tile', axis=0, tiled=True)  64.7 us
    all_gather x1, waiting for transfers between devices, body(): lax.all_gather(select(keys_values, 2), ('tile', 'seq'), axis=0, tiled=True)  52.7 us
    dot_general x1, matrix products, body(): jnp.dot(hidden, w_down, preferred_element_type=jnp.float32)  14.6 us
    all_to_all x1, waiting for transfers between devices, body(): lax.all_to_all(meta_table.reshape(devices, capacity, 3), ('tile', 'seq'),...  9.2 us
    all_gather x1, waiting for transfers between devices, body(): segment_kv = lax.all_gather(keys_values, 'seq', axis=0, tiled=True)  8.69 us
    all_to_all x1, starting transfers between devices, body(): lax.all_to_all(meta_table.reshape(devices, capacity, 3), ('tile', 'seq'),...  8.32 us
    all_to_all x1, starting transfers between devices, body(): lax.all_to_all(payload.reshape(devices, capacity, hidden_width), ('tile',...  7.79 us
  transfers between devices with their start and end apart: 6, of which 6 were waited for; matrix products, arithmetic and copies ran while one was open for 13% of the time, Pallas kernels for 0%

commit v1 on v0

--- a/solution.py
+++ b/solution.py
@@ -1,11 +1,47 @@
+import functools
+
 import jax
 import jax.numpy as jnp
 from jax import lax
+from jax.experimental import pallas as pl
+from jax.experimental.pallas import tpu as pltpu
 from jax.sharding import PartitionSpec as P
 
 HEAD_COUNT = 12
 HEAD_WIDTH = 64
 SEGMENT_SPACING = 16
+RING = 4
+CORES = 2
+AXES = ("tile", "seq")
+VMEM = pl.BlockSpec(memory_space=pltpu.VMEM)
+PARAMS = pltpu.CompilerParams(vmem_limit_bytes=48 * 1024 * 1024)
+
+
+def device_at(z, y, x, c):
+    return ((z * RING + y) * RING + x) * CORES + c
+
+
+def shift(value, z=0, y=0, x=0, c=0):
+    pairs = []
+    for zi in range(RING):
+        for yi in range(RING):
+            for xi in range(RING):
+                for ci in range(CORES):
+                    to = device_at((zi + z) % RING, (yi + y) % RING, (xi + x) % RING, (ci + c) % CORES)
+                    pairs.append((device_at(zi, yi, xi, ci), to))
+    return lax.ppermute(value, AXES, pairs)
+
+
+def call(kernel, outs, *args, flops=0):
+    nbytes = sum(a.size * a.dtype.itemsize for a in (*args, *outs))
+    return pl.pallas_call(
+        kernel,
+        out_shape=outs,
+        in_specs=[VMEM] * len(args),
+        out_specs=tuple(VMEM for _ in outs),
+        compiler_params=PARAMS,
+        cost_estimate=pl.CostEstimate(flops=flops, bytes_accessed=nbytes, transcendentals=0),
+    )(*args)
 
 
 def layer_norm(sender_rows, gain):
@@ -13,6 +49,128 @@
     centered = sender_rows - average
     variance = jnp.mean(centered * centered, axis=-1, keepdims=True)
     return centered * lax.rsqrt(variance + 1e-06) * gain
+
+
+def dot(a, b):
+    return jnp.dot(a, b, preferred_element_type=jnp.float32)
+
+
+def norm_kernel(x_ref, gain_ref, out_ref):
+    out_ref[...] = layer_norm(x_ref[...].astype(jnp.float32), gain_ref[...]).astype(jnp.bfloat16)
+
+
+def gated(gate, up):
+    return (gate / (1.0 + jnp.exp(-gate)) * up).astype(jnp.bfloat16)
+
+
+def mlp_own_kernel(x0, x1, x2, x3, gate_ref, up_ref, down_ref, rows_ref, total_ref):
+    for n, x in enumerate((x0, x1, x2, x3)):
+        rows_ref[128 * n : 128 * (n + 1), :] = x[...]
+    for n in range(2):
+        part = slice(256 * n, 256 * (n + 1))
+        rows = rows_ref[part, :]
+        hidden = gated(dot(rows, gate_ref[...]), dot(rows, up_ref[...]))
+        total_ref[part, :] = dot(hidden, down_ref[...])
+
+
+def chunk_hidden(rows, top_ref, bottom_ref):
+    both = dot(rows[:, :1152], top_ref[...]) + dot(rows[:, 1152:], bottom_ref[:384, :])
+    return gated(both[:, :128], both[:, 128:])
+
+
+def mlp_chunks(rows_ref, part, chunks):
+    rows = rows_ref[part, :]
+    hidden = [chunk_hidden(rows, top, bottom) for top, bottom in chunks]
+    out = []
+    for j in range(6):
+        block = slice(384 + 128 * j, 512 + 128 * j)
+        add = None
+        for n in range(0, len(chunks), 2):
+            pair = jnp.concatenate([hidden[n], hidden[n + 1]], axis=1)
+            down = jnp.concatenate([chunks[n][1][block, :], chunks[n + 1][1][block, :]], axis=0)
+            term = dot(pair, down)
+            add = term if add is None else add + term
+        out.append(add)
+    return out
+
+
+def mlp_middle_kernel(rows_ref, total_ref, a0, b0, a1, b1, a2, b2, a3, b3, out_ref):
+    for n in range(2):
+        part = slice(256 * n, 256 * (n + 1))
+        blocks = mlp_chunks(rows_ref, part, ((a0, b0), (a1, b1), (a2, b2), (a3, b3)))
+        for j in range(6):
+            cols = slice(256 * j, 256 * (j + 1))
+            out_ref[part, cols] = total_ref[part, cols] + blocks[j]
+
+
+def mlp_last_kernel(rows_ref, total_ref, a0, b0, a1, b1, own_ref, r1, r2, r3):
+    for n in range(2):
+        part = slice(256 * n, 256 * (n + 1))
+        blocks = mlp_chunks(rows_ref, part, ((a0, b0), (a1, b1)))
+        for j in range(6):
+            cols = slice(256 * j, 256 * (j + 1))
+            value = total_ref[part, cols] + blocks[j]
+            for k, ref in enumerate((own_ref, r1) if n == 0 else (r2, r3)):
+                ref[:, cols] = value[128 * k : 128 * (k + 1)].astype(ref.dtype)
+
+
+def encoder_mlp(cls_tokens, norm_gain, w_gate, w_up, w_down):
+    core = lax.axis_index("seq") % CORES
+    f32, bf16 = jnp.float32, jnp.bfloat16
+    half = w_gate.shape[1] // CORES
+    both = jnp.concatenate(
+        [
+            lax.dynamic_slice_in_dim(w_gate, core * half, half, 1),
+            lax.dynamic_slice_in_dim(w_up, core * half, half, 1),
+        ],
+        axis=1,
+    )
+    down = lax.dynamic_slice_in_dim(w_down, core * half, half, 0)
+    top = both[:1152]
+    bottom = jnp.concatenate([both[1152:]] + [down[:, 256 * j : 256 * (j + 1)] for j in range(6)], axis=0)
+    before_top, before_bottom = shift(top, z=1), shift(bottom, z=1)
+    after_bottom, after_top = shift(bottom, z=-1), shift(top, z=-1)
+    across_top, across_bottom = shift(before_top, z=1), shift(after_bottom, z=-1)
+
+    (normed,) = call(norm_kernel, [jax.ShapeDtypeStruct(cls_tokens.shape, bf16)], cls_tokens, norm_gain[None])
+    gathered = [normed, shift(normed, y=1), shift(normed, y=-1), shift(normed, y=2)]
+    rows, total = call(
+        mlp_own_kernel,
+        [jax.ShapeDtypeStruct((512, 1536), bf16), jax.ShapeDtypeStruct((512, 1536), f32)],
+        *gathered,
+        w_gate,
+        w_up,
+        w_down,
+        flops=2 * 512 * 1536 * 768,
+    )
+    swap = functools.partial(shift, c=1)
+    (total,) = call(
+        mlp_middle_kernel,
+        [jax.ShapeDtypeStruct((512, 1536), f32)],
+        rows,
+        total,
+        before_top,
+        before_bottom,
+        after_top,
+        after_bottom,
+        swap(before_top),
+        swap(before_bottom),
+        swap(after_top),
+        swap(after_bottom),
+        flops=4 * 512 * 1536 * 768,
+    )
+    own, back_1, fore_1, back_2 = call(
+        mlp_last_kernel,
+        [jax.ShapeDtypeStruct((128, 1536), t) for t in (f32, bf16, bf16, bf16)],
+        rows,
+        total,
+        across_top,
+        across_bottom,
+        swap(across_top),
+        swap(across_bottom),
+        flops=2 * 512 * 1536 * 768,
+    )
+    return own, shift(back_1, y=-1), shift(fore_1, y=1), shift(back_2, y=2)
 
 
 def position_table(coords, hidden_width):
@@ -60,17 +218,8 @@
 ):
     resident_rows = cls_tokens.shape[0]
     tokens = cls_tokens.astype(jnp.float32)
-    normed = layer_norm(tokens, norm_gain).astype(jnp.bfloat16)
-    shard_rows = lax.all_gather(normed, "tile", axis=0, tiled=True)
-    gate_proj = jnp.dot(shard_rows, w_gate, preferred_element_type=jnp.float32)
-    upward = jnp.dot(shard_rows, w_up, preferred_element_type=jnp.float32)
-    hidden = (jax.nn.silu(gate_proj) * upward).astype(jnp.bfloat16)
-    projected = lax.psum_scatter(
-        jnp.dot(hidden, w_down, preferred_element_type=jnp.float32),
-        "tile",
-        scatter_dimension=0,
-        tiled=True,
-    )
+    terms = encoder_mlp(cls_tokens, norm_gain, w_gate, w_up, w_down)
+    projected = terms[0] + terms[1].astype(jnp.float32) + terms[2].astype(jnp.float32) + terms[3].astype(jnp.float32)
     mixed_rows = tokens + layer_scale * projected
     final_rows = layer_norm(mixed_rows, final_gain).astype(jnp.bfloat16)
     embedded = jnp.dot(final_rows, w_embed, preferred_element_type=jnp.float32).astype(jnp.bfloat16)

time: 358 us -> 280 us (0.78)
  waiting for transfers between devices: 210 us -> 92.9 us
  starting transfers between devices: 16.2 us -> 49.3 us
  matrix products: 36.7 us -> 12.9 us
  Pallas kernels: 0 us -> 17.4 us
  local copies, waits for them, and re-layouts: 56.9 us -> 73.1 us
  other arithmetic: 24.2 us -> 19.1 us
    reduce_scatter x1 -> x0, waiting for transfers between devices: 68.9 us -> none  [body(): lax.psum_scatter(jnp.dot(hidden, w_down, preferred_element_type=jnp.float...]
    all_gather x1 -> x0, waiting for transfers between devices: 64.7 us -> none  [body(): shard_rows = lax.all_gather(normed, 'tile', axis=0, tiled=True)]
    ppermute x0 -> x18, starting transfers between devices: none -> 35.6 us  [shift(): return lax.ppermute(value, AXES, pairs)]
    dot_general x2 -> x0, matrix products: 20.7 us -> none  [the longest x1 14.6 us: body(): jnp.dot(hidden, w_down, preferred_element_type=jnp.float32)]
    pallas_call x0 -> x4, Pallas kernels: none -> 17.4 us  [call(): pl.pallas_call(kernel, out_shape=outs, in_specs=[VMEM] * len(args), out_s...]
    ppermute x0 -> x18, waiting for transfers between devices: none -> 15.3 us  [shift(): return lax.ppermute(value, AXES, pairs)]
    unnamed x29 -> x52, local copies, waits for them, and re-layouts: 6.38 us -> 19.1 us
  transfers between devices with their start and end apart: 6 -> 22, of which waited for: 6 -> 10; matrix products, arithmetic and copies ran while one was open for 13% -> 19% of each run, Pallas kernels for 0% -> 4%
where the time goes in v1:
time: 280 us; the launch traced here: 278 us
  waiting for transfers between devices  92.9 us (33%)
  local copies, waits for them, and re-layouts  73.1 us (26%)
  starting transfers between devices  49.3 us (18%)
  other arithmetic  19.1 us (7%)
  Pallas kernels  17.4 us (6%)
  between operations  13.8 us (5%)
  matrix products  12.9 us (5%)
    all_gather x1, waiting for transfers between devices, body(): lax.all_gather(select(keys_values, 2), ('tile', 'seq'), axis=0, tiled=True)  53.5 us
    ppermute x18, starting transfers between devices, shift(): return lax.ppermute(value, AXES, pairs)  35.6 us
    unnamed x52, local copies, waits for them, and re-layouts  19.1 us
    pallas_call x4, Pallas kernels, call(): pl.pallas_call(kernel, out_shape=outs, in_specs=[VMEM] * len(args), out_s...  17.4 us
    ppermute x18, waiting for transfers between devices, shift(): return lax.ppermute(value, AXES, pairs)  15.3 us
    all_to_all x1, waiting for transfers between devices, body(): lax.all_to_all(meta_table.reshape(devices, capacity, 3), ('tile', 'seq'),...  9.26 us
    all_gather x1, waiting for transfers between devices, body(): segment_kv = lax.all_gather(keys_values, 'seq', axis=0, tiled=True)  8.47 us
    all_to_all x1, starting transfers between devices, body(): lax.all_to_all(meta_table.reshape(devices, capacity, 3), ('tile', 'seq'),...  8.06 us
  transfers between devices with their start and end apart: 22, of which 10 were waited for; matrix products, arithmetic and copies ran while one was open for 19% of the time, Pallas kernels for 4%

profile of v1, /device:TPU:1, one launch (start us, length us, event | category | flops | bytes accessed | tf_op | source)
XLA Modules:
  0.0 278.4 jit_solution(13953856524958350056)
XLA Ops:
  30.2 2.7 collective-permute-start.5
  32.9 2.4 collective-permute-start.7
  35.2 4.2 %collective-permute-done.2.x3 = bf16[128,1536]{1,0:T(8,128)(2,1)S(1)} collective-permute-done((bf16[128,1536]{1,0:T(8,128)(2,1)}, bf16[128,1536]{1,0:T(8,128)(2,1)S(1)}, u32[]{:S(2)}, u32[]{:S(2)}) %collective-permute-start.2) | collective-permute-done | bytes 393248 | tf_op jit(solution)/shard_map/ppermute | solution.py:32
  40.3 3.3 %collective-permute-start.12 = (bf16[1152,256]{1,0:T(8,128)(2,1)S(1)}, bf16[1152,256]{1,0:T(8,128)(2,1)S(1)}, u32[]{:S(2)}, u32[]{:S(2)}) collective-permute-start(bf16[1152,256]{1,0:T(8,128)(2,1)S(1)} %collective-permute-done.6.b1), channel_id=1, source_target_pairs={{0,96},{1,97},{2,98},{3,99},{4,100},{5,101},{6,102},{7,103},{8,104... | collective-permute-start | bytes 1769480 | tf_op jit(solution)/shard_map/ppermute | solution.py:32
  44.6 5.0 %collective-permute-start.10 = (bf16[1152,256]{1,0:T(8,128)(2,1)S(1)}, bf16[1152,256]{1,0:T(8,128)(2,1)S(1)}, u32[]{:S(2)}, u32[]{:S(2)}) collective-permute-start(bf16[1152,256]{1,0:T(8,128)(2,1)S(1)} %collective-permute-done.6.b1), channel_id=1, source_target_pairs={{0,1},{1,0},{2,3},{3,2},{4,5},{5,4},{6,7},{7,6},{8,9},{9,8},{10,11... | collective-permute-start | bytes 1769480 | tf_op jit(solution)/shard_map/ppermute | solution.py:32
  49.7 3.3 %collective-permute-done.5.a1 = bf16[1152,256]{1,0:T(8,128)(2,1)S(1)} collective-permute-done((bf16[1152,256]{1,0:T(8,128)(2,1)}, bf16[1152,256]{1,0:T(8,128)(2,1)S(1)}, u32[]{:S(2)}, u32[]{:S(2)}) %collective-permute-start.5) | collective-permute-done | bytes 589856 | tf_op jit(solution)/shard_map/ppermute | solution.py:32
  53.0 4.0 %collective-permute-start.8 = (bf16[1152,256]{1,0:T(8,128)(2,1)S(1)}, bf16[1152,256]{1,0:T(8,128)(2,1)S(1)}, u32[]{:S(2)}, u32[]{:S(2)}) collective-permute-start(bf16[1152,256]{1,0:T(8,128)(2,1)S(1)} %collective-permute-done.4.b0), channel_id=1, source_target_pairs={{0,1},{1,0},{2,3},{3,2},{4,5},{5,4},{6,7},{7,6},{8,9},{9,8},{10,11... | collective-permute-start | bytes 1769480 | tf_op jit(solution)/shard_map/ppermute | solution.py:32
  57.3 2.7 collective-permute-start.13
  60.0 5.6 %collective-permute-done.12.b0 = bf16[1152,256]{1,0:T(8,128)(2,1)S(1)} collective-permute-done((bf16[1152,256]{1,0:T(8,128)(2,1)S(1)}, bf16[1152,256]{1,0:T(8,128)(2,1)S(1)}, u32[]{:S(2)}, u32[]{:S(2)}) %collective-permute-start.12) | collective-permute-done | bytes 589856 | tf_op jit(solution)/shard_map/ppermute | solution.py:32
  72.0 4.5 %shard_map.137 = (bf16[512,1536]{1,0:T(8,128)(2,1)S(1)}, f32[512,1536]{1,0:T(8,128)}) custom-call(bf16[128,1536]{1,0:T(8,128)(2,1)} %shard_map.136.x0, bf16[128,1536]{1,0:T(8,128)(2,1)} %collective-permute-done.x1, bf16[128,1536]{1,0:T(8,128)(2,1)} %collective-permute-done.1.x2, bf16[128,1536]{1,0:T(8,128)(2,1)S(1)} %collective-permute-done.2.x3, ...), custom_call_target="tpu_custom_call" | custom-call | flops 1207959552 | bytes 8650752 | tf_op jit(solution)/shard_map/pallas_call | solution.py:37
  77.6 7.4 %shard_map.138.total_ref = f32[512,1536]{1,0:T(8,128)} custom-call(bf16[512,1536]{1,0:T(8,128)(2,1)} %copy-done.1, f32[512,1536]{1,0:T(8,128)} %get-tuple-element.12.total_ref, bf16[1152,256]{1,0:T(8,128)(2,1)} %collective-permute-done.3.a0, bf16[1152,256]{1,0:T(8,128)(2,1)S(1)} %collective-permute-done.4.b0, ...), custom_call_target="tpu_custom_call" | custom-call | flops 2415919104 | bytes 12582912 | tf_op jit(solution)/shard_map/pallas_call | solution.py:37
  85.0 4.5 %shard_map.139 = (f32[128,1536]{1,0:T(8,128)S(1)}, bf16[128,1536]{1,0:T(8,128)(2,1)}, bf16[128,1536]{1,0:T(8,128)(2,1)}, bf16[128,1536]{1,0:T(8,128)(2,1)}) custom-call(bf16[512,1536]{1,0:T(8,128)(2,1)S(1)} %copy-done.2, f32[512,1536]{1,0:T(8,128)} %shard_map.138.total_ref, bf16[1152,256]{1,0:T(8,128)(2,1)S(1)} %collective-permute-done.11.a0, ...), custom_call_target="tpu_custom_call" | custom-call | flops 1207959552 | bytes 9043968 | tf_op jit(solution)/shard_map/pallas_call | solution.py:37
  92.5 2.3 collective-permute-start.15
  99.8 8.1 %all-to-all-start = ((s32[128,2,3]{2,1,0:T(2,128)}), s32[128,2,3]{2,1,0:T(2,128)}, u32[]{:S(2)}, u32[]{:S(2)}) async-start(s32[128,2,3]{2,1,0:T(2,128)} %bitcast.71), calls=%async_computation | async-start | bytes 262144 | tf_op jit(solution)/shard_map/all_to_all | solution.py:247
  108.4 9.3 %all-to-all-done = s32[128,2,3]{2,1,0:T(2,128)} async-done(((s32[128,2,3]{2,1,0:T(2,128)}), s32[128,2,3]{2,1,0:T(2,128)}, u32[]{:S(2)}, u32[]{:S(2)}) %all-to-all-start) | async-done | bytes 3104 | tf_op jit(solution)/shard_map/all_to_all | solution.py:247
  122.8 2.3 scatter_custom_fusion.1
  127.0 5.3 %all-to-all-start.1 = ((bf16[128,2,768]{2,1,0:T(2,128)(2,1)}), bf16[128,2,768]{2,1,0:T(2,128)(2,1)}, u32[]{:S(2)}, u32[]{:S(2)}) async-start(bf16[128,2,768]{2,1,0:T(2,128)(2,1)} %reshape.181), calls=%async_computation.1 | async-start | bytes 786432 | tf_op jit(solution)/shard_map/all_to_all | solution.py:240
  135.7 2.4 multiply_sine_fusion.1
  138.1 6.3 %all-to-all-done.1 = bf16[128,2,768]{2,1,0:T(2,128)(2,1)} async-done(((bf16[128,2,768]{2,1,0:T(2,128)(2,1)}), bf16[128,2,768]{2,1,0:T(2,128)(2,1)}, u32[]{:S(2)}, u32[]{:S(2)}) %all-to-all-start.1) | async-done | bytes 393248 | tf_op jit(solution)/shard_map/all_to_all | solution.py:240
  146.3 2.7 scatter_custom_fusion.2
  153.2 2.6 reshape.186
  169.0 8.5 %all-gather.3.cloned.1.call-done = bf16[1024,1536]{1,0:T(8,128)(2,1)} async-done(((bf16[128,1536]{1,0:T(8,128)(2,1)}), bf16[1024,1536]{1,0:T(8,128)(2,1)}) %all-gather.3.cloned.1.call-update) | async-done | bytes 3145744 | tf_op jit(solution)/shard_map/all_gather | solution.py:272
  177.5 3.8 %fusion.58 = (bf16[1024,768]{1,0:T(8,128)(2,1)}, bf16[1024,768]{1,0:T(8,128)(2,1)}) fusion(bf16[1024,1536]{1,0:T(8,128)(2,1)} %all-gather.3.cloned.1.call-done), kind=kLoop, calls=%fused_computation.106 | loop fusion | bytes 6291456 | tf_op jit(solution)/shard_map/slice | solution.py:275
  181.3 2.6 copy.85
  183.9 2.6 copy.82
  186.5 2.6 multiply_reduce_fusion
  189.1 2.7 copy-done.8
  193.1 53.5 %all-gather.5.cloned.1.call-done = bf16[1024,1536]{1,0:T(8,128)(2,1)} async-done(((bf16[8,1536]{1,0:T(8,128)(2,1)}), bf16[1024,1536]{1,0:T(8,128)(2,1)}) %all-gather.5.cloned.1.call-update) | async-done | bytes 3145744 | tf_op jit(solution)/shard_map/all_gather | solution.py:292
  246.6 3.8 %fusion.57 = (bf16[1024,768]{1,0:T(8,128)(2,1)}, bf16[1024,768]{1,0:T(8,128)(2,1)}) fusion(bf16[1024,1536]{1,0:T(8,128)(2,1)} %all-gather.5.cloned.1.call-done), kind=kLoop, calls=%fused_computation.105 | loop fusion | bytes 6291456 | tf_op jit(solution)/shard_map/slice | solution.py:295
  250.4 2.6 copy.86
  253.0 2.6 copy.83
  265.7 4.8 %fusion.20 = bf16[128,12,64]{0,2,1:T(8,128)(2,1)S(1)} fusion(bf16[1024,12,64]{0,2,1:T(8,128)(2,1)} %bitcast.69, f32[12,128,1024]{2,1,0:T(8,128)} %copy-done.8, f32[12,128]{1,0:T(8,128)S(1)} %get-tuple-element.37, f32[128,12,64]{0,2,1:T(8,128)} %copy.89, f32[128,12]{0,1:T(8,128)S(1)} %get-tuple-element.20, f32[128,12]{0,1:T(8,128)S(1)} %bitcast.74, ...), kind=kOutput, calls=%fused_computation.23 | convolution fusion | flops 206635008 | bytes 8480256 | tf_op jit(solution)/shard_map/hqk,khd->qhd/dot_general | solution.py:195
  (132 shorter events, 83.9 us)
Async XLA Ops:
  6.5 144.1 %copy-start = (bf16[768,2304]{1,0:T(8,128)(2,1)S(1)}, bf16[768,2304]{1,0:T(8,128)(2,1)}, u32[]{:S(2)}) copy-start(bf16[768,2304]{1,0:T(8,128)(2,1)} %param.25) | copy-start | bytes 10616836
  9.6 20.6 %collective-permute-start = (bf16[128,1536]{1,0:T(8,128)(2,1)}, bf16[128,1536]{1,0:T(8,128)(2,1)}, u32[]{:S(2)}, u32[]{:S(2)}) collective-permute-start(bf16[128,1536]{1,0:T(8,128)(2,1)} %shard_map.136.x0), channel_id=1, source_target_pairs={{0,8},{1,9},{2,10},{3,11},{4,12},{5,13},{6,14},{7,15},{8,16},{9,17... | collective-permute-start | bytes 1179656 | tf_op jit(solution)/shard_map/ppermute | solution.py:32
  11.8 18.4 %collective-permute-start.1 = (bf16[128,1536]{1,0:T(8,128)(2,1)}, bf16[128,1536]{1,0:T(8,128)(2,1)}, u32[]{:S(2)}, u32[]{:S(2)}) collective-permute-start(bf16[128,1536]{1,0:T(8,128)(2,1)} %shard_map.136.x0), channel_id=1, source_target_pairs={{0,24},{1,25},{2,26},{3,27},{4,28},{5,29},{6,30},{7,31},{8,0},{9,1... | collective-permute-start | bytes 1179656 | tf_op jit(solution)/shard_map/ppermute | solution.py:32
  13.2 43.8 %copy-start.20 = (s32[128]{0:T(128)S(1)}, s32[128]{0:T(128)}, u32[]{:S(2)}) copy-start(s32[128]{0:T(128)} %param.22) | copy-start | bytes 1540
  13.2 55.4 %copy-start.19 = (s32[2,128]{1,0:T(2,128)S(1)}, s32[2,128]{1,0:T(2,128)}, u32[]{:S(2)}) copy-start(s32[2,128]{1,0:T(2,128)} %param.23) | copy-start | bytes 3076
  15.3 17.6 %collective-permute-start.3 = (bf16[1152,256]{1,0:T(8,128)(2,1)}, bf16[1152,256]{1,0:T(8,128)(2,1)}, u32[]{:S(2)}, u32[]{:S(2)}) collective-permute-start(bf16[1152,256]{1,0:T(8,128)(2,1)} %fusion.23), channel_id=1, source_target_pairs={{0,32},{1,33},{2,34},{3,35},{4,36},{5,37},{6,38},{7,39},{8,40},{9,... | collective-permute-start | bytes 1769480 | tf_op jit(solution)/shard_map/ppermute | solution.py:32
  26.4 13.9 %collective-permute-start.6 = (bf16[1152,256]{1,0:T(8,128)(2,1)}, bf16[1152,256]{1,0:T(8,128)(2,1)S(1)}, u32[]{:S(2)}, u32[]{:S(2)}) collective-permute-start(bf16[1152,256]{1,0:T(8,128)(2,1)} %dynamic-slice_dynamic-update-slice_fusion), channel_id=1, source_target_pairs={{0,96},{1,97},{2,98},{3,99},{4,100},{5,101},{6,102},{7,103},{8,104... | collective-permute-start | bytes 1769480 | tf_op jit(solution)/shard_map/ppermute | solution.py:32
  28.5 10.9 %collective-permute-start.2 = (bf16[128,1536]{1,0:T(8,128)(2,1)}, bf16[128,1536]{1,0:T(8,128)(2,1)S(1)}, u32[]{:S(2)}, u32[]{:S(2)}) collective-permute-start(bf16[128,1536]{1,0:T(8,128)(2,1)} %shard_map.136.x0), channel_id=1, source_target_pairs={{0,16},{1,17},{2,18},{3,19},{4,20},{5,21},{6,22},{7,23},{8,24},{9,... | collective-permute-start | bytes 1179656 | tf_op jit(solution)/shard_map/ppermute | solution.py:32
  30.2 14.4 %collective-permute-start.4 = (bf16[1152,256]{1,0:T(8,128)(2,1)}, bf16[1152,256]{1,0:T(8,128)(2,1)S(1)}, u32[]{:S(2)}, u32[]{:S(2)}) collective-permute-start(bf16[1152,256]{1,0:T(8,128)(2,1)} %dynamic-slice_dynamic-update-slice_fusion), channel_id=1, source_target_pairs={{0,32},{1,33},{2,34},{3,35},{4,36},{5,37},{6,38},{7,39},{8,40},{9,... | collective-permute-start | bytes 1769480 | tf_op jit(solution)/shard_map/ppermute | solution.py:32
  30.2 22.8 %collective-permute-start.5 = (bf16[1152,256]{1,0:T(8,128)(2,1)}, bf16[1152,256]{1,0:T(8,128)(2,1)S(1)}, u32[]{:S(2)}, u32[]{:S(2)}) collective-permute-start(bf16[1152,256]{1,0:T(8,128)(2,1)} %fusion.23), channel_id=1, source_target_pairs={{0,96},{1,97},{2,98},{3,99},{4,100},{5,101},{6,102},{7,103},{8,104... | collective-permute-start | bytes 1769480 | tf_op jit(solution)/shard_map/ppermute | solution.py:32
  32.9 24.1 %collective-permute-start.7 = (bf16[1152,256]{1,0:T(8,128)(2,1)}, bf16[1152,256]{1,0:T(8,128)(2,1)S(1)}, u32[]{:S(2)}, u32[]{:S(2)}) collective-permute-start(bf16[1152,256]{1,0:T(8,128)(2,1)} %collective-permute-done.3.a0), channel_id=1, source_target_pairs={{0,1},{1,0},{2,3},{3,2},{4,5},{5,4},{6,7},{7,6},{8,9},{9,8},{10,11... | collective-permute-start | bytes 1769480 | tf_op jit(solution)/shard_map/ppermute | solution.py:32
  39.4 17.9 %collective-permute-start.11 = (bf16[1152,256]{1,0:T(8,128)(2,1)}, bf16[1152,256]{1,0:T(8,128)(2,1)S(1)}, u32[]{:S(2)}, u32[]{:S(2)}) collective-permute-start(bf16[1152,256]{1,0:T(8,128)(2,1)} %collective-permute-done.3.a0), channel_id=1, source_target_pairs={{0,32},{1,33},{2,34},{3,35},{4,36},{5,37},{6,38},{7,39},{8,40},{9,... | collective-permute-start | bytes 1769480 | tf_op jit(solution)/shard_map/ppermute | solution.py:32
  40.3 25.3 %collective-permute-start.12 = (bf16[1152,256]{1,0:T(8,128)(2,1)S(1)}, bf16[1152,256]{1,0:T(8,128)(2,1)S(1)}, u32[]{:S(2)}, u32[]{:S(2)}) collective-permute-start(bf16[1152,256]{1,0:T(8,128)(2,1)S(1)} %collective-permute-done.6.b1), channel_id=1, source_target_pairs={{0,96},{1,97},{2,98},{3,99},{4,100},{5,101},{6,102},{7,103},{8,104... | collective-permute-start | bytes 1769480 | tf_op jit(solution)/shard_map/ppermute | solution.py:32
  44.6 33.0 %collective-permute-start.10 = (bf16[1152,256]{1,0:T(8,128)(2,1)S(1)}, bf16[1152,256]{1,0:T(8,128)(2,1)S(1)}, u32[]{:S(2)}, u32[]{:S(2)}) collective-permute-start(bf16[1152,256]{1,0:T(8,128)(2,1)S(1)} %collective-permute-done.6.b1), channel_id=1, source_target_pairs={{0,1},{1,0},{2,3},{3,2},{4,5},{5,4},{6,7},{7,6},{8,9},{9,8},{10,11... | collective-permute-start | bytes 1769480 | tf_op jit(solution)/shard_map/ppermute | solution.py:32
  53.0 24.6 %collective-permute-start.8 = (bf16[1152,256]{1,0:T(8,128)(2,1)S(1)}, bf16[1152,256]{1,0:T(8,128)(2,1)S(1)}, u32[]{:S(2)}, u32[]{:S(2)}) collective-permute-start(bf16[1152,256]{1,0:T(8,128)(2,1)S(1)} %collective-permute-done.4.b0), channel_id=1, source_target_pairs={{0,1},{1,0},{2,3},{3,2},{4,5},{5,4},{6,7},{7,6},{8,9},{9,8},{10,11... | collective-permute-start | bytes 1769480 | tf_op jit(solution)/shard_map/ppermute | solution.py:32
  57.0 20.6 %collective-permute-start.9 = (bf16[1152,256]{1,0:T(8,128)(2,1)S(1)}, bf16[1152,256]{1,0:T(8,128)(2,1)S(1)}, u32[]{:S(2)}, u32[]{:S(2)}) collective-permute-start(bf16[1152,256]{1,0:T(8,128)(2,1)S(1)} %collective-permute-done.5.a1), channel_id=1, source_target_pairs={{0,1},{1,0},{2,3},{3,2},{4,5},{5,4},{6,7},{7,6},{8,9},{9,8},{10,11... | collective-permute-start | bytes 1769480 | tf_op jit(solution)/shard_map/ppermute | solution.py:32
  57.3 27.7 %collective-permute-start.13 = (bf16[1152,256]{1,0:T(8,128)(2,1)S(1)}, bf16[1152,256]{1,0:T(8,128)(2,1)S(1)}, u32[]{:S(2)}, u32[]{:S(2)}) collective-permute-start(bf16[1152,256]{1,0:T(8,128)(2,1)S(1)} %collective-permute-done.11.a0), channel_id=1, source_target_pairs={{0,1},{1,0},{2,3},{3,2},{4,5},{5,4},{6,7},{7,6},{8,9},{9,8},{10,11... | collective-permute-start | bytes 1769480 | tf_op jit(solution)/shard_map/ppermute | solution.py:32
  65.6 19.4 %collective-permute-start.14 = (bf16[1152,256]{1,0:T(8,128)(2,1)S(1)}, bf16[1152,256]{1,0:T(8,128)(2,1)S(1)}, u32[]{:S(2)}, u32[]{:S(2)}) collective-permute-start(bf16[1152,256]{1,0:T(8,128)(2,1)S(1)} %collective-permute-done.12.b0), channel_id=1, source_target_pairs={{0,1},{1,0},{2,3},{3,2},{4,5},{5,4},{6,7},{7,6},{8,9},{9,8},{10,11... | collective-permute-start | bytes 1769480 | tf_op jit(solution)/shard_map/ppermute | solution.py:32
  77.6 7.4 %copy-start.2 = (bf16[512,1536]{1,0:T(8,128)(2,1)S(1)}, bf16[512,1536]{1,0:T(8,128)(2,1)}, u32[]{:S(2)}) copy-start(bf16[512,1536]{1,0:T(8,128)(2,1)} %copy-done.1) | copy-start | bytes 4718596
  85.0 9.7 %copy-start.21 = (s32[128]{0:T(128)S(1)}, s32[128]{0:T(128)}, u32[]{:S(2)}) copy-start(s32[128]{0:T(128)} %param.22) | copy-start | bytes 1540
  85.0 34.3 %copy-start.15 = (f32[1536]{0:T(1024)S(1)}, f32[1536]{0:T(1024)}, u32[]{:S(2)}) copy-start(f32[1536]{0:T(1024)} %param.19) | copy-start | bytes 18436
  90.4 31.2 %copy-start.16 = (f32[1536]{0:T(1024)S(1)}, f32[1536]{0:T(1024)}, u32[]{:S(2)}) copy-start(f32[1536]{0:T(1024)} %param.20) | copy-start | bytes 18436
  90.4 28.8 %collective-permute-start.17 = (bf16[128,1536]{1,0:T(8,128)(2,1)}, bf16[128,1536]{1,0:T(8,128)(2,1)}, u32[]{:S(2)}, u32[]{:S(2)}) collective-permute-start(bf16[128,1536]{1,0:T(8,128)(2,1)} %get-tuple-element.16), channel_id=1, source_target_pairs={{0,16},{1,17},{2,18},{3,19},{4,20},{5,21},{6,22},{7,23},{8,24},{9,... | collective-permute-start | bytes 1179656 | tf_op jit(solution)/shard_map/ppermute | solution.py:32
  92.1 27.2 %collective-permute-start.16 = (bf16[128,1536]{1,0:T(8,128)(2,1)}, bf16[128,1536]{1,0:T(8,128)(2,1)}, u32[]{:S(2)}, u32[]{:S(2)}) collective-permute-start(bf16[128,1536]{1,0:T(8,128)(2,1)} %get-tuple-element.15), channel_id=1, source_target_pairs={{0,8},{1,9},{2,10},{3,11},{4,12},{5,13},{6,14},{7,15},{8,16},{9,17... | collective-permute-start | bytes 1179656 | tf_op jit(solution)/shard_map/ppermute | solution.py:32
  92.5 26.8 %collective-permute-start.15 = (bf16[128,1536]{1,0:T(8,128)(2,1)}, bf16[128,1536]{1,0:T(8,128)(2,1)}, u32[]{:S(2)}, u32[]{:S(2)}) collective-permute-start(bf16[128,1536]{1,0:T(8,128)(2,1)} %get-tuple-element.14), channel_id=1, source_target_pairs={{0,24},{1,25},{2,26},{3,27},{4,28},{5,29},{6,30},{7,31},{8,0},{9,1... | collective-permute-start | bytes 1179656 | tf_op jit(solution)/shard_map/ppermute | solution.py:32
  99.8 17.9 %all-to-all-start = ((s32[128,2,3]{2,1,0:T(2,128)}), s32[128,2,3]{2,1,0:T(2,128)}, u32[]{:S(2)}, u32[]{:S(2)}) async-start(s32[128,2,3]{2,1,0:T(2,128)} %bitcast.71), calls=%async_computation | async-start | bytes 262144 | tf_op jit(solution)/shard_map/all_to_all | solution.py:247
  121.6 10.8 %copy-start.17 = (s32[256,1]{0,1:T(1,128)S(1)}, s32[256,1]{0,1:T(1,128)}, u32[]{:S(2)}) copy-start(s32[256,1]{0,1:T(1,128)} %copy.93) | copy-start | bytes 3076
  125.1 25.5 %copy-start.18 = (f32[768]{0:T(1024)S(1)}, f32[768]{0:T(1024)}, u32[]{:S(2)}) copy-start(f32[768]{0:T(1024)} %param.24) | copy-start | bytes 9220
  127.0 17.4 %all-to-all-start.1 = ((bf16[128,2,768]{2,1,0:T(2,128)(2,1)}), bf16[128,2,768]{2,1,0:T(2,128)(2,1)}, u32[]{:S(2)}, u32[]{:S(2)}) async-start(bf16[128,2,768]{2,1,0:T(2,128)(2,1)} %reshape.181), calls=%async_computation.1 | async-start | bytes 786432 | tf_op jit(solution)/shard_map/all_to_all | solution.py:240
  132.3 45.2 %all-gather.3.cloned.1.call-start = ((), (), s32[]{:S(2)}) async-start(), calls=%async_computation.2 | async-start | bytes 3538944 | tf_op jit(solution)/shard_map/all_gather | solution.py:272
  152.9 93.6 %all-gather.5.cloned.1.call-start = ((), (), s32[]{:S(2)}) async-start(), calls=%async_computation.3 | async-start | bytes 3170304 | tf_op jit(solution)/shard_map/all_gather | solution.py:292
  265.7 4.8 %copy-start.11 = (f32[128,768]{1,0:T(8,128)S(1)}, f32[128,768]{1,0:T(8,128)}, u32[]{:S(2)}) copy-start(f32[128,768]{1,0:T(8,128)} %copy-done.10) | copy-start | bytes 1179652
  (13 other events, 23.6 us)
Sparse Core Ops, SparseCore 0:
  153.1 24.3 all-gather.2
  180.6 65.9 all-gather.4

commit v2 on v0

v2 whole, which is shorter than its diff:
```python
import functools

import jax
import jax.numpy as jnp
from jax import lax
from jax.experimental import pallas as pl
from jax.experimental.pallas import tpu as pltpu
from jax.sharding import PartitionSpec as P

ROWS = 128
D_VIT = 1536
D = 768
HEAD_COUNT = 12
HEAD_WIDTH = 64
SEGMENT_SPACING = 16
KEPT = ROWS // SEGMENT_SPACING
RING = 4
CORES = 2
SEGMENT_DEVICES = RING * CORES
PAIR = 2 * HEAD_WIDTH
PAIRS = D // PAIR
AXES = ("tile", "seq")
VMEM = pl.BlockSpec(memory_space=pltpu.VMEM)
PARAMS = pltpu.CompilerParams(vmem_limit_bytes=48 * 1024 * 1024)
F32, BF16, I32 = jnp.float32, jnp.bfloat16, jnp.int32


def device_at(z, y, x, c):
    return ((z * RING + y) * RING + x) * CORES + c


def shift(value, z=0, y=0, x=0, c=0):
    pairs = []
    for zi in range(RING):
        for yi in range(RING):
            for xi in range(RING):
                for ci in range(CORES):
                    to = device_at((zi + z) % RING, (yi + y) % RING, (xi + x) % RING, (ci + c) % CORES)
                    pairs.append((device_at(zi, yi, xi, ci), to))
    return lax.ppermute(value, AXES, pairs)


def call(kernel, outs, *args, flops=0, scratch=()):
    outs = [jax.ShapeDtypeStruct(shape, dtype) for shape, dtype in outs]
    nbytes = sum(a.size * a.dtype.itemsize for a in (*args, *outs))
    return pl.pallas_call(
        kernel,
        out_shape=outs,
        in_specs=[VMEM] * len(args),
        out_specs=tuple(VMEM for _ in outs),
        scratch_shapes=scratch,
        compiler_params=PARAMS,
        cost_estimate=pl.CostEstimate(flops=flops, bytes_accessed=nbytes, transcendentals=0),
    )(*args)


def layer_norm(sender_rows, gain):
    average = jnp.mean(sender_rows, axis=-1, keepdims=True)
    centered = sender_rows - average
    variance = jnp.mean(centered * centered, axis=-1, keepdims=True)
    return centered * lax.rsqrt(variance + 1e-06) * gain


def dot(a, b):
    return jnp.dot(a, b, preferred_element_type=F32)


def dot_t(a, b):
    return lax.dot_general(a, b, (((1,), (1,)), ((), ())), preferred_element_type=F32)


def pack_kernel(gate_ref, up_ref, down_ref, out_ref):
    core = lax.rem(lax.axis_index("seq"), CORES)
    half = pl.ds(pl.multiple_of(core * 128, 128), 128)
    out_ref[:D_VIT, :128] = gate_ref[:, half]
    out_ref[:D_VIT, 128:] = up_ref[:, half]
    for j in range(6):
        out_ref[D_VIT + 128 * j : D_VIT + 128 * (j + 1), :] = down_ref[half, 256 * j : 256 * (j + 1)]


def norm_kernel(x_ref, gain_ref, out_ref):
    out_ref[...] = layer_norm(x_ref[...].astype(F32), gain_ref[...]).astype(BF16)


def gated(gate, up):
    return (gate / (1.0 + jnp.exp(-gate)) * up).astype(BF16)


def mlp_own_kernel(x0, x1, x2, x3, gate_ref, up_ref, down_ref, rows_ref, total_ref):
    for n, x in enumerate((x0, x1, x2, x3)):
        rows_ref[ROWS * n : ROWS * (n + 1), :] = x[...]
    hidden = gated(dot(rows_ref[...], gate_ref[...]), dot(rows_ref[...], up_ref[...]))
    for j in range(3):
        cols = slice(512 * j, 512 * (j + 1))
        total_ref[:, cols] = dot(hidden, down_ref[:, cols])


def hidden_of(rows_ref, chunk, hidden_ref, at):
    if len(chunk) == 1:
        both = dot(rows_ref[...], chunk[0][:D_VIT, :])
    else:
        both = dot(rows_ref[:, :1152], chunk[0][...]) + dot(rows_ref[:, 1152:], chunk[1][:384, :])
    hidden_ref[:, 128 * at : 128 * (at + 1)] = gated(both[:, :128], both[:, 128:])


def mlp_chunks(rows_ref, chunks, hidden_ref, down_ref):
    for n, chunk in enumerate(chunks):
        hidden_of(rows_ref, chunk, hidden_ref, n)
        first = D_VIT if len(chunk) == 1 else D_VIT - 1152
        for j in range(6):
            down_ref[128 * n : 128 * (n + 1), 256 * j : 256 * (j + 1)] = chunk[-1][first + 128 * j : first + 128 * (j + 1), :]


def mlp_middle_kernel(rows_ref, total_ref, a, b, c, d, out_ref, hidden_ref, down_ref):
    mlp_chunks(rows_ref, ((a,), (b,), (c,), (d,)), hidden_ref, down_ref)
    for j in range(3):
        cols = slice(512 * j, 512 * (j + 1))
        out_ref[:, cols] = total_ref[:, cols] + dot(hidden_ref[...], down_ref[:, cols])


def mlp_last_kernel(rows_ref, total_ref, a0, b0, a1, b1, own_ref, r1, r2, r3, hidden_ref, down_ref):
    mlp_chunks(rows_ref, ((a0, b0), (a1, b1)), hidden_ref, down_ref)
    for j in range(3):
        cols = slice(512 * j, 512 * (j + 1))
        value = total_ref[:, cols] + dot(hidden_ref[...], down_ref[:, cols])
        for k, ref in enumerate((own_ref, r1, r2, r3)):
            ref[:, cols] = value[ROWS * k : ROWS * (k + 1)].astype(ref.dtype)


def encoder_mlp(cls_tokens, norm_gain, w_gate, w_up, w_down):
    swap = functools.partial(shift, c=1)
    (chunk,) = call(pack_kernel, [((2304, 256), BF16)], w_gate, w_up, w_down)
    before, after = shift(chunk, z=1), shift(chunk, z=-1)

    (normed,) = call(norm_kernel, [((ROWS, D_VIT), BF16)], cls_tokens, norm_gain[None])
    gathered = [normed, shift(normed, y=1), shift(normed, y=-1), shift(normed, y=2)]
    rows, total = call(
        mlp_own_kernel,
        [((4 * ROWS, D_VIT), BF16), ((4 * ROWS, D_VIT), F32)],
        *gathered,
        w_gate,
        w_up,
        w_down,
        flops=2 * 512 * 1536 * 768,
    )
    before, after, total = lax.optimization_barrier((before, after, total))
    across_top, across_bottom = shift(before[:1152], z=1), shift(after[1152:], z=-1)
    (total,) = call(
        mlp_middle_kernel,
        [((4 * ROWS, D_VIT), F32)],
        rows,
        total,
        before,
        after,
        swap(before),
        swap(after),
        flops=4 * 512 * 1536 * 768,
        scratch=[pltpu.VMEM((4 * ROWS, 512), BF16), pltpu.VMEM((512, D_VIT), BF16)],
    )
    across_top, across_bottom, total = lax.optimization_barrier((across_top, across_bottom, total))
    own, back_1, fore_1, back_2 = call(
        mlp_last_kernel,
        [((ROWS, D_VIT), t) for t in (F32, BF16, BF16, BF16)],
        rows,
        total,
        across_top,
        across_bottom,
        swap(across_top),
        swap(across_bottom),
        flops=2 * 512 * 1536 * 768,
        scratch=[pltpu.VMEM((4 * ROWS, 256), BF16), pltpu.VMEM((256, D_VIT), BF16)],
    )
    return own, shift(back_1, y=-1), shift(fore_1, y=1), shift(back_2, y=2)


def route_kernel(dest_ref, coords_ref, pack_ref, meta_ref):
    dest = jnp.broadcast_to(dest_ref[...], (ROWS, ROWS))
    target = lax.shift_right_logical(dest, 7).astype(F32)
    here = lax.broadcasted_iota(I32, (ROWS, ROWS), 1)
    peer = lax.broadcasted_iota(I32, (ROWS, ROWS), 0)
    earlier = jnp.where((target == target.T) & (peer < here), 1.0, 0.0)
    slot = jnp.sum(earlier, axis=0, keepdims=True)
    fields = (dest_ref[...] & 127, coords_ref[0:1, :], coords_ref[1:2, :])
    meta = jnp.full((ROWS, ROWS), -1.0, F32)
    for s in range(2):
        taken = (target == peer.astype(F32)) & (slot == float(s))
        pack_ref[ROWS * s : ROWS * (s + 1), :] = jnp.where(taken, 1.0, 0.0).astype(BF16)
        for k, field in enumerate(fields):
            column = jnp.sum(jnp.where(taken, field.astype(F32) + 1.0, 0.0), axis=1, keepdims=True) - 1.0
            meta = jnp.where(here == 3 * s + k, column, meta)
    meta_ref[...] = meta


def plan_kernel(meta_ref, place_ref, coords_ref):
    fields = meta_ref[...].T
    row = lax.broadcasted_iota(I32, (ROWS, ROWS), 0)
    lane = lax.broadcasted_iota(I32, (ROWS, ROWS), 1)
    coords = [0.0, 0.0]
    for s in range(2):
        taken = row.astype(F32) == fields[3 * s : 3 * s + 1, :]
        place_ref[:, ROWS * s : ROWS * (s + 1)] = jnp.where(taken, 1.0, 0.0).astype(BF16)
        for k in range(2):
            value = fields[3 * s + 1 + k : 3 * s + 2 + k, :]
            coords[k] = coords[k] + jnp.sum(jnp.where(taken, value, 0.0), axis=1, keepdims=True)
    coords_ref[...] = jnp.where(lane == 0, coords[0], jnp.where(lane == 1, coords[1], 0.0))


def position_table(coords):
    quarter = D // 4
    frequency = 1.0 / 10000.0 ** (jnp.arange(quarter).astype(F32) / quarter)
    along_x = coords[:, 0:1] * frequency[None, :]
    along_y = coords[:, 1:2] * frequency[None, :]
    return jnp.concatenate([jnp.sin(along_x), jnp.cos(along_x), jnp.sin(along_y), jnp.cos(along_y)], axis=1)


def embed_kernel(tokens_ref, own_ref, a, b, c, scale_ref, gain_ref, w_ref, pack_ref, out_ref):
    total = own_ref[...] + a[...].astype(F32) + b[...].astype(F32) + c[...].astype(F32)
    mixed = tokens_ref[...].astype(F32) + scale_ref[...] * total
    final_rows = layer_norm(mixed, gain_ref[...]).astype(BF16)
    embedded = dot(final_rows, w_ref[...]).astype(BF16)
    out_ref[...] = dot(pack_ref[...], embedded).astype(BF16)


def kept_columns(rows, offsets_ref):
    place = lax.broadcasted_iota(I32, (rows, D), 0) & (SEGMENT_SPACING - 1)
    return place == offsets_ref[...]


def group_matrix(groups):
    group = lax.broadcasted_iota(I32, (groups, groups * SEGMENT_SPACING), 0)
    row = lax.broadcasted_iota(I32, (groups, groups * SEGMENT_SPACING), 1)
    return jnp.where(lax.shift_right_logical(row, 4) == group, 1.0, 0.0).astype(BF16)


def place_kernel(payload_ref, place_ref, pos_ref, gain_ref, w_ref, offsets_ref, seq_ref, normed_ref, far_ref):
    placed = dot(place_ref[...], payload_ref[...])
    seq_in = placed + pos_ref[...]
    seq_ref[...] = seq_in
    normed = layer_norm(seq_in, gain_ref[...]).astype(BF16)
    normed_ref[...] = normed
    kept = kept_columns(ROWS, offsets_ref)
    groups = group_matrix(KEPT)
    for part in range(2):
        cols = slice(D * (part + 1), D * (part + 2))
        rows = jnp.where(kept, dot(normed, w_ref[:, cols]), 0.0).astype(BF16)
        chosen = dot(groups, rows).astype(BF16)
        for n in range(16):
            far_ref[KEPT * n : KEPT * (n + 1), D * part : D * (part + 1)] = chosen


def qkv_kernel(b0, b1, b2, b3, b4, b5, b6, b7, w_ref, offsets_ref, q_ref, far_q_ref, k_ref, v_ref, rows_ref):
    for n, b in enumerate((b0, b1, b2, b3, b4, b5, b6, b7)):
        rows_ref[ROWS * n : ROWS * (n + 1), :] = b[...]
    kept = kept_columns(512, offsets_ref)
    groups = group_matrix(4 * KEPT)
    for n in range(2):
        part = slice(512 * n, 512 * (n + 1))
        queries = dot(rows_ref[part, :], w_ref[:, :D]) * (HEAD_WIDTH ** -0.5)
        if n == 0:
            q_ref[...] = queries[:ROWS].astype(BF16)
        far_q_ref[4 * KEPT * n : 4 * KEPT * (n + 1), :] = dot(groups, jnp.where(kept, queries, 0.0).astype(BF16)).astype(BF16)
        k_ref[part, :] = dot(rows_ref[part, :], w_ref[:, D : 2 * D]).astype(BF16)
        v_ref[part, :] = dot(rows_ref[part, :], w_ref[:, 2 * D :]).astype(BF16)


def attend_pair(queries, keys, values):
    n = queries.shape[0]
    lane = lax.broadcasted_iota(I32, (n, PAIR), 1)
    zero = jnp.zeros((), BF16)
    both = jnp.concatenate(
        [jnp.where(lane < HEAD_WIDTH, queries, zero), jnp.where(lane < HEAD_WIDTH, zero, queries)], axis=0
    )
    scores = dot_t(both, keys)
    highest = jnp.max(scores, axis=-1, keepdims=True)
    weights = jnp.exp(scores - highest)
    totals = jnp.sum(weights, axis=-1, keepdims=True)
    mixed = dot(weights.astype(BF16), values) / totals
    logsum = highest + jnp.log(totals)
    return jnp.where(lane < HEAD_WIDTH, mixed[:n], mixed[n:]), logsum[:n], logsum[n:]


def far_kernel(q_ref, kv_ref, out_ref):
    x, c = lax.axis_index("seq") // CORES, lax.rem(lax.axis_index("seq"), CORES)
    queries = SEGMENT_DEVICES * KEPT
    lane = lax.broadcasted_iota(I32, (queries, 128), 1)
    table = jnp.zeros((queries, 128), F32)
    blocks = []
    for j in range(PAIRS):
        cols = slice(PAIR * j, PAIR * (j + 1))
        mixed, even, odd = attend_pair(q_ref[:, cols], kv_ref[:, cols], kv_ref[:, D + PAIR * j : D + PAIR * (j + 1)])
        blocks.append(mixed)
        table = jnp.where(lane == 2 * j, even, jnp.where(lane == 2 * j + 1, odd, table))
    blocks.append(table)
    for n, (dx, dc) in enumerate(BLOCKS):
        peer = lax.rem(x - dx + RING, RING) * CORES + lax.rem(c + dc, CORES)
        where = pl.ds(pl.multiple_of(peer * KEPT, KEPT), KEPT)
        for j, block in enumerate(blocks):
            out_ref[where, 128 * j : 128 * (j + 1)] = block[KEPT * n : KEPT * (n + 1), :]


def near_kernel(q_ref, k_ref, v_ref, out_ref, lse_ref):
    lane = lax.broadcasted_iota(I32, (ROWS, PAIR), 1)
    for j in range(PAIRS):
        cols = slice(PAIR * j, PAIR * (j + 1))
        mixed, even, odd = attend_pair(q_ref[:, cols], k_ref[:, cols], v_ref[:, cols])
        out_ref[:, cols] = mixed
        lse_ref[:, cols] = jnp.where(lane < HEAD_WIDTH, even, odd)


def spread(rows):
    n, width = rows.shape
    return jnp.broadcast_to(rows[:, None, :], (n, SEGMENT_SPACING, width)).reshape(n * SEGMENT_SPACING, width)


def final_kernel(seq_ref, near_ref, lse_ref, far_ref, offsets_ref, w_ref, out_ref):
    parts = [slice(KEPT * n, KEPT * (n + 1)) for n in range(SEGMENT_DEVICES)]
    tables = [far_ref[part, D:] for part in parts]
    highest = functools.reduce(jnp.maximum, tables)
    shares = [jnp.exp(table - highest) for table in tables]
    totals = functools.reduce(jnp.add, shares)
    far_lse = highest + jnp.log(totals)
    lane = lax.broadcasted_iota(I32, (KEPT, PAIR), 1)

    def over_lanes(table, j):
        return jnp.where(lane < HEAD_WIDTH, table[:, 2 * j : 2 * j + 1], table[:, 2 * j + 1 : 2 * j + 2])

    result = seq_ref[...]
    combined = []
    place = lax.broadcasted_iota(I32, (ROWS, PAIR), 0) & (SEGMENT_SPACING - 1)
    for j in range(PAIRS):
        cols = slice(PAIR * j, PAIR * (j + 1))
        far = functools.reduce(jnp.add, [over_lanes(s, j) * far_ref[part, cols] for s, part in zip(shares, parts)])
        far = spread(far / over_lanes(totals, j))
        kept = place == offsets_ref[:, cols]
        share = jnp.where(kept, 1.0 / (1.0 + jnp.exp(lse_ref[:, cols] - spread(over_lanes(far_lse, j)))), 0.0)
        combined.append(((1.0 - share) * near_ref[:, cols] + share * far).astype(BF16))
    out_ref[...] = (result + dot(jnp.concatenate(combined, axis=1), w_ref[...])).astype(BF16)


BLOCKS = ((0, 0), (0, 1), (1, 0), (1, 1), (-1, 0), (-1, 1), (2, 0), (2, 1))


def body(
    cls_tokens,
    norm_gain,
    w_gate,
    w_up,
    w_down,
    layer_scale,
    final_gain,
    w_embed,
    dest_pos,
    tile_coords,
    attn_gain,
    w_qkv,
    offsets,
    w_out,
):
    swap = functools.partial(shift, c=1)
    devices = lax.axis_size("tile") * lax.axis_size("seq")
    pack, meta = call(
        route_kernel, [((2 * ROWS, ROWS), BF16), ((ROWS, ROWS), F32)], dest_pos[None], tile_coords
    )
    meta = lax.all_to_all(meta.reshape(devices, 1, ROWS), AXES, split_axis=0, concat_axis=0, tiled=True)
    place, coords = call(plan_kernel, [((ROWS, 2 * ROWS), BF16), ((ROWS, ROWS), F32)], meta.reshape(ROWS, ROWS))
    pos = position_table(coords)
    offset_columns = jnp.repeat(offsets, HEAD_WIDTH)[None]

    terms = encoder_mlp(cls_tokens, norm_gain, w_gate, w_up, w_down)
    (payload,) = call(
        embed_kernel,
        [((2 * ROWS, D), BF16)],
        cls_tokens,
        *terms,
        layer_scale[None],
        final_gain[None],
        w_embed,
        pack,
        flops=2 * ROWS * D_VIT * D,
    )
    payload = lax.all_to_all(payload.reshape(2, devices, D), AXES, split_axis=1, concat_axis=1, tiled=True)
    seq_in, normed, far_kv = call(
        place_kernel,
        [((ROWS, D), F32), ((ROWS, D), BF16), ((ROWS, 2 * D), BF16)],
        payload.reshape(2 * ROWS, D),
        place,
        pos,
        attn_gain[None],
        w_qkv,
        offset_columns,
        flops=4 * ROWS * D * D,
    )
    far_kv = lax.all_to_all(far_kv, "tile", split_axis=0, concat_axis=0, tiled=True)
    held = [normed, shift(normed, x=1), shift(normed, x=-1), shift(normed, x=2)]
    blocks = []
    for block in held:
        blocks += [block, swap(block)]
    queries, far_queries, keys, values = call(
        qkv_kernel,
        [((ROWS, D), BF16), ((SEGMENT_DEVICES * KEPT, D), BF16), ((1024, D), BF16), ((1024, D), BF16)],
        *blocks,
        w_qkv,
        offset_columns,
        flops=2 * 1024 * D * 3 * D,
        scratch=[pltpu.VMEM((1024, D), BF16)],
    )
    (far_parts,) = call(far_kernel, [((SEGMENT_DEVICES * KEPT, D + 128), F32)], far_queries, far_kv)
    far_parts = lax.all_to_all(far_parts, "seq", split_axis=0, concat_axis=0, tiled=True)
    near, near_lse = call(near_kernel, [((ROWS, D), F32), ((ROWS, D), F32)], queries, keys, values, flops=8 * 128 * 1024 * D)
    (out,) = call(
        final_kernel,
        [((ROWS, D), BF16)],
        seq_in,
        near,
        near_lse,
        far_parts,
        offset_columns,
        w_out,
        flops=2 * ROWS * D * D,
    )
    return out


def solution(mesh):
    in_specs = (
        P(("tile", "seq"), None),
        P(),
        P(None, "tile"),
        P(None, "tile"),
        P("tile", None),
        P(),
        P(),
        P(),
        P(("tile", "seq")),
        P(None, ("tile", "seq")),
        P(),
        P(),
        P(),
        P(),
    )
    out_specs = P(("tile", "seq"), None)
    return jax.shard_map(body, mesh=mesh, in_specs=in_specs, out_specs=out_specs, check_vma=False)
```

time: 358 us -> 172 us (0.48)
  waiting for transfers between devices: 210 us -> 43.7 us
  matrix products: 36.7 us -> 0 us
  starting transfers between devices: 16.2 us -> 52.7 us
  Pallas kernels: 0 us -> 32.4 us
  other arithmetic: 24.2 us -> 3.13 us
  local copies, waits for them, and re-layouts: 56.9 us -> 38.3 us
  between operations: 13.4 us -> 0.33 us
    all_gather x3 -> x0, waiting for transfers between devices: 126 us -> none  [the longest x1 64.7 us: body(): shard_rows = lax.all_gather(normed, 'tile', axis=0, tiled=True)]
    reduce_scatter x1 -> x0, waiting for transfers between devices: 68.9 us -> none  [body(): lax.psum_scatter(jnp.dot(hidden, w_down, preferred_element_type=jnp.float...]
    dot_general x9 -> x0, matrix products: 36.7 us -> none  [the longest x1 14.6 us: body(): jnp.dot(hidden, w_down, preferred_element_type=jnp.float32)]
    pallas_call x0 -> x13, Pallas kernels: none -> 32.4 us  [call(): pl.pallas_call(kernel, out_shape=outs, in_specs=[VMEM] * len(args), out_s...]
    ppermute x0 -> x21, starting transfers between devices: none -> 29.5 us  [shift(): return lax.ppermute(value, AXES, pairs)]
    ppermute x0 -> x21, waiting for transfers between devices: none -> 28.1 us  [shift(): return lax.ppermute(value, AXES, pairs)]
    unnamed x29 -> x100, local copies, waits for them, and re-layouts: 6.38 us -> 30.9 us
    slice x9 -> x3, local copies, waits for them, and re-layouts: 22.1 us -> 1.17 us  [the longest x1 1.09 us: position_table(): along_x = coords[:, 0:1] * frequency[None, :]]
  transfers between devices with their start and end apart: 6 -> 25, of which waited for: 6 -> 11; matrix products, arithmetic and copies ran while one was open for 13% -> 5% of each run, Pallas kernels for 0% -> 12%
where the time goes in v2:
time: 172 us; the launch traced here: 171 us
  starting transfers between devices  52.7 us (31%)
  waiting for transfers between devices  43.7 us (25%)
  local copies, waits for them, and re-layouts  38.3 us (22%)
  Pallas kernels  32.4 us (19%)
  other arithmetic  3.13 us (2%)
    pallas_call x13, Pallas kernels, call(): pl.pallas_call(kernel, out_shape=outs, in_specs=[VMEM] * len(args), out_s...  32.4 us
    unnamed x100, local copies, waits for them, and re-layouts  30.9 us
    ppermute x21, starting transfers between devices, shift(): return lax.ppermute(value, AXES, pairs)  29.5 us
    ppermute x21, waiting for transfers between devices, shift(): return lax.ppermute(value, AXES, pairs)  28.1 us
    all_to_all x1, starting transfers between devices, body(): lax.all_to_all(meta.reshape(devices, 1, ROWS), AXES, split_axis=0, concat...  9.35 us
    all_to_all x1, waiting for transfers between devices, body(): lax.all_to_all(payload.reshape(2, devices, D), AXES, split_axis=1, concat...  8.37 us
    all_to_all x1, waiting for transfers between devices, body(): lax.all_to_all(meta.reshape(devices, 1, ROWS), AXES, split_axis=0, concat...  6.46 us
    all_to_all x1, starting transfers between devices, body(): lax.all_to_all(payload.reshape(2, devices, D), AXES, split_axis=1, concat...  6.08 us
  transfers between devices with their start and end apart: 25, of which 11 were waited for; matrix products, arithmetic and copies ran while one was open for 5% of the time, Pallas kernels for 12%

profile of v2, /device:TPU:1, one launch (start us, length us, event | category | flops | bytes accessed | tf_op | source)
XLA Modules:
  0.0 170.6 jit_solution(10931668760596886817)
XLA Ops:
  3.6 2.5 %collective-permute-start.3 = (bf16[2304,256]{1,0:T(8,128)(2,1)S(1)}, bf16[2304,256]{1,0:T(8,128)(2,1)S(1)}, u32[]{:S(2)}, u32[]{:S(2)}) collective-permute-start(bf16[2304,256]{1,0:T(8,128)(2,1)S(1)} %shard_map.138), channel_id=1, source_target_pairs={{0,32},{1,33},{2,34},{3,35},{4,36},{5,37},{6,38},{7,39},{8,40},{9,... | collective-permute-start | bytes 3538952 | tf_op jit(solution)/shard_map/ppermute | solution.py:40
  6.2 2.2 %collective-permute-start.4 = (bf16[2304,256]{1,0:T(8,128)(2,1)S(1)}, bf16[2304,256]{1,0:T(8,128)(2,1)S(1)}, u32[]{:S(2)}, u32[]{:S(2)}) collective-permute-start(bf16[2304,256]{1,0:T(8,128)(2,1)S(1)} %shard_map.138), channel_id=1, source_target_pairs={{0,96},{1,97},{2,98},{3,99},{4,100},{5,101},{6,102},{7,103},{8,104... | collective-permute-start | bytes 3538952 | tf_op jit(solution)/shard_map/ppermute | solution.py:40
  8.7 1.4 collective-permute-start
  10.1 1.5 collective-permute-start.1
  11.6 1.6 collective-permute-start.2
  13.2 6.6 %collective-permute-done.x1 = bf16[128,1536]{1,0:T(8,128)(2,1)S(1)} collective-permute-done((bf16[128,1536]{1,0:T(8,128)(2,1)S(1)}, bf16[128,1536]{1,0:T(8,128)(2,1)S(1)}, u32[]{:S(2)}, u32[]{:S(2)}) %collective-permute-start) | collective-permute-done | bytes 393248 | tf_op jit(solution)/shard_map/ppermute | solution.py:40
  19.8 9.5 %collective-permute-done.2.x3 = bf16[128,1536]{1,0:T(8,128)(2,1)S(1)} collective-permute-done((bf16[128,1536]{1,0:T(8,128)(2,1)S(1)}, bf16[128,1536]{1,0:T(8,128)(2,1)S(1)}, u32[]{:S(2)}, u32[]{:S(2)}) %collective-permute-start.2) | collective-permute-done | bytes 393248 | tf_op jit(solution)/shard_map/ppermute | solution.py:40
  29.3 3.1 %shard_map.137 = (bf16[512,1536]{1,0:T(8,128)(2,1)S(1)}, f32[512,1536]{1,0:T(8,128)}) custom-call(bf16[128,1536]{1,0:T(8,128)(2,1)S(1)} %shard_map.136.x0, bf16[128,1536]{1,0:T(8,128)(2,1)S(1)} %collective-permute-done.x1, bf16[128,1536]{1,0:T(8,128)(2,1)S(1)} %collective-permute-done.1.x2, bf16[128,1536]{1,0:T(8,128)(2,1)S(1)} %collective-permute-done.2.x3, ...), custom_call_target="tpu_custom_call" | custom-call | flops 1207959552 | bytes 8650752 | tf_op jit(solution)/shard_map/pallas_call | solution.py:46
  34.0 1.5 collective-permute-start.7
  36.4 2.1 %collective-permute-start.6 = (bf16[1152,256]{1,0:T(8,128)(2,1)S(1)}, bf16[1152,256]{1,0:T(8,128)(2,1)S(1)}, u32[]{:S(2)}, u32[]{:S(2)}) collective-permute-start(bf16[1152,256]{1,0:T(8,128)(2,1)S(1)} %slice.13), channel_id=1, source_target_pairs={{0,96},{1,97},{2,98},{3,99},{4,100},{5,101},{6,102},{7,103},{8,104... | collective-permute-start | bytes 1769480 | tf_op jit(solution)/shard_map/ppermute | solution.py:40
  39.7 6.7 %shard_map.139.total_ref = f32[512,1536]{1,0:T(8,128)} custom-call(bf16[512,1536]{1,0:T(8,128)(2,1)} %copy-done, f32[512,1536]{1,0:T(8,128)} %get-tuple-element.34.total_ref, bf16[2304,256]{1,0:T(8,128)(2,1)S(1)} %collective-permute-done.3.a, bf16[2304,256]{1,0:T(8,128)(2,1)S(1)} %collective-permute-done.4.b, ...), custom_call_target="tpu_custom_call" | custom-call | flops 2415919104 | bytes 12582912 | tf_op jit(solution)/shard_map/pallas_call | solution.py:46
  46.4 5.0 %collective-permute-done.5.a0 = bf16[1152,256]{1,0:T(8,128)(2,1)S(1)} collective-permute-done((bf16[1152,256]{1,0:T(8,128)(2,1)S(1)}, bf16[1152,256]{1,0:T(8,128)(2,1)S(1)}, u32[]{:S(2)}, u32[]{:S(2)}) %collective-permute-start.5) | collective-permute-done | bytes 589856 | tf_op jit(solution)/shard_map/ppermute | solution.py:40
  52.7 1.6 collective-permute-done.10.b1
  55.2 4.6 %shard_map.140 = (f32[128,1536]{1,0:T(8,128)S(1)}, bf16[128,1536]{1,0:T(8,128)(2,1)}, bf16[128,1536]{1,0:T(8,128)(2,1)}, bf16[128,1536]{1,0:T(8,128)(2,1)}) custom-call(bf16[512,1536]{1,0:T(8,128)(2,1)S(1)} %copy-done.1, f32[512,1536]{1,0:T(8,128)} %shard_map.139.total_ref, bf16[1152,256]{1,0:T(8,128)(2,1)S(1)} %collective-permute-done.5.a0, ...), custom_call_target="tpu_custom_call" | custom-call | flops 1207959552 | bytes 9043968 | tf_op jit(solution)/shard_map/pallas_call | solution.py:46
  59.8 2.4 %collective-permute-start.11 = (bf16[128,1536]{1,0:T(8,128)(2,1)}, bf16[128,1536]{1,0:T(8,128)(2,1)}, u32[]{:S(2)}, u32[]{:S(2)}) collective-permute-start(bf16[128,1536]{1,0:T(8,128)(2,1)} %get-tuple-element.39), channel_id=1, source_target_pairs={{0,24},{1,25},{2,26},{3,27},{4,28},{5,29},{6,30},{7,31},{8,0},{9,1... | collective-permute-start | bytes 1179656 | tf_op jit(solution)/shard_map/ppermute | solution.py:40
  62.2 1.6 collective-permute-start.13
  65.5 9.4 %all-to-all-start.1 = ((f32[128,1,128]{2,1,0:T(1,128)}), f32[128,1,128]{2,1,0:T(1,128)}, u32[]{:S(2)}, u32[]{:S(2)}) async-start(f32[128,1,128]{2,1,0:T(1,128)} %bitcast.17), calls=%async_computation.1 | async-start | bytes 131072 | tf_op jit(solution)/shard_map/all_to_all | solution.py:364
  75.5 1.3 broadcast_in_dim.22.gain_ref
  79.5 6.5 %all-to-all-done.1 = f32[128,1,128]{2,1,0:T(1,128)} async-done(((f32[128,1,128]{2,1,0:T(1,128)}), f32[128,1,128]{2,1,0:T(1,128)}, u32[]{:S(2)}, u32[]{:S(2)}) %all-to-all-start.1) | async-done | bytes 65568 | tf_op jit(solution)/shard_map/all_to_all | solution.py:364
  89.9 2.4 %shard_map.142 = bf16[256,768]{1,0:T(8,128)(2,1)S(1)} custom-call(bf16[128,1536]{1,0:T(8,128)(2,1)S(1)} %copy-done.5, f32[128,1536]{1,0:T(8,128)S(1)} %get-tuple-element.38.own_ref, bf16[128,1536]{1,0:T(8,128)(2,1)} %collective-permute-done.11.a, bf16[128,1536]{1,0:T(8,128)(2,1)} %collective-permute-done.12.b, bf16[128,1536]{1,0:T(8,128)(2,1)} %collective-permute-done.13.c, ...), custom_call_target="tpu_custom_call" | custom-call | flops 301989888 | bytes 5189632 | tf_op jit(solution)/shard_map/pallas_call | solution.py:46
  93.4 6.1 %all-to-all-start = ((bf16[2,128,768]{2,0,1:T(2,128)(2,1)}), bf16[2,128,768]{2,0,1:T(2,128)(2,1)}, u32[]{:S(2)}, u32[]{:S(2)}) async-start(bf16[2,128,768]{2,0,1:T(2,128)(2,1)} %copy.15), calls=%async_computation | async-start | bytes 786432 | tf_op jit(solution)/shard_map/all_to_all | solution.py:381
  100.6 1.6 multiply_sine_fusion.1
  103.2 8.4 %all-to-all-done = bf16[2,128,768]{2,0,1:T(2,128)(2,1)} async-done(((bf16[2,128,768]{2,0,1:T(2,128)(2,1)}), bf16[2,128,768]{2,0,1:T(2,128)(2,1)}, u32[]{:S(2)}, u32[]{:S(2)}) %all-to-all-start) | async-done | bytes 393248 | tf_op jit(solution)/shard_map/all_to_all | solution.py:381
  117.2 2.7 %collective-permute-start.17 = (bf16[128,768]{1,0:T(8,128)(2,1)}, bf16[128,768]{1,0:T(8,128)(2,1)S(1)}, u32[]{:S(2)}, u32[]{:S(2)}) collective-permute-start(bf16[128,768]{1,0:T(8,128)(2,1)} %get-tuple-element.47.b0), channel_id=1, source_target_pairs={{0,6},{1,7},{2,0},{3,1},{4,2},{5,3},{6,4},{7,5},{8,14},{9,15},{10,... | collective-permute-start | bytes 589832 | tf_op jit(solution)/shard_map/ppermute | solution.py:40
  119.9 1.4 collective-permute-start.14
  121.3 2.9 %collective-permute-done.15.b2 = bf16[128,768]{1,0:T(8,128)(2,1)S(1)} collective-permute-done((bf16[128,768]{1,0:T(8,128)(2,1)}, bf16[128,768]{1,0:T(8,128)(2,1)S(1)}, u32[]{:S(2)}, u32[]{:S(2)}) %collective-permute-start.15) | collective-permute-done | bytes 196640 | tf_op jit(solution)/shard_map/ppermute | solution.py:40
  124.2 6.0 %collective-permute-start.16 = (bf16[128,768]{1,0:T(8,128)(2,1)S(1)}, bf16[128,768]{1,0:T(8,128)(2,1)S(1)}, u32[]{:S(2)}, u32[]{:S(2)}) collective-permute-start(bf16[128,768]{1,0:T(8,128)(2,1)S(1)} %collective-permute-done.15.b2), channel_id=1, source_target_pairs={{0,1},{1,0},{2,3},{3,2},{4,5},{5,4},{6,7},{7,6},{8,9},{9,8},{10,11... | collective-permute-start | bytes 589832 | tf_op jit(solution)/shard_map/ppermute | solution.py:40
  130.7 3.6 %all-to-all-start.2 = ((bf16[16,8,1536]{2,1,0:T(8,128)(2,1)}), bf16[16,8,1536]{2,1,0:T(8,128)(2,1)S(1)}, u32[]{:S(2)}, u32[]{:S(2)}) async-start(bf16[16,8,1536]{2,1,0:T(8,128)(2,1)} %bitcast.16), calls=%async_computation.2 | async-start | bytes 786432 | tf_op jit(solution)/shard_map/all_to_all | solution.py:393
  143.5 6.7 %shard_map.145 = (bf16[128,768]{1,0:T(8,128)(2,1)S(1)}, bf16[64,768]{1,0:T(8,128)(2,1)S(1)}, bf16[1024,768]{1,0:T(8,128)(2,1)S(1)}, bf16[1024,768]{1,0:T(8,128)(2,1)S(1)}) custom-call(bf16[128,768]{1,0:T(8,128)(2,1)} %get-tuple-element.47.b0, bf16[128,768]{1,0:T(8,128)(2,1)S(1)} %copy-done.39, bf16[128,768]{1,0:T(8,128)(2,1)S(1)} %copy-done.33, ...), custom_call_target="tpu_custom_call" | custom-call | flops 3623878656 | bytes 8555520 | tf_op jit(solution)/shard_map/pallas_call | solution.py:46
  152.4 1.6 shard_map.147
  154.6 4.2 %all-to-all-start.3 = ((f32[8,8,896]{2,1,0:T(8,128)}), f32[8,8,896]{2,1,0:T(8,128)S(1)}, u32[]{:S(2)}, u32[]{:S(2)}) async-start(f32[8,8,896]{2,1,0:T(8,128)} %bitcast.15), calls=%async_computation.3 | async-start | bytes 458752 | tf_op jit(solution)/shard_map/all_to_all | solution.py:408
  159.8 3.1 %shard_map.146 = (f32[128,768]{1,0:T(8,128)S(1)}, f32[128,768]{1,0:T(8,128)S(1)}) custom-call(bf16[128,768]{1,0:T(8,128)(2,1)S(1)} %copy-done.23, bf16[1024,768]{1,0:T(8,128)(2,1)S(1)} %get-tuple-element.49.k_ref, bf16[1024,768]{1,0:T(8,128)(2,1)S(1)} %get-tuple-element.50.v_ref), custom_call_target="tpu_custom_call" | custom-call | flops 805306368 | bytes 4128768 | tf_op jit(solution)/shard_map/pallas_call | solution.py:46
  (145 shorter events, 48.6 us)
Async XLA Ops:
  3.5 25.9 %copy-start.9 = (bf16[1536,256]{1,0:T(8,128)(2,1)S(1)}, bf16[1536,256]{1,0:T(8,128)(2,1)}, u32[]{:S(2)}) copy-start(bf16[1536,256]{1,0:T(8,128)(2,1)} %gate_ref.3) | copy-start | bytes 2359300
  3.5 25.9 %copy-start.11 = (bf16[1536,256]{1,0:T(8,128)(2,1)S(1)}, bf16[1536,256]{1,0:T(8,128)(2,1)}, u32[]{:S(2)}) copy-start(bf16[1536,256]{1,0:T(8,128)(2,1)} %up_ref.3) | copy-start | bytes 2359300
  3.5 25.9 %copy-start.13 = (bf16[256,1536]{1,0:T(8,128)(2,1)S(1)}, bf16[256,1536]{1,0:T(8,128)(2,1)}, u32[]{:S(2)}) copy-start(bf16[256,1536]{1,0:T(8,128)(2,1)} %down_ref.3) | copy-start | bytes 2359300
  3.6 30.3 %collective-permute-start.3 = (bf16[2304,256]{1,0:T(8,128)(2,1)S(1)}, bf16[2304,256]{1,0:T(8,128)(2,1)S(1)}, u32[]{:S(2)}, u32[]{:S(2)}) collective-permute-start(bf16[2304,256]{1,0:T(8,128)(2,1)S(1)} %shard_map.138), channel_id=1, source_target_pairs={{0,32},{1,33},{2,34},{3,35},{4,36},{5,37},{6,38},{7,39},{8,40},{9,... | collective-permute-start | bytes 3538952 | tf_op jit(solution)/shard_map/ppermute | solution.py:40
  6.2 27.8 %collective-permute-start.4 = (bf16[2304,256]{1,0:T(8,128)(2,1)S(1)}, bf16[2304,256]{1,0:T(8,128)(2,1)S(1)}, u32[]{:S(2)}, u32[]{:S(2)}) collective-permute-start(bf16[2304,256]{1,0:T(8,128)(2,1)S(1)} %shard_map.138), channel_id=1, source_target_pairs={{0,96},{1,97},{2,98},{3,99},{4,100},{5,101},{6,102},{7,103},{8,104... | collective-permute-start | bytes 3538952 | tf_op jit(solution)/shard_map/ppermute | solution.py:40
  8.7 11.1 %collective-permute-start = (bf16[128,1536]{1,0:T(8,128)(2,1)S(1)}, bf16[128,1536]{1,0:T(8,128)(2,1)S(1)}, u32[]{:S(2)}, u32[]{:S(2)}) collective-permute-start(bf16[128,1536]{1,0:T(8,128)(2,1)S(1)} %shard_map.136.x0), channel_id=1, source_target_pairs={{0,8},{1,9},{2,10},{3,11},{4,12},{5,13},{6,14},{7,15},{8,16},{9,17... | collective-permute-start | bytes 1179656 | tf_op jit(solution)/shard_map/ppermute | solution.py:40
  10.1 9.7 %collective-permute-start.1 = (bf16[128,1536]{1,0:T(8,128)(2,1)S(1)}, bf16[128,1536]{1,0:T(8,128)(2,1)S(1)}, u32[]{:S(2)}, u32[]{:S(2)}) collective-permute-start(bf16[128,1536]{1,0:T(8,128)(2,1)S(1)} %shard_map.136.x0), channel_id=1, source_target_pairs={{0,24},{1,25},{2,26},{3,27},{4,28},{5,29},{6,30},{7,31},{8,0},{9,1... | collective-permute-start | bytes 1179656 | tf_op jit(solution)/shard_map/ppermute | solution.py:40
  11.6 17.7 %collective-permute-start.2 = (bf16[128,1536]{1,0:T(8,128)(2,1)S(1)}, bf16[128,1536]{1,0:T(8,128)(2,1)S(1)}, u32[]{:S(2)}, u32[]{:S(2)}) collective-permute-start(bf16[128,1536]{1,0:T(8,128)(2,1)S(1)} %shard_map.136.x0), channel_id=1, source_target_pairs={{0,16},{1,17},{2,18},{3,19},{4,20},{5,21},{6,22},{7,23},{8,24},{9,... | collective-permute-start | bytes 1179656 | tf_op jit(solution)/shard_map/ppermute | solution.py:40
  34.0 4.5 %collective-permute-start.7 = (bf16[2304,256]{1,0:T(8,128)(2,1)S(1)}, bf16[2304,256]{1,0:T(8,128)(2,1)S(1)}, u32[]{:S(2)}, u32[]{:S(2)}) collective-permute-start(bf16[2304,256]{1,0:T(8,128)(2,1)S(1)} %collective-permute-done.3.a), channel_id=1, source_target_pairs={{0,1},{1,0},{2,3},{3,2},{4,5},{5,4},{6,7},{7,6},{8,9},{9,8},{10,11... | collective-permute-start | bytes 3538952 | tf_op jit(solution)/shard_map/ppermute | solution.py:40
  35.5 4.2 %collective-permute-start.8 = (bf16[2304,256]{1,0:T(8,128)(2,1)S(1)}, bf16[2304,256]{1,0:T(8,128)(2,1)S(1)}, u32[]{:S(2)}, u32[]{:S(2)}) collective-permute-start(bf16[2304,256]{1,0:T(8,128)(2,1)S(1)} %collective-permute-done.4.b), channel_id=1, source_target_pairs={{0,1},{1,0},{2,3},{3,2},{4,5},{5,4},{6,7},{7,6},{8,9},{9,8},{10,11... | collective-permute-start | bytes 3538952 | tf_op jit(solution)/shard_map/ppermute | solution.py:40
  35.7 15.8 %collective-permute-start.5 = (bf16[1152,256]{1,0:T(8,128)(2,1)S(1)}, bf16[1152,256]{1,0:T(8,128)(2,1)S(1)}, u32[]{:S(2)}, u32[]{:S(2)}) collective-permute-start(bf16[1152,256]{1,0:T(8,128)(2,1)S(1)} %slice.12), channel_id=1, source_target_pairs={{0,32},{1,33},{2,34},{3,35},{4,36},{5,37},{6,38},{7,39},{8,40},{9,... | collective-permute-start | bytes 1769480 | tf_op jit(solution)/shard_map/ppermute | solution.py:40
  36.4 15.1 %collective-permute-start.6 = (bf16[1152,256]{1,0:T(8,128)(2,1)S(1)}, bf16[1152,256]{1,0:T(8,128)(2,1)S(1)}, u32[]{:S(2)}, u32[]{:S(2)}) collective-permute-start(bf16[1152,256]{1,0:T(8,128)(2,1)S(1)} %slice.13), channel_id=1, source_target_pairs={{0,96},{1,97},{2,98},{3,99},{4,100},{5,101},{6,102},{7,103},{8,104... | collective-permute-start | bytes 1769480 | tf_op jit(solution)/shard_map/ppermute | solution.py:40
  46.4 17.5 %copy-start.47 = (s32[128]{0:T(128)S(1)}, s32[128]{0:T(128)}, u32[]{:S(2)}) copy-start(s32[128]{0:T(128)} %param.22) | copy-start | bytes 1540
  46.4 30.4 %copy-start.49 = (s32[12]{0:T(128)S(1)}, s32[12]{0:T(128)}, u32[]{:S(2)}) copy-start(s32[12]{0:T(128)} %param.26) | copy-start | bytes 148
  51.5 2.9 %collective-permute-start.10 = (bf16[1152,256]{1,0:T(8,128)(2,1)S(1)}, bf16[1152,256]{1,0:T(8,128)(2,1)S(1)}, u32[]{:S(2)}, u32[]{:S(2)}) collective-permute-start(bf16[1152,256]{1,0:T(8,128)(2,1)S(1)} %collective-permute-done.6.b0), channel_id=1, source_target_pairs={{0,1},{1,0},{2,3},{3,2},{4,5},{5,4},{6,7},{7,6},{8,9},{9,8},{10,11... | collective-permute-start | bytes 1769480 | tf_op jit(solution)/shard_map/ppermute | solution.py:40
  52.7 2.5 %collective-permute-start.9 = (bf16[1152,256]{1,0:T(8,128)(2,1)S(1)}, bf16[1152,256]{1,0:T(8,128)(2,1)S(1)}, u32[]{:S(2)}, u32[]{:S(2)}) collective-permute-start(bf16[1152,256]{1,0:T(8,128)(2,1)S(1)} %collective-permute-done.5.a0), channel_id=1, source_target_pairs={{0,1},{1,0},{2,3},{3,2},{4,5},{5,4},{6,7},{7,6},{8,9},{9,8},{10,11... | collective-permute-start | bytes 1769480 | tf_op jit(solution)/shard_map/ppermute | solution.py:40
  55.2 33.1 %copy-start.3 = (bf16[1536,768]{1,0:T(8,128)(2,1)S(1)}, bf16[1536,768]{1,0:T(8,128)(2,1)}, u32[]{:S(2)}) copy-start(bf16[1536,768]{1,0:T(8,128)(2,1)} %w_ref.4) | copy-start | bytes 7077892
  59.8 28.5 %collective-permute-start.11 = (bf16[128,1536]{1,0:T(8,128)(2,1)}, bf16[128,1536]{1,0:T(8,128)(2,1)}, u32[]{:S(2)}, u32[]{:S(2)}) collective-permute-start(bf16[128,1536]{1,0:T(8,128)(2,1)} %get-tuple-element.39), channel_id=1, source_target_pairs={{0,24},{1,25},{2,26},{3,27},{4,28},{5,29},{6,30},{7,31},{8,0},{9,1... | collective-permute-start | bytes 1179656 | tf_op jit(solution)/shard_map/ppermute | solution.py:40
  62.2 26.1 %collective-permute-start.12 = (bf16[128,1536]{1,0:T(8,128)(2,1)}, bf16[128,1536]{1,0:T(8,128)(2,1)}, u32[]{:S(2)}, u32[]{:S(2)}) collective-permute-start(bf16[128,1536]{1,0:T(8,128)(2,1)} %get-tuple-element.40), channel_id=1, source_target_pairs={{0,8},{1,9},{2,10},{3,11},{4,12},{5,13},{6,14},{7,15},{8,16},{9,17... | collective-permute-start | bytes 1179656 | tf_op jit(solution)/shard_map/ppermute | solution.py:40
  62.2 26.1 %collective-permute-start.13 = (bf16[128,1536]{1,0:T(8,128)(2,1)}, bf16[128,1536]{1,0:T(8,128)(2,1)}, u32[]{:S(2)}, u32[]{:S(2)}) collective-permute-start(bf16[128,1536]{1,0:T(8,128)(2,1)} %get-tuple-element.41), channel_id=1, source_target_pairs={{0,16},{1,17},{2,18},{3,19},{4,20},{5,21},{6,22},{7,23},{8,24},{9,... | collective-permute-start | bytes 1179656 | tf_op jit(solution)/shard_map/ppermute | solution.py:40
  65.5 20.5 %all-to-all-start.1 = ((f32[128,1,128]{2,1,0:T(1,128)}), f32[128,1,128]{2,1,0:T(1,128)}, u32[]{:S(2)}, u32[]{:S(2)}) async-start(f32[128,1,128]{2,1,0:T(1,128)} %bitcast.17), calls=%async_computation.1 | async-start | bytes 131072 | tf_op jit(solution)/shard_map/all_to_all | solution.py:364
  92.3 20.3 %copy-start.2 = (bf16[768,2304]{1,0:T(8,128)(2,1)S(1)}, bf16[768,2304]{1,0:T(8,128)(2,1)}, u32[]{:S(2)}) copy-start(bf16[768,2304]{1,0:T(8,128)(2,1)} %w_ref.6) | copy-start | bytes 10616836
  93.4 18.1 %all-to-all-start = ((bf16[2,128,768]{2,0,1:T(2,128)(2,1)}), bf16[2,128,768]{2,0,1:T(2,128)(2,1)}, u32[]{:S(2)}, u32[]{:S(2)}) async-start(bf16[2,128,768]{2,0,1:T(2,128)(2,1)} %copy.15), calls=%async_computation | async-start | bytes 786432 | tf_op jit(solution)/shard_map/all_to_all | solution.py:381
  117.2 7.0 %collective-permute-start.15 = (bf16[128,768]{1,0:T(8,128)(2,1)}, bf16[128,768]{1,0:T(8,128)(2,1)S(1)}, u32[]{:S(2)}, u32[]{:S(2)}) collective-permute-start(bf16[128,768]{1,0:T(8,128)(2,1)} %get-tuple-element.47.b0), channel_id=1, source_target_pairs={{0,2},{1,3},{2,4},{3,5},{4,6},{5,7},{6,0},{7,1},{8,10},{9,11},{10,... | collective-permute-start | bytes 589832 | tf_op jit(solution)/shard_map/ppermute | solution.py:40
  117.2 13.0 %collective-permute-start.17 = (bf16[128,768]{1,0:T(8,128)(2,1)}, bf16[128,768]{1,0:T(8,128)(2,1)S(1)}, u32[]{:S(2)}, u32[]{:S(2)}) collective-permute-start(bf16[128,768]{1,0:T(8,128)(2,1)} %get-tuple-element.47.b0), channel_id=1, source_target_pairs={{0,6},{1,7},{2,0},{3,1},{4,2},{5,3},{6,4},{7,5},{8,14},{9,15},{10,... | collective-permute-start | bytes 589832 | tf_op jit(solution)/shard_map/ppermute | solution.py:40
  119.9 10.4 %collective-permute-start.19 = (bf16[128,768]{1,0:T(8,128)(2,1)}, bf16[128,768]{1,0:T(8,128)(2,1)S(1)}, u32[]{:S(2)}, u32[]{:S(2)}) collective-permute-start(bf16[128,768]{1,0:T(8,128)(2,1)} %get-tuple-element.47.b0), channel_id=1, source_target_pairs={{0,4},{1,5},{2,6},{3,7},{4,0},{5,1},{6,2},{7,3},{8,12},{9,13},{10,... | collective-permute-start | bytes 589832 | tf_op jit(solution)/shard_map/ppermute | solution.py:40
  119.9 14.4 %collective-permute-start.14 = (bf16[128,768]{1,0:T(8,128)(2,1)}, bf16[128,768]{1,0:T(8,128)(2,1)S(1)}, u32[]{:S(2)}, u32[]{:S(2)}) collective-permute-start(bf16[128,768]{1,0:T(8,128)(2,1)} %get-tuple-element.47.b0), channel_id=1, source_target_pairs={{0,1},{1,0},{2,3},{3,2},{4,5},{5,4},{6,7},{7,6},{8,9},{9,8},{10,11... | collective-permute-start | bytes 589832 | tf_op jit(solution)/shard_map/ppermute | solution.py:40
  124.2 10.8 %collective-permute-start.16 = (bf16[128,768]{1,0:T(8,128)(2,1)S(1)}, bf16[128,768]{1,0:T(8,128)(2,1)S(1)}, u32[]{:S(2)}, u32[]{:S(2)}) collective-permute-start(bf16[128,768]{1,0:T(8,128)(2,1)S(1)} %collective-permute-done.15.b2), channel_id=1, source_target_pairs={{0,1},{1,0},{2,3},{3,2},{4,5},{5,4},{6,7},{7,6},{8,9},{9,8},{10,11... | collective-permute-start | bytes 589832 | tf_op jit(solution)/shard_map/ppermute | solution.py:40
  130.1 5.5 %collective-permute-start.18 = (bf16[128,768]{1,0:T(8,128)(2,1)S(1)}, bf16[128,768]{1,0:T(8,128)(2,1)S(1)}, u32[]{:S(2)}, u32[]{:S(2)}) collective-permute-start(bf16[128,768]{1,0:T(8,128)(2,1)S(1)} %collective-permute-done.17.b4), channel_id=1, source_target_pairs={{0,1},{1,0},{2,3},{3,2},{4,5},{5,4},{6,7},{7,6},{8,9},{9,8},{10,11... | collective-permute-start | bytes 589832 | tf_op jit(solution)/shard_map/ppermute | solution.py:40
  130.2 6.1 %collective-permute-start.20 = (bf16[128,768]{1,0:T(8,128)(2,1)S(1)}, bf16[128,768]{1,0:T(8,128)(2,1)S(1)}, u32[]{:S(2)}, u32[]{:S(2)}) collective-permute-start(bf16[128,768]{1,0:T(8,128)(2,1)S(1)} %collective-permute-done.19.b6), channel_id=1, source_target_pairs={{0,1},{1,0},{2,3},{3,2},{4,5},{5,4},{6,7},{7,6},{8,9},{9,8},{10,11... | collective-permute-start | bytes 589832 | tf_op jit(solution)/shard_map/ppermute | solution.py:40
  130.7 20.8 %all-to-all-start.2 = ((bf16[16,8,1536]{2,1,0:T(8,128)(2,1)}), bf16[16,8,1536]{2,1,0:T(8,128)(2,1)S(1)}, u32[]{:S(2)}, u32[]{:S(2)}) async-start(bf16[16,8,1536]{2,1,0:T(8,128)(2,1)} %bitcast.16), calls=%async_computation.2 | async-start | bytes 786432 | tf_op jit(solution)/shard_map/all_to_all | solution.py:393
  154.6 10.4 %all-to-all-start.3 = ((f32[8,8,896]{2,1,0:T(8,128)}), f32[8,8,896]{2,1,0:T(8,128)S(1)}, u32[]{:S(2)}, u32[]{:S(2)}) async-start(f32[8,8,896]{2,1,0:T(8,128)} %bitcast.15), calls=%async_computation.3 | async-start | bytes 458752 | tf_op jit(solution)/shard_map/all_to_all | solution.py:408
  (43 other events, 99.5 us)

commit v3 on v2

v3 whole, which is shorter than its diff:
```python
import functools

import jax
import jax.numpy as jnp
from jax import lax
from jax.experimental import pallas as pl
from jax.experimental.pallas import tpu as pltpu
from jax.sharding import PartitionSpec as P

ROWS = 128
D_VIT = 1536
D = 768
HEAD_COUNT = 12
HEAD_WIDTH = 64
SEGMENT_SPACING = 16
KEPT = ROWS // SEGMENT_SPACING
RING = 4
CORES = 2
SEGMENT_DEVICES = RING * CORES
PAIR = 2 * HEAD_WIDTH
PAIRS = D // PAIR
AXES = ("tile", "seq")
VMEM = pl.BlockSpec(memory_space=pltpu.VMEM)
MIB = 1024 * 1024
HBM = pl.BlockSpec(memory_space=pltpu.HBM)
CHUNK = 2304
QUARTER = CHUNK // RING
F32, BF16, I32 = jnp.float32, jnp.bfloat16, jnp.int32


def device_at(z, y, x, c):
    return ((z * RING + y) * RING + x) * CORES + c


def shift(value, z=0, y=0, x=0, c=0):
    pairs = []
    for zi in range(RING):
        for yi in range(RING):
            for xi in range(RING):
                for ci in range(CORES):
                    to = device_at((zi + z) % RING, (yi + y) % RING, (xi + x) % RING, (ci + c) % CORES)
                    pairs.append((device_at(zi, yi, xi, ci), to))
    return lax.ppermute(value, AXES, pairs)


def along_y(value):
    groups = [[z * RING + y for y in range(RING)] for z in range(RING)]
    return lax.all_to_all(value, "tile", split_axis=0, concat_axis=0, axis_index_groups=groups, tiled=True)


def call(kernel, outs, *args, scratch=(), vmem=12, spaces=None):
    outs = [jax.ShapeDtypeStruct(shape, dtype) for shape, dtype in outs]
    return pl.pallas_call(
        kernel,
        out_shape=outs,
        in_specs=spaces or [VMEM] * len(args),
        out_specs=tuple(VMEM for _ in outs),
        scratch_shapes=scratch,
        compiler_params=pltpu.CompilerParams(vmem_limit_bytes=vmem * MIB),
        cost_estimate=pl.CostEstimate(flops=1024, bytes_accessed=1024, transcendentals=0),
    )(*args)


def layer_norm(sender_rows, gain):
    average = jnp.mean(sender_rows, axis=-1, keepdims=True)
    centered = sender_rows - average
    variance = jnp.mean(centered * centered, axis=-1, keepdims=True)
    return centered * lax.rsqrt(variance + 1e-06) * gain


def dot(a, b):
    return jnp.dot(a, b, preferred_element_type=F32)


def dot_t(a, b):
    return lax.dot_general(a, b, (((1,), (1,)), ((), ())), preferred_element_type=F32)


def pack_kernel(gate_ref, up_ref, down_ref, out_ref, quarter_ref, sems):
    core = lax.rem(lax.axis_index("seq"), CORES)
    x = lax.div(lax.axis_index("seq"), CORES)
    half = pl.ds(pl.multiple_of(core * 128, 128), 128)
    copies = [(gate_ref.at[:, half], out_ref.at[:D_VIT, :128]), (up_ref.at[:, half], out_ref.at[:D_VIT, 128:])]
    for j in range(6):
        copies.append(
            (down_ref.at[half, 256 * j : 256 * (j + 1)], out_ref.at[D_VIT + 128 * j : D_VIT + 128 * (j + 1), :])
        )
    copies = [pltpu.make_async_copy(source, to, sems.at[n]) for n, (source, to) in enumerate(copies)]
    for copy in copies:
        copy.start()
    for copy in copies:
        copy.wait()
    quarter_ref[...] = out_ref[pl.ds(pl.multiple_of(x * QUARTER, QUARTER), QUARTER), :]


def join_kernel(q0, q1, q2, q3, out_ref):
    x = lax.div(lax.axis_index("seq"), CORES)
    for dx, q in ((0, q0), (1, q1), (3, q2), (2, q3)):
        place = lax.rem(x - dx + RING, RING)
        out_ref[pl.ds(pl.multiple_of(place * QUARTER, QUARTER), QUARTER), :] = q[...]


def norm_kernel(x_ref, gain_ref, out_ref):
    normed = layer_norm(x_ref[...].astype(F32), gain_ref[...]).astype(BF16)
    for n in range(RING):
        out_ref[ROWS * n : ROWS * (n + 1), :] = normed


def gated(gate, up):
    return (gate / (1.0 + jnp.exp(-gate)) * up).astype(BF16)


def mlp_own_kernel(rows_ref, gate_ref, up_ref, down_ref, total_ref):
    hidden = gated(dot(rows_ref[...], gate_ref[...]), dot(rows_ref[...], up_ref[...]))
    for j in range(3):
        cols = slice(512 * j, 512 * (j + 1))
        total_ref[:, cols] = dot(hidden, down_ref[:, cols])


def mlp_chunks(rows_ref, chunks, hidden_ref, down_ref):
    for n, chunk in enumerate(chunks):
        both = dot(rows_ref[...], chunk[:D_VIT, :])
        hidden_ref[:, 128 * n : 128 * (n + 1)] = gated(both[:, :128], both[:, 128:])
        for j in range(6):
            block = slice(D_VIT + 128 * j, D_VIT + 128 * (j + 1))
            down_ref[128 * n : 128 * (n + 1), 256 * j : 256 * (j + 1)] = chunk[block, :]


def mlp_middle_kernel(rows_ref, total_ref, a, b, out_ref, hidden_ref, down_ref):
    mlp_chunks(rows_ref, (a, b), hidden_ref, down_ref)
    for j in range(3):
        cols = slice(512 * j, 512 * (j + 1))
        out_ref[:, cols] = total_ref[:, cols] + dot(hidden_ref[...], down_ref[:, cols])


def mlp_last_kernel(rows_ref, total_ref, a, b, c, d, own_ref, r1, r2, r3, hidden_ref, down_ref, sum_ref):
    mlp_chunks(rows_ref, (a, b, c, d), hidden_ref, down_ref)
    for j in range(3):
        cols = slice(512 * j, 512 * (j + 1))
        sum_ref[:, cols] = total_ref[:, cols] + dot(hidden_ref[...], down_ref[:, cols])
    y = lax.rem(lax.axis_index("tile"), RING)
    for dy, ref in ((0, own_ref), (3, r1), (1, r2), (2, r3)):
        place = lax.rem(y + dy, RING)
        ref[...] = sum_ref[pl.ds(pl.multiple_of(place * ROWS, ROWS), ROWS), :].astype(ref.dtype)


def encoder_mlp(cls_tokens, norm_gain, w_gate, w_up, w_down):
    swap = functools.partial(shift, c=1)
    chunk, quarter = call(
        pack_kernel,
        [((CHUNK, 256), BF16), ((QUARTER, 256), BF16)],
        w_gate,
        w_up,
        w_down,
        scratch=[pltpu.SemaphoreType.DMA((8,))],
        spaces=[HBM] * 3,
        vmem=56,
    )
    quarter = shift(quarter, z=2)
    (normed,) = call(norm_kernel, [((RING * ROWS, D_VIT), BF16)], cls_tokens, norm_gain[None])
    chunk, quarter, rows = lax.optimization_barrier((chunk, quarter, normed))
    before, after = shift(chunk, z=1), shift(chunk, z=-1)
    rows = along_y(rows)
    quarters = [quarter, shift(quarter, x=1), shift(quarter, x=-1), shift(quarter, x=2)]
    (total,) = call(
        mlp_own_kernel,
        [((RING * ROWS, D_VIT), F32)],
        rows,
        w_gate,
        w_up,
        w_down,
        vmem=20,
    )
    (across,) = call(join_kernel, [((CHUNK, 256), BF16)], *quarters)
    (total,) = call(
        mlp_middle_kernel,
        [((4 * ROWS, D_VIT), F32)],
        rows,
        total,
        across,
        swap(across),
        scratch=[pltpu.VMEM((4 * ROWS, 256), BF16), pltpu.VMEM((256, D_VIT), BF16)],
        vmem=20,
    )
    sums = call(
        mlp_last_kernel,
        [((ROWS, D_VIT), t) for t in (F32, BF16, BF16, BF16)],
        rows,
        total,
        before,
        after,
        swap(before),
        swap(after),
        scratch=[
            pltpu.VMEM((4 * ROWS, 512), BF16),
            pltpu.VMEM((512, D_VIT), BF16),
            pltpu.VMEM((4 * ROWS, D_VIT), F32),
        ],
        vmem=20,
    )
    return sums


def route_kernel(dest_ref, coords_ref, pack_ref, meta_ref):
    dest = jnp.broadcast_to(dest_ref[...], (ROWS, ROWS))
    target = lax.shift_right_logical(dest, 7).astype(F32)
    here = lax.broadcasted_iota(I32, (ROWS, ROWS), 1)
    peer = lax.broadcasted_iota(I32, (ROWS, ROWS), 0)
    earlier = jnp.where((target == target.T) & (peer < here), 1.0, 0.0)
    slot = jnp.sum(earlier, axis=0, keepdims=True)
    fields = (dest_ref[...] & 127, coords_ref[0:1, :], coords_ref[1:2, :])
    meta = jnp.full((ROWS, ROWS), -1.0, F32)
    for s in range(2):
        taken = (target == peer.astype(F32)) & (slot == float(s))
        pack_ref[ROWS * s : ROWS * (s + 1), :] = jnp.where(taken, 1.0, 0.0).astype(BF16)
        for k, field in enumerate(fields):
            column = jnp.sum(jnp.where(taken, field.astype(F32) + 1.0, 0.0), axis=1, keepdims=True) - 1.0
            meta = jnp.where(here == 3 * s + k, column, meta)
    meta_ref[...] = meta


def plan_kernel(meta_ref, frequency_ref, out_ref):
    fields = meta_ref[...].T
    row = lax.broadcasted_iota(I32, (ROWS, ROWS), 0)
    coords = [0.0, 0.0]
    for s in range(2):
        taken = row.astype(F32) == fields[3 * s : 3 * s + 1, :]
        out_ref[:, D + ROWS * s : D + ROWS * (s + 1)] = jnp.where(taken, 1.0, 0.0)
        for k in range(2):
            value = fields[3 * s + 1 + k : 3 * s + 2 + k, :]
            coords[k] = coords[k] + jnp.sum(jnp.where(taken, value, 0.0), axis=1, keepdims=True)
    lane = lax.broadcasted_iota(I32, (ROWS, D), 1)
    angle = jnp.where(lane < D // 2, coords[0], coords[1]) * frequency_ref[...]
    sine = (lane < D // 4) | ((lane >= D // 2) & (lane < 3 * D // 4))
    out_ref[:, :D] = jnp.where(sine, jnp.sin(angle), jnp.cos(angle))


def load_all(sources, targets, sems):
    copies = [pltpu.make_async_copy(a, b, sems.at[n]) for n, (a, b) in enumerate(zip(sources, targets))]
    for copy in copies:
        copy.start()
    return copies


def embed_kernel(
    tokens, own, a, b, c, scale_ref, gain_ref, w, pack, out_ref, tokens_ref, own_ref, a_ref, b_ref, c_ref, w_ref, pack_ref, sems
):
    copies = load_all(
        (tokens, own, a, b, c, w, pack), (tokens_ref, own_ref, a_ref, b_ref, c_ref, w_ref, pack_ref), sems
    )
    for copy in copies[:5]:
        copy.wait()
    total = own_ref[...] + a_ref[...].astype(F32) + b_ref[...].astype(F32) + c_ref[...].astype(F32)
    mixed = tokens_ref[...].astype(F32) + scale_ref[...] * total
    final_rows = layer_norm(mixed, gain_ref[...]).astype(BF16)
    for copy in copies[5:]:
        copy.wait()
    embedded = dot(final_rows, w_ref[...]).astype(BF16)
    out_ref[...] = dot(pack_ref[...], embedded).astype(BF16)


def kept_columns(rows, offsets_ref):
    place = lax.broadcasted_iota(I32, (rows, D), 0) & (SEGMENT_SPACING - 1)
    return place == offsets_ref[...]


def group_matrix(groups):
    group = lax.broadcasted_iota(I32, (groups, groups * SEGMENT_SPACING), 0)
    row = lax.broadcasted_iota(I32, (groups, groups * SEGMENT_SPACING), 1)
    return jnp.where(lax.shift_right_logical(row, 4) == group, 1.0, 0.0).astype(BF16)


def slide_rows(payload_ref, plan_ref):
    return dot(plan_ref[:, D:].astype(BF16), payload_ref[...]) + plan_ref[:, :D]


def place_kernel(payload_ref, plan_ref, gain_ref, normed_ref):
    seq_in = slide_rows(payload_ref, plan_ref)
    normed_ref[...] = layer_norm(seq_in, gain_ref[...]).astype(BF16)


def far_keys_kernel(normed_ref, w_ref, offsets_ref, far_ref):
    kept = kept_columns(ROWS, offsets_ref)
    groups = group_matrix(KEPT)
    for part in range(2):
        cols = slice(D * (part + 1), D * (part + 2))
        rows = jnp.where(kept, dot(normed_ref[...], w_ref[:, cols]), 0.0).astype(BF16)
        chosen = dot(groups, rows).astype(BF16)
        for n in range(16):
            far_ref[KEPT * n : KEPT * (n + 1), D * part : D * (part + 1)] = chosen


def far_queries_kernel(b0, b1, b2, b3, b4, b5, b6, b7, w_ref, offsets_ref, q_ref, rows_ref):
    for n, b in enumerate((b0, b1, b2, b3, b4, b5, b6, b7)):
        rows_ref[ROWS * n : ROWS * (n + 1), :] = b[...]
    kept = kept_columns(512, offsets_ref)
    groups = group_matrix(4 * KEPT)
    for n in range(2):
        rows = dot(rows_ref[512 * n : 512 * (n + 1), :], w_ref[:, :D]) * (HEAD_WIDTH ** -0.5)
        chosen = dot(groups, jnp.where(kept, rows, 0.0).astype(BF16))
        q_ref[4 * KEPT * n : 4 * KEPT * (n + 1), :] = chosen.astype(BF16)


def attend_pair(queries, keys, values):
    n = queries.shape[0]
    lane = lax.broadcasted_iota(I32, (n, PAIR), 1)
    zero = jnp.zeros((), BF16)
    both = jnp.concatenate(
        [jnp.where(lane < HEAD_WIDTH, queries, zero), jnp.where(lane < HEAD_WIDTH, zero, queries)], axis=0
    )
    scores = dot_t(both, keys)
    highest = jnp.max(scores, axis=-1, keepdims=True)
    weights = jnp.exp(scores - highest)
    totals = jnp.sum(weights, axis=-1, keepdims=True)
    mixed = dot(weights.astype(BF16), values) / totals
    logsum = highest + jnp.log(totals)
    return jnp.where(lane < HEAD_WIDTH, mixed[:n], mixed[n:]), logsum[:n], logsum[n:]


def far_kernel(q_ref, kv_ref, out_ref):
    x, c = lax.div(lax.axis_index("seq"), CORES), lax.rem(lax.axis_index("seq"), CORES)
    queries = SEGMENT_DEVICES * KEPT
    lane = lax.broadcasted_iota(I32, (queries, 128), 1)
    table = jnp.zeros((queries, 128), F32)
    blocks = []
    for j in range(PAIRS):
        cols = slice(PAIR * j, PAIR * (j + 1))
        mixed, even, odd = attend_pair(q_ref[:, cols], kv_ref[:, cols], kv_ref[:, D + PAIR * j : D + PAIR * (j + 1)])
        blocks.append(mixed)
        table = jnp.where(lane == 2 * j, even, jnp.where(lane == 2 * j + 1, odd, table))
    blocks.append(table)
    for n, (dx, dc) in enumerate(BLOCKS):
        peer = lax.rem(x - dx + RING, RING) * CORES + lax.rem(c + dc, CORES)
        where = pl.ds(pl.multiple_of(peer * KEPT, KEPT), KEPT)
        for j, block in enumerate(blocks):
            out_ref[where, 128 * j : 128 * (j + 1)] = block[KEPT * n : KEPT * (n + 1), :]


def near_kernel(rows_ref, w_ref, payload_ref, plan_ref, out_ref, q_ref, k_ref, v_ref):
    out_ref[:, 2 * D :] = slide_rows(payload_ref, plan_ref)
    q_ref[...] = (dot(rows_ref[:ROWS, :], w_ref[:, :D]) * (HEAD_WIDTH ** -0.5)).astype(BF16)
    for n in range(2):
        part = slice(512 * n, 512 * (n + 1))
        k_ref[part, :] = dot(rows_ref[part, :], w_ref[:, D : 2 * D]).astype(BF16)
        v_ref[part, :] = dot(rows_ref[part, :], w_ref[:, 2 * D :]).astype(BF16)
    lane = lax.broadcasted_iota(I32, (ROWS, PAIR), 1)
    for j in range(PAIRS):
        cols = slice(PAIR * j, PAIR * (j + 1))
        mixed, even, odd = attend_pair(q_ref[:, cols], k_ref[:, cols], v_ref[:, cols])
        out_ref[:, cols] = mixed
        out_ref[:, D + PAIR * j : D + PAIR * (j + 1)] = jnp.where(lane < HEAD_WIDTH, even, odd)


def spread(rows):
    n, width = rows.shape
    return jnp.broadcast_to(rows[:, None, :], (n, SEGMENT_SPACING, width)).reshape(n * SEGMENT_SPACING, width)


def final_kernel(near, far, offsets_ref, w, out_ref, near_ref, far_ref, w_ref, sems):
    copies = load_all((far, near, w), (far_ref, near_ref, w_ref), sems)
    copies[0].wait()
    copies[1].wait()
    parts = [slice(KEPT * n, KEPT * (n + 1)) for n in range(SEGMENT_DEVICES)]
    tables = [far_ref[part, D:] for part in parts]
    highest = functools.reduce(jnp.maximum, tables)
    shares = [jnp.exp(table - highest) for table in tables]
    totals = functools.reduce(jnp.add, shares)
    far_lse = highest + jnp.log(totals)
    lane = lax.broadcasted_iota(I32, (KEPT, PAIR), 1)

    def over_lanes(table, j):
        return jnp.where(lane < HEAD_WIDTH, table[:, 2 * j : 2 * j + 1], table[:, 2 * j + 1 : 2 * j + 2])

    combined = []
    place = lax.broadcasted_iota(I32, (ROWS, PAIR), 0) & (SEGMENT_SPACING - 1)
    for j in range(PAIRS):
        cols = slice(PAIR * j, PAIR * (j + 1))
        far = functools.reduce(jnp.add, [over_lanes(s, j) * far_ref[part, cols] for s, part in zip(shares, parts)])
        far = spread(far / over_lanes(totals, j))
        kept = place == offsets_ref[:, cols]
        share = jnp.where(kept, 1.0 / (1.0 + jnp.exp(near_ref[:, D + PAIR * j : D + PAIR * (j + 1)] - spread(over_lanes(far_lse, j)))), 0.0)
        combined.append(((1.0 - share) * near_ref[:, cols] + share * far).astype(BF16))
    copies[2].wait()
    out_ref[...] = (near_ref[:, 2 * D :] + dot(jnp.concatenate(combined, axis=1), w_ref[...])).astype(BF16)


BLOCKS = ((0, 0), (0, 1), (1, 0), (1, 1), (-1, 0), (-1, 1), (2, 0), (2, 1))


def body(
    cls_tokens,
    norm_gain,
    w_gate,
    w_up,
    w_down,
    layer_scale,
    final_gain,
    w_embed,
    dest_pos,
    tile_coords,
    attn_gain,
    w_qkv,
    offsets,
    w_out,
):
    swap = functools.partial(shift, c=1)
    devices = lax.axis_size("tile") * lax.axis_size("seq")
    own, back_1, fore_1, back_2 = encoder_mlp(cls_tokens, norm_gain, w_gate, w_up, w_down)
    dest_pos, own = lax.optimization_barrier((dest_pos, own))
    terms = (own, shift(back_1, y=-1), shift(fore_1, y=1), shift(back_2, y=2))
    pack, meta = call(
        route_kernel, [((2 * ROWS, ROWS), BF16), ((ROWS, ROWS), F32)], dest_pos[None], tile_coords
    )
    meta = lax.all_to_all(meta.reshape(devices, 1, ROWS), AXES, split_axis=0, concat_axis=0, tiled=True)
    frequency = 1.0 / 10000.0 ** (jnp.arange(D // 4).astype(F32) / (D // 4))
    frequency = jnp.tile(frequency, 4)[None]
    (plan,) = call(plan_kernel, [((ROWS, D + 2 * ROWS), F32)], meta.reshape(ROWS, ROWS), frequency)
    offset_columns = jnp.repeat(offsets, HEAD_WIDTH)[None]
    (payload,) = call(
        embed_kernel,
        [((2 * ROWS, D), BF16)],
        cls_tokens,
        *terms,
        layer_scale[None],
        final_gain[None],
        w_embed,
        pack,
        scratch=[
            pltpu.VMEM((ROWS, D_VIT), BF16),
            pltpu.VMEM((ROWS, D_VIT), F32),
            pltpu.VMEM((ROWS, D_VIT), BF16),
            pltpu.VMEM((ROWS, D_VIT), BF16),
            pltpu.VMEM((ROWS, D_VIT), BF16),
            pltpu.VMEM((D_VIT, D), BF16),
            pltpu.VMEM((2 * ROWS, ROWS), BF16),
            pltpu.SemaphoreType.DMA((7,)),
        ],
        spaces=[HBM] * 5 + [VMEM] * 2 + [HBM] * 2,
        vmem=56,
    )
    payload, plan = lax.optimization_barrier((payload, plan))
    payload = lax.all_to_all(payload.reshape(2, devices, D), AXES, split_axis=1, concat_axis=1, tiled=True)
    payload = payload.reshape(2 * ROWS, D)
    (normed,) = call(place_kernel, [((ROWS, D), BF16)], payload, plan, attn_gain[None])
    held = [normed, shift(normed, x=1), shift(normed, x=-1), shift(normed, x=2)]
    (far_kv,) = call(far_keys_kernel, [((ROWS, 2 * D), BF16)], normed, w_qkv, offset_columns)
    far_kv = lax.all_to_all(far_kv, "tile", split_axis=0, concat_axis=0, tiled=True)
    blocks = []
    for block in held:
        blocks += [block, swap(block)]
    segment = SEGMENT_DEVICES * ROWS
    far_queries, rows = call(
        far_queries_kernel,
        [((SEGMENT_DEVICES * KEPT, D), BF16), ((segment, D), BF16)],
        *blocks,
        w_qkv,
        offset_columns,
    )
    (far_parts,) = call(far_kernel, [((SEGMENT_DEVICES * KEPT, D + 128), F32)], far_queries, far_kv)
    far_parts = lax.all_to_all(far_parts, "seq", split_axis=0, concat_axis=0, tiled=True)
    (near,) = call(
        near_kernel,
        [((ROWS, 3 * D), F32)],
        rows,
        w_qkv,
        payload,
        plan,
        scratch=[
            pltpu.VMEM((ROWS, D), BF16),
            pltpu.VMEM((segment, D), BF16),
            pltpu.VMEM((segment, D), BF16),
        ],
        vmem=16,
    )
    (out,) = call(
        final_kernel,
        [((ROWS, D), BF16)],
        near,
        far_parts,
        offset_columns,
        w_out,
        scratch=[
            pltpu.VMEM((ROWS, 3 * D), F32),
            pltpu.VMEM((SEGMENT_DEVICES * KEPT, D + 128), F32),
            pltpu.VMEM((D, D), BF16),
            pltpu.SemaphoreType.DMA((3,)),
        ],
        spaces=[HBM, HBM, VMEM, HBM],
        vmem=56,
    )
    return out


def solution(mesh):
    in_specs = (
        P(("tile", "seq"), None),
        P(),
        P(None, "tile"),
        P(None, "tile"),
        P("tile", None),
        P(),
        P(),
        P(),
        P(("tile", "seq")),
        P(None, ("tile", "seq")),
        P(),
        P(),
        P(),
        P(),
    )
    out_specs = P(("tile", "seq"), None)
    return jax.shard_map(body, mesh=mesh, in_specs=in_specs, out_specs=out_specs, check_vma=False)
```

time: 172 us -> 160 us (0.930)
  local copies, waits for them, and re-layouts: 38.3 us -> 26.8 us
  waiting for transfers between devices: 43.7 us -> 36.1 us
  Pallas kernels: 32.4 us -> 38.7 us
  starting transfers between devices: 52.7 us -> 56.8 us
  other arithmetic: 3.13 us -> 0.01 us
    ppermute x21 -> x19, waiting for transfers between devices: 28.1 us -> 14.5 us  [shift(): return lax.ppermute(value, AXES, pairs)]
    unnamed x100 -> x76, local copies, waits for them, and re-layouts: 30.9 us -> 22.1 us
    pallas_call x13 -> x15, Pallas kernels: 32.4 us -> 38.7 us  [call(): pl.pallas_call(kernel, out_shape=outs, in_specs=spaces or [VMEM] * len(ar...]
    all_to_all x0 -> x1, starting transfers between devices: none -> 4.18 us  [along_y(): lax.all_to_all(value, 'tile', split_axis=0, concat_axis=0, axis_index_gro...]
    all_to_all x1, waiting for transfers between devices: 8.37 us -> 12 us  [body(): lax.all_to_all(payload.reshape(2, devices, D), AXES, split_axis=1, concat...]
    all_to_all x1, waiting for transfers between devices: 6.46 us -> 9.59 us  [body(): lax.all_to_all(meta.reshape(devices, 1, ROWS), AXES, split_axis=0, concat...]
    all_to_all x1, starting transfers between devices: 9.35 us -> 7.23 us  [body(): lax.all_to_all(meta.reshape(devices, 1, ROWS), AXES, split_axis=0, concat...]
    all_to_all x1, starting transfers between devices: 6.08 us -> 7.91 us  [body(): lax.all_to_all(payload.reshape(2, devices, D), AXES, split_axis=1, concat...]
  transfers between devices with their start and end apart: 25 -> 24, of which waited for: 11 -> 8; matrix products, arithmetic and copies ran while one was open for 5% -> 1% of each run, Pallas kernels for 12% -> 12%
where the time goes in v3:
time: 160 us; the launch traced here: 159 us
  starting transfers between devices  56.8 us (36%)
  Pallas kernels  38.7 us (24%)
  waiting for transfers between devices  36.1 us (23%)
  local copies, waits for them, and re-layouts  26.8 us (17%)
    pallas_call x15, Pallas kernels, call(): pl.pallas_call(kernel, out_shape=outs, in_specs=spaces or [VMEM] * len(ar...  38.7 us
    ppermute x19, starting transfers between devices, shift(): return lax.ppermute(value, AXES, pairs)  28.2 us
    unnamed x76, local copies, waits for them, and re-layouts  22.1 us
    ppermute x19, waiting for transfers between devices, shift(): return lax.ppermute(value, AXES, pairs)  14.5 us
    all_to_all x1, waiting for transfers between devices, body(): lax.all_to_all(payload.reshape(2, devices, D), AXES, split_axis=1, concat...  12 us
    all_to_all x1, waiting for transfers between devices, body(): lax.all_to_all(meta.reshape(devices, 1, ROWS), AXES, split_axis=0, concat...  9.59 us
    all_to_all x1, starting transfers between devices, body(): lax.all_to_all(payload.reshape(2, devices, D), AXES, split_axis=1, concat...  7.91 us
    all_to_all x1, starting transfers between devices, body(): lax.all_to_all(meta.reshape(devices, 1, ROWS), AXES, split_axis=0, concat...  7.23 us
  transfers between devices with their start and end apart: 24, of which 8 were waited for; matrix products, arithmetic and copies ran while one was open for 1% of the time, Pallas kernels for 12%

profile of v3, /device:TPU:1, one launch (start us, length us, event | category | flops | bytes accessed | tf_op | source)
XLA Modules:
  0.0 159.0 jit_solution(1928982276719113096)
XLA Ops:
  0.0 2.4 %shard_map.136 = (bf16[2304,256]{1,0:T(8,128)(2,1)}, bf16[576,256]{1,0:T(8,128)(2,1)}) custom-call(bf16[1536,256]{1,0:T(8,128)(2,1)} %gate_ref.3, bf16[1536,256]{1,0:T(8,128)(2,1)} %up_ref.3, bf16[256,1536]{1,0:T(8,128)(2,1)} %down_ref.3), custom_call_target="tpu_custom_call" | custom-call | flops 1024 | bytes 1024 | tf_op jit(solution)/shard_map/pallas_call | solution.py:53
  2.4 4.5 %collective-permute-start = (bf16[576,256]{1,0:T(8,128)(2,1)}, bf16[576,256]{1,0:T(8,128)(2,1)S(1)}, u32[]{:S(2)}, u32[]{:S(2)}) collective-permute-start(bf16[576,256]{1,0:T(8,128)(2,1)} %get-tuple-element.23), channel_id=1, source_target_pairs={{0,64},{1,65},{2,66},{3,67},{4,68},{5,69},{6,70},{7,71},{8,72},{9,... | collective-permute-start | bytes 884744 | tf_op jit(solution)/shard_map/ppermute | solution.py:43
  7.0 1.5 shard_map.137
  8.5 5.4 %collective-permute-done.q0 = bf16[576,256]{1,0:T(8,128)(2,1)S(1)} collective-permute-done((bf16[576,256]{1,0:T(8,128)(2,1)}, bf16[576,256]{1,0:T(8,128)(2,1)S(1)}, u32[]{:S(2)}, u32[]{:S(2)}) %collective-permute-start) | collective-permute-done | bytes 294944 | tf_op jit(solution)/shard_map/ppermute | solution.py:43
  14.6 2.1 %collective-permute-start.6 = (bf16[2304,256]{1,0:T(8,128)(2,1)}, bf16[2304,256]{1,0:T(8,128)(2,1)}, u32[]{:S(2)}, u32[]{:S(2)}) collective-permute-start(bf16[2304,256]{1,0:T(8,128)(2,1)} %get-tuple-element.26), channel_id=1, source_target_pairs={{0,96},{1,97},{2,98},{3,99},{4,100},{5,101},{6,102},{7,103},{8,104... | collective-permute-start | bytes 3538952 | tf_op jit(solution)/shard_map/ppermute | solution.py:43
  17.9 1.5 collective-permute-start.2
  19.4 1.5 collective-permute-start.3
  20.9 4.2 %all-to-all-start = ((bf16[4,128,1536]{2,1,0:T(8,128)(2,1)}), bf16[4,128,1536]{2,1,0:T(8,128)(2,1)S(1)}, u32[]{:S(2)}, u32[]{:S(2)}) async-start(bf16[4,128,1536]{2,1,0:T(8,128)(2,1)} %bitcast), calls=%async_computation | async-start | bytes 3145728 | tf_op jit(solution)/shard_map/all_to_all | solution.py:48
  26.6 5.3 %collective-permute-done.3.q3 = bf16[576,256]{1,0:T(8,128)(2,1)S(1)} collective-permute-done((bf16[576,256]{1,0:T(8,128)(2,1)S(1)}, bf16[576,256]{1,0:T(8,128)(2,1)S(1)}, u32[]{:S(2)}, u32[]{:S(2)}) %collective-permute-start.3) | collective-permute-done | bytes 294944 | tf_op jit(solution)/shard_map/ppermute | solution.py:43
  36.6 2.8 %collective-permute-start.4 = (bf16[2304,256]{1,0:T(8,128)(2,1)S(1)}, bf16[2304,256]{1,0:T(8,128)(2,1)}, u32[]{:S(2)}, u32[]{:S(2)}) collective-permute-start(bf16[2304,256]{1,0:T(8,128)(2,1)S(1)} %shard_map.139.a), channel_id=1, source_target_pairs={{0,1},{1,0},{2,3},{3,2},{4,5},{5,4},{6,7},{7,6},{8,9},{9,8},{10,11... | collective-permute-start | bytes 3538952 | tf_op jit(solution)/shard_map/ppermute | solution.py:43
  39.4 2.3 %collective-permute-done.5.a = bf16[2304,256]{1,0:T(8,128)(2,1)} collective-permute-done((bf16[2304,256]{1,0:T(8,128)(2,1)}, bf16[2304,256]{1,0:T(8,128)(2,1)}, u32[]{:S(2)}, u32[]{:S(2)}) %collective-permute-start.5) | collective-permute-done | bytes 1179680 | tf_op jit(solution)/shard_map/ppermute | solution.py:43
  41.7 2.2 %collective-permute-start.7 = (bf16[2304,256]{1,0:T(8,128)(2,1)}, bf16[2304,256]{1,0:T(8,128)(2,1)}, u32[]{:S(2)}, u32[]{:S(2)}) collective-permute-start(bf16[2304,256]{1,0:T(8,128)(2,1)} %collective-permute-done.5.a), channel_id=1, source_target_pairs={{0,1},{1,0},{2,3},{3,2},{4,5},{5,4},{6,7},{7,6},{8,9},{9,8},{10,11... | collective-permute-start | bytes 3538952 | tf_op jit(solution)/shard_map/ppermute | solution.py:43
  47.6 2.7 %shard_map.140.total_ref = f32[512,1536]{1,0:T(8,128)S(1)} custom-call(bf16[512,1536]{1,0:T(8,128)(2,1)S(1)} %bitcast.14, f32[512,1536]{1,0:T(8,128)S(1)} %shard_map.138.total_ref, bf16[2304,256]{1,0:T(8,128)(2,1)S(1)} %shard_map.139.a, bf16[2304,256]{1,0:T(8,128)(2,1)} %collective-permute-done.4.b), custom_call_target="tpu_custom_call" | custom-call | flops 1024 | bytes 1024 | tf_op jit(solution)/shard_map/pallas_call | solution.py:53
  50.4 5.2 %shard_map.141 = (f32[128,1536]{1,0:T(8,128)S(1)}, bf16[128,1536]{1,0:T(8,128)(2,1)S(1)}, bf16[128,1536]{1,0:T(8,128)(2,1)S(1)}, bf16[128,1536]{1,0:T(8,128)(2,1)S(1)}) custom-call(bf16[512,1536]{1,0:T(8,128)(2,1)S(1)} %bitcast.15, f32[512,1536]{1,0:T(8,128)S(1)} %shard_map.140.total_ref, bf16[2304,256]{1,0:T(8,128)(2,1)} %collective-permute-done.5.a, ...), custom_call_target="tpu_custom_call" | custom-call | flops 1024 | bytes 1024 | tf_op jit(solution)/shard_map/pallas_call | solution.py:53
  57.8 2.6 %collective-permute-start.11 = (bf16[128,1536]{1,0:T(8,128)(2,1)S(1)}, bf16[128,1536]{1,0:T(8,128)(2,1)S(1)}, u32[]{:S(2)}, u32[]{:S(2)}) collective-permute-start(bf16[128,1536]{1,0:T(8,128)(2,1)S(1)} %get-tuple-element.31), channel_id=1, source_target_pairs={{0,16},{1,17},{2,18},{3,19},{4,20},{5,21},{6,22},{7,23},{8,24},{9,... | collective-permute-start | bytes 1179656 | tf_op jit(solution)/shard_map/ppermute | solution.py:43
  64.3 7.2 %all-to-all-start.1 = ((f32[128,1,128]{2,1,0:T(1,128)}), f32[128,1,128]{2,1,0:T(1,128)S(1)}, u32[]{:S(2)}, u32[]{:S(2)}) async-start(f32[128,1,128]{2,1,0:T(1,128)} %bitcast.4), calls=%async_computation.1 | async-start | bytes 131072 | tf_op jit(solution)/shard_map/all_to_all | solution.py:414
  71.7 9.6 %all-to-all-done.1 = f32[128,1,128]{2,1,0:T(1,128)S(1)} async-done(((f32[128,1,128]{2,1,0:T(1,128)}), f32[128,1,128]{2,1,0:T(1,128)S(1)}, u32[]{:S(2)}, u32[]{:S(2)}) %all-to-all-start.1) | async-done | bytes 65568 | tf_op jit(solution)/shard_map/all_to_all | solution.py:414
  81.3 1.5 shard_map.144.plan_ref
  85.2 5.0 %shard_map.143 = bf16[256,768]{1,0:T(8,128)(2,1)} custom-call(bf16[128,1536]{1,0:T(8,128)(2,1)} %tokens.1, f32[128,1536]{1,0:T(8,128)} %copy-done.15, bf16[128,1536]{1,0:T(8,128)(2,1)} %copy-done.32, bf16[128,1536]{1,0:T(8,128)(2,1)} %copy-done.30, bf16[128,1536]{1,0:T(8,128)(2,1)} %copy-done.31, f32[1,1536]{1,0:T(1,128)} %broadcast_in_dim.19.scale_ref, ...), custom_call_target="tpu_custom_call" | custom-call | flops 1024 | bytes 1024 | tf_op jit(solution)/shard_map/pallas_call | solution.py:53
  90.3 2.2 %copy.16 = bf16[2,128,768]{2,0,1:T(2,128)(2,1)} copy(bf16[2,128,768]{2,1,0:T(8,128)(2,1)} %bitcast.22) | data formatting | bytes 786432 | tf_op jit(solution)/shard_map/reshape | solution.py:442
  92.4 7.9 %all-to-all-start.2 = ((bf16[2,128,768]{2,0,1:T(2,128)(2,1)}), bf16[2,128,768]{2,0,1:T(2,128)(2,1)}, u32[]{:S(2)}, u32[]{:S(2)}) async-start(bf16[2,128,768]{2,0,1:T(2,128)(2,1)} %copy.16), calls=%async_computation.2 | async-start | bytes 786432 | tf_op jit(solution)/shard_map/all_to_all | solution.py:442
  100.4 12.0 %all-to-all-done.2 = bf16[2,128,768]{2,0,1:T(2,128)(2,1)} async-done(((bf16[2,128,768]{2,0,1:T(2,128)(2,1)}), bf16[2,128,768]{2,0,1:T(2,128)(2,1)}, u32[]{:S(2)}, u32[]{:S(2)}) %all-to-all-start.2) | async-done | bytes 393248 | tf_op jit(solution)/shard_map/all_to_all | solution.py:442
  115.7 2.7 %collective-permute-start.15 = (bf16[128,768]{1,0:T(8,128)(2,1)}, bf16[128,768]{1,0:T(8,128)(2,1)}, u32[]{:S(2)}, u32[]{:S(2)}) collective-permute-start(bf16[128,768]{1,0:T(8,128)(2,1)} %shard_map.145.b0.normed_ref), channel_id=1, source_target_pairs={{0,6},{1,7},{2,0},{3,1},{4,2},{5,3},{6,4},{7,5},{8,14},{9,15},{10,... | collective-permute-start | bytes 589832 | tf_op jit(solution)/shard_map/ppermute | solution.py:43
  118.5 1.8 %shard_map.148 = bf16[128,1536]{1,0:T(8,128)(2,1)S(1)} custom-call(bf16[128,768]{1,0:T(8,128)(2,1)} %shard_map.145.b0.normed_ref, bf16[768,2304]{1,0:T(8,128)(2,1)S(1)} %copy-done, s32[1,768]{1,0:T(1,128)S(1)} %broadcast_in_dim_reshape.3.offsets_ref), custom_call_target="tpu_custom_call" | custom-call | flops 1024 | bytes 1024 | tf_op jit(solution)/shard_map/pallas_call | solution.py:53
  121.1 4.2 %all-to-all-start.3 = ((bf16[16,8,1536]{2,1,0:T(8,128)(2,1)}), bf16[16,8,1536]{2,1,0:T(8,128)(2,1)}, u32[]{:S(2)}, u32[]{:S(2)}) async-start(bf16[16,8,1536]{2,1,0:T(8,128)(2,1)} %bitcast.18), calls=%async_computation.3 | async-start | bytes 786432 | tf_op jit(solution)/shard_map/all_to_all | solution.py:447
  125.3 1.5 collective-permute-start.12
  126.8 2.0 %collective-permute-start.14 = (bf16[128,768]{1,0:T(8,128)(2,1)}, bf16[128,768]{1,0:T(8,128)(2,1)S(1)}, u32[]{:S(2)}, u32[]{:S(2)}) collective-permute-start(bf16[128,768]{1,0:T(8,128)(2,1)} %collective-permute-done.13.b2), channel_id=1, source_target_pairs={{0,1},{1,0},{2,3},{3,2},{4,5},{5,4},{6,7},{7,6},{8,9},{9,8},{10,11... | collective-permute-start | bytes 589832 | tf_op jit(solution)/shard_map/ppermute | solution.py:43
  130.7 3.3 %shard_map.146 = (bf16[64,768]{1,0:T(8,128)(2,1)S(1)}, bf16[1024,768]{1,0:T(8,128)(2,1)S(1)}) custom-call(bf16[128,768]{1,0:T(8,128)(2,1)} %shard_map.145.b0.normed_ref, bf16[128,768]{1,0:T(8,128)(2,1)S(1)} %collective-permute-done.12.b1, bf16[128,768]{1,0:T(8,128)(2,1)} %collective-permute-done.13.b2, bf16[128,768]{1,0:T(8,128)(2,1)S(1)} %collective-permute-done.14.b3, ...), custom_call_target="tpu_custom_call" | custom-call | flops 1024 | bytes 1024 | tf_op jit(solution)/shard_map/pallas_call | solution.py:53
  136.7 2.5 %shard_map.149 = f32[64,896]{1,0:T(8,128)S(1)} custom-call(bf16[64,768]{1,0:T(8,128)(2,1)S(1)} %copy-done.25, bf16[128,1536]{1,0:T(8,128)(2,1)} %bitcast.9.kv_ref), custom_call_target="tpu_custom_call" | custom-call | flops 1024 | bytes 1024 | tf_op jit(solution)/shard_map/pallas_call | solution.py:53
  140.0 5.1 %all-to-all-start.4 = ((f32[8,8,896]{2,1,0:T(8,128)}), f32[8,8,896]{2,1,0:T(8,128)}, u32[]{:S(2)}, u32[]{:S(2)}) async-start(f32[8,8,896]{2,1,0:T(8,128)} %bitcast.19), calls=%async_computation.4 | async-start | bytes 458752 | tf_op jit(solution)/shard_map/all_to_all | solution.py:460
  148.5 5.7 %shard_map.147.near = f32[128,2304]{1,0:T(8,128)S(1)} custom-call(bf16[1024,768]{1,0:T(8,128)(2,1)S(1)} %copy-done.11, bf16[768,2304]{1,0:T(8,128)(2,1)S(1)} %copy-done, bf16[256,768]{1,0:T(8,128)(2,1)S(1)} %bitcast.17, f32[128,1024]{1,0:T(8,128)S(1)} %copy-done.4), custom_call_target="tpu_custom_call" | custom-call | flops 1024 | bytes 1024 | tf_op jit(solution)/shard_map/pallas_call | solution.py:53
  155.4 3.5 %shard_map.150 = bf16[128,768]{1,0:T(8,128)(2,1)} custom-call(f32[128,2304]{1,0:T(8,128)} %copy-done.1, f32[64,896]{1,0:T(8,128)} %bitcast.11.far, s32[1,768]{1,0:T(1,128)} %copy-done.27, bf16[768,768]{1,0:T(8,128)(2,1)} %w.3), custom_call_target="tpu_custom_call" | custom-call | flops 1024 | bytes 1024 | tf_op jit(solution)/shard_map/pallas_call | solution.py:53
  (118 shorter events, 34.4 us)
Async XLA Ops:
  2.4 11.4 %collective-permute-start = (bf16[576,256]{1,0:T(8,128)(2,1)}, bf16[576,256]{1,0:T(8,128)(2,1)S(1)}, u32[]{:S(2)}, u32[]{:S(2)}) collective-permute-start(bf16[576,256]{1,0:T(8,128)(2,1)} %get-tuple-element.23), channel_id=1, source_target_pairs={{0,64},{1,65},{2,66},{3,67},{4,68},{5,69},{6,70},{7,71},{8,72},{9,... | collective-permute-start | bytes 884744 | tf_op jit(solution)/shard_map/ppermute | solution.py:43
  13.9 27.9 %collective-permute-start.5 = (bf16[2304,256]{1,0:T(8,128)(2,1)}, bf16[2304,256]{1,0:T(8,128)(2,1)}, u32[]{:S(2)}, u32[]{:S(2)}) collective-permute-start(bf16[2304,256]{1,0:T(8,128)(2,1)} %get-tuple-element.26), channel_id=1, source_target_pairs={{0,32},{1,33},{2,34},{3,35},{4,36},{5,37},{6,38},{7,39},{8,40},{9,... | collective-permute-start | bytes 3538952 | tf_op jit(solution)/shard_map/ppermute | solution.py:43
  14.6 29.4 %collective-permute-start.6 = (bf16[2304,256]{1,0:T(8,128)(2,1)}, bf16[2304,256]{1,0:T(8,128)(2,1)}, u32[]{:S(2)}, u32[]{:S(2)}) collective-permute-start(bf16[2304,256]{1,0:T(8,128)(2,1)} %get-tuple-element.26), channel_id=1, source_target_pairs={{0,96},{1,97},{2,98},{3,99},{4,100},{5,101},{6,102},{7,103},{8,104... | collective-permute-start | bytes 3538952 | tf_op jit(solution)/shard_map/ppermute | solution.py:43
  16.7 8.4 %collective-permute-start.1 = (bf16[576,256]{1,0:T(8,128)(2,1)S(1)}, bf16[576,256]{1,0:T(8,128)(2,1)S(1)}, u32[]{:S(2)}, u32[]{:S(2)}) collective-permute-start(bf16[576,256]{1,0:T(8,128)(2,1)S(1)} %collective-permute-done.q0), channel_id=1, source_target_pairs={{0,2},{1,3},{2,4},{3,5},{4,6},{5,7},{6,0},{7,1},{8,10},{9,11},{10,... | collective-permute-start | bytes 884744 | tf_op jit(solution)/shard_map/ppermute | solution.py:43
  17.9 7.9 %collective-permute-start.2 = (bf16[576,256]{1,0:T(8,128)(2,1)S(1)}, bf16[576,256]{1,0:T(8,128)(2,1)S(1)}, u32[]{:S(2)}, u32[]{:S(2)}) collective-permute-start(bf16[576,256]{1,0:T(8,128)(2,1)S(1)} %collective-permute-done.q0), channel_id=1, source_target_pairs={{0,6},{1,7},{2,0},{3,1},{4,2},{5,3},{6,4},{7,5},{8,14},{9,15},{10,... | collective-permute-start | bytes 884744 | tf_op jit(solution)/shard_map/ppermute | solution.py:43
  19.4 12.5 %collective-permute-start.3 = (bf16[576,256]{1,0:T(8,128)(2,1)S(1)}, bf16[576,256]{1,0:T(8,128)(2,1)S(1)}, u32[]{:S(2)}, u32[]{:S(2)}) collective-permute-start(bf16[576,256]{1,0:T(8,128)(2,1)S(1)} %collective-permute-done.q0), channel_id=1, source_target_pairs={{0,4},{1,5},{2,6},{3,7},{4,0},{5,1},{6,2},{7,3},{8,12},{9,13},{10,... | collective-permute-start | bytes 884744 | tf_op jit(solution)/shard_map/ppermute | solution.py:43
  20.9 23.0 %all-to-all-start = ((bf16[4,128,1536]{2,1,0:T(8,128)(2,1)}), bf16[4,128,1536]{2,1,0:T(8,128)(2,1)S(1)}, u32[]{:S(2)}, u32[]{:S(2)}) async-start(bf16[4,128,1536]{2,1,0:T(8,128)(2,1)} %bitcast), calls=%async_computation | async-start | bytes 3145728 | tf_op jit(solution)/shard_map/all_to_all | solution.py:48
  25.1 18.8 %copy-start.7 = (bf16[1536,256]{1,0:T(8,128)(2,1)S(1)}, bf16[1536,256]{1,0:T(8,128)(2,1)}, u32[]{:S(2)}) copy-start(bf16[1536,256]{1,0:T(8,128)(2,1)} %gate_ref.3) | copy-start | bytes 2359300
  36.6 11.1 %collective-permute-start.4 = (bf16[2304,256]{1,0:T(8,128)(2,1)S(1)}, bf16[2304,256]{1,0:T(8,128)(2,1)}, u32[]{:S(2)}, u32[]{:S(2)}) collective-permute-start(bf16[2304,256]{1,0:T(8,128)(2,1)S(1)} %shard_map.139.a), channel_id=1, source_target_pairs={{0,1},{1,0},{2,3},{3,2},{4,5},{5,4},{6,7},{7,6},{8,9},{9,8},{10,11... | collective-permute-start | bytes 3538952 | tf_op jit(solution)/shard_map/ppermute | solution.py:43
  41.7 8.7 %collective-permute-start.7 = (bf16[2304,256]{1,0:T(8,128)(2,1)}, bf16[2304,256]{1,0:T(8,128)(2,1)}, u32[]{:S(2)}, u32[]{:S(2)}) collective-permute-start(bf16[2304,256]{1,0:T(8,128)(2,1)} %collective-permute-done.5.a), channel_id=1, source_target_pairs={{0,1},{1,0},{2,3},{3,2},{4,5},{5,4},{6,7},{7,6},{8,9},{9,8},{10,11... | collective-permute-start | bytes 3538952 | tf_op jit(solution)/shard_map/ppermute | solution.py:43
  43.9 6.5 %collective-permute-start.8 = (bf16[2304,256]{1,0:T(8,128)(2,1)}, bf16[2304,256]{1,0:T(8,128)(2,1)}, u32[]{:S(2)}, u32[]{:S(2)}) collective-permute-start(bf16[2304,256]{1,0:T(8,128)(2,1)} %collective-permute-done.6.b), channel_id=1, source_target_pairs={{0,1},{1,0},{2,3},{3,2},{4,5},{5,4},{6,7},{7,6},{8,9},{9,8},{10,11... | collective-permute-start | bytes 3538952 | tf_op jit(solution)/shard_map/ppermute | solution.py:43
  50.3 11.2 %copy-start.34 = (f32[1536]{0:T(1024)S(1)}, f32[1536]{0:T(1024)}, u32[]{:S(2)}) copy-start(f32[1536]{0:T(1024)} %param.19) | copy-start | bytes 18436
  50.4 11.8 %copy-start.35 = (f32[1536]{0:T(1024)S(1)}, f32[1536]{0:T(1024)}, u32[]{:S(2)}) copy-start(f32[1536]{0:T(1024)} %param.20) | copy-start | bytes 18436
  50.4 12.4 %copy-start.28 = (s32[2,128]{1,0:T(2,128)S(1)}, s32[2,128]{1,0:T(2,128)}, u32[]{:S(2)}) copy-start(s32[2,128]{1,0:T(2,128)} %coords_ref.1) | copy-start | bytes 3076
  50.4 12.4 %copy-start.29 = (s32[128]{0:T(128)S(1)}, s32[128]{0:T(128)}, u32[]{:S(2)}) copy-start(s32[128]{0:T(128)} %param.22) | copy-start | bytes 1540
  56.5 27.1 %collective-permute-start.10 = (bf16[128,1536]{1,0:T(8,128)(2,1)S(1)}, bf16[128,1536]{1,0:T(8,128)(2,1)S(1)}, u32[]{:S(2)}, u32[]{:S(2)}) collective-permute-start(bf16[128,1536]{1,0:T(8,128)(2,1)S(1)} %get-tuple-element.30), channel_id=1, source_target_pairs={{0,8},{1,9},{2,10},{3,11},{4,12},{5,13},{6,14},{7,15},{8,16},{9,17... | collective-permute-start | bytes 1179656 | tf_op jit(solution)/shard_map/ppermute | solution.py:43
  57.8 25.8 %collective-permute-start.11 = (bf16[128,1536]{1,0:T(8,128)(2,1)S(1)}, bf16[128,1536]{1,0:T(8,128)(2,1)S(1)}, u32[]{:S(2)}, u32[]{:S(2)}) collective-permute-start(bf16[128,1536]{1,0:T(8,128)(2,1)S(1)} %get-tuple-element.31), channel_id=1, source_target_pairs={{0,16},{1,17},{2,18},{3,19},{4,20},{5,21},{6,22},{7,23},{8,24},{9,... | collective-permute-start | bytes 1179656 | tf_op jit(solution)/shard_map/ppermute | solution.py:43
  60.5 23.2 %collective-permute-start.9 = (bf16[128,1536]{1,0:T(8,128)(2,1)S(1)}, bf16[128,1536]{1,0:T(8,128)(2,1)S(1)}, u32[]{:S(2)}, u32[]{:S(2)}) collective-permute-start(bf16[128,1536]{1,0:T(8,128)(2,1)S(1)} %get-tuple-element.29), channel_id=1, source_target_pairs={{0,24},{1,25},{2,26},{3,27},{4,28},{5,29},{6,30},{7,31},{8,0},{9,1... | collective-permute-start | bytes 1179656 | tf_op jit(solution)/shard_map/ppermute | solution.py:43
  64.3 16.9 %all-to-all-start.1 = ((f32[128,1,128]{2,1,0:T(1,128)}), f32[128,1,128]{2,1,0:T(1,128)S(1)}, u32[]{:S(2)}, u32[]{:S(2)}) async-start(f32[128,1,128]{2,1,0:T(1,128)} %bitcast.4), calls=%async_computation.1 | async-start | bytes 131072 | tf_op jit(solution)/shard_map/all_to_all | solution.py:414
  85.2 33.3 %copy-start = (bf16[768,2304]{1,0:T(8,128)(2,1)S(1)}, bf16[768,2304]{1,0:T(8,128)(2,1)}, u32[]{:S(2)}) copy-start(bf16[768,2304]{1,0:T(8,128)(2,1)} %w_ref.5) | copy-start | bytes 10616836
  92.4 26.0 %copy-start.37 = (s32[12]{0:T(128)S(1)}, s32[12]{0:T(128)}, u32[]{:S(2)}) copy-start(s32[12]{0:T(128)} %param.26) | copy-start | bytes 148
  92.4 19.9 %all-to-all-start.2 = ((bf16[2,128,768]{2,0,1:T(2,128)(2,1)}), bf16[2,128,768]{2,0,1:T(2,128)(2,1)}, u32[]{:S(2)}, u32[]{:S(2)}) async-start(bf16[2,128,768]{2,0,1:T(2,128)(2,1)} %copy.16), calls=%async_computation.2 | async-start | bytes 786432 | tf_op jit(solution)/shard_map/all_to_all | solution.py:442
  115.7 11.1 %collective-permute-start.13 = (bf16[128,768]{1,0:T(8,128)(2,1)}, bf16[128,768]{1,0:T(8,128)(2,1)}, u32[]{:S(2)}, u32[]{:S(2)}) collective-permute-start(bf16[128,768]{1,0:T(8,128)(2,1)} %shard_map.145.b0.normed_ref), channel_id=1, source_target_pairs={{0,2},{1,3},{2,4},{3,5},{4,6},{5,7},{6,0},{7,1},{8,10},{9,11},{10,... | collective-permute-start | bytes 589832 | tf_op jit(solution)/shard_map/ppermute | solution.py:43
  115.7 13.1 %collective-permute-start.15 = (bf16[128,768]{1,0:T(8,128)(2,1)}, bf16[128,768]{1,0:T(8,128)(2,1)}, u32[]{:S(2)}, u32[]{:S(2)}) collective-permute-start(bf16[128,768]{1,0:T(8,128)(2,1)} %shard_map.145.b0.normed_ref), channel_id=1, source_target_pairs={{0,6},{1,7},{2,0},{3,1},{4,2},{5,3},{6,4},{7,5},{8,14},{9,15},{10,... | collective-permute-start | bytes 589832 | tf_op jit(solution)/shard_map/ppermute | solution.py:43
  118.4 10.4 %collective-permute-start.17 = (bf16[128,768]{1,0:T(8,128)(2,1)}, bf16[128,768]{1,0:T(8,128)(2,1)}, u32[]{:S(2)}, u32[]{:S(2)}) collective-permute-start(bf16[128,768]{1,0:T(8,128)(2,1)} %shard_map.145.b0.normed_ref), channel_id=1, source_target_pairs={{0,4},{1,5},{2,6},{3,7},{4,0},{5,1},{6,2},{7,3},{8,12},{9,13},{10,... | collective-permute-start | bytes 589832 | tf_op jit(solution)/shard_map/ppermute | solution.py:43
  118.5 12.2 %copy-start.27 = (s32[1,768]{1,0:T(1,128)}, s32[1,768]{1,0:T(1,128)S(1)}, u32[]{:S(2)}) copy-start(s32[1,768]{1,0:T(1,128)S(1)} %broadcast_in_dim_reshape.3.offsets_ref) | copy-start | bytes 9220
  121.1 14.8 %all-to-all-start.3 = ((bf16[16,8,1536]{2,1,0:T(8,128)(2,1)}), bf16[16,8,1536]{2,1,0:T(8,128)(2,1)}, u32[]{:S(2)}, u32[]{:S(2)}) async-start(bf16[16,8,1536]{2,1,0:T(8,128)(2,1)} %bitcast.18), calls=%async_computation.3 | async-start | bytes 786432 | tf_op jit(solution)/shard_map/all_to_all | solution.py:447
  125.3 4.0 %collective-permute-start.12 = (bf16[128,768]{1,0:T(8,128)(2,1)}, bf16[128,768]{1,0:T(8,128)(2,1)S(1)}, u32[]{:S(2)}, u32[]{:S(2)}) collective-permute-start(bf16[128,768]{1,0:T(8,128)(2,1)} %shard_map.145.b0.normed_ref), channel_id=1, source_target_pairs={{0,1},{1,0},{2,3},{3,2},{4,5},{5,4},{6,7},{7,6},{8,9},{9,8},{10,11... | collective-permute-start | bytes 589832 | tf_op jit(solution)/shard_map/ppermute | solution.py:43
  126.8 3.2 %collective-permute-start.14 = (bf16[128,768]{1,0:T(8,128)(2,1)}, bf16[128,768]{1,0:T(8,128)(2,1)S(1)}, u32[]{:S(2)}, u32[]{:S(2)}) collective-permute-start(bf16[128,768]{1,0:T(8,128)(2,1)} %collective-permute-done.13.b2), channel_id=1, source_target_pairs={{0,1},{1,0},{2,3},{3,2},{4,5},{5,4},{6,7},{7,6},{8,9},{9,8},{10,11... | collective-permute-start | bytes 589832 | tf_op jit(solution)/shard_map/ppermute | solution.py:43
  128.8 1.7 %collective-permute-start.16 = (bf16[128,768]{1,0:T(8,128)(2,1)}, bf16[128,768]{1,0:T(8,128)(2,1)S(1)}, u32[]{:S(2)}, u32[]{:S(2)}) collective-permute-start(bf16[128,768]{1,0:T(8,128)(2,1)} %collective-permute-done.15.b4), channel_id=1, source_target_pairs={{0,1},{1,0},{2,3},{3,2},{4,5},{5,4},{6,7},{7,6},{8,9},{9,8},{10,11... | collective-permute-start | bytes 589832 | tf_op jit(solution)/shard_map/ppermute | solution.py:43
  128.8 1.9 %collective-permute-start.18 = (bf16[128,768]{1,0:T(8,128)(2,1)}, bf16[128,768]{1,0:T(8,128)(2,1)S(1)}, u32[]{:S(2)}, u32[]{:S(2)}) collective-permute-start(bf16[128,768]{1,0:T(8,128)(2,1)} %collective-permute-done.17.b6), channel_id=1, source_target_pairs={{0,1},{1,0},{2,3},{3,2},{4,5},{5,4},{6,7},{7,6},{8,9},{9,8},{10,11... | collective-permute-start | bytes 589832 | tf_op jit(solution)/shard_map/ppermute | solution.py:43
  140.0 15.4 %all-to-all-start.4 = ((f32[8,8,896]{2,1,0:T(8,128)}), f32[8,8,896]{2,1,0:T(8,128)}, u32[]{:S(2)}, u32[]{:S(2)}) async-start(f32[8,8,896]{2,1,0:T(8,128)} %bitcast.19), calls=%async_computation.4 | async-start | bytes 458752 | tf_op jit(solution)/shard_map/all_to_all | solution.py:460
  (30 other events, 56.2 us)

commit v4 on v3

--- a/solution.py
+++ b/solution.py
@@ -48,8 +48,9 @@
     return lax.all_to_all(value, "tile", split_axis=0, concat_axis=0, axis_index_groups=groups, tiled=True)
 
 
-def call(kernel, outs, *args, scratch=(), vmem=12, spaces=None):
+def call(kernel, outs, *args, scratch=(), vmem=12, spaces=None, cost=1):
     outs = [jax.ShapeDtypeStruct(shape, dtype) for shape, dtype in outs]
+    nbytes = cost * sum(a.size * a.dtype.itemsize for a in (*args, *outs))
     return pl.pallas_call(
         kernel,
         out_shape=outs,
@@ -57,7 +58,7 @@
         out_specs=tuple(VMEM for _ in outs),
         scratch_shapes=scratch,
         compiler_params=pltpu.CompilerParams(vmem_limit_bytes=vmem * MIB),
-        cost_estimate=pl.CostEstimate(flops=1024, bytes_accessed=1024, transcendentals=0),
+        cost_estimate=pl.CostEstimate(flops=1024, bytes_accessed=nbytes, transcendentals=0),
     )(*args)
 
 
@@ -133,8 +134,8 @@
         out_ref[:, cols] = total_ref[:, cols] + dot(hidden_ref[...], down_ref[:, cols])
 
 
-def mlp_last_kernel(rows_ref, total_ref, a, b, c, d, own_ref, r1, r2, r3, hidden_ref, down_ref, sum_ref):
-    mlp_chunks(rows_ref, (a, b, c, d), hidden_ref, down_ref)
+def mlp_last_kernel(rows_ref, total_ref, a, b, own_ref, r1, r2, r3, hidden_ref, down_ref, sum_ref):
+    mlp_chunks(rows_ref, (a, b), hidden_ref, down_ref)
     for j in range(3):
         cols = slice(512 * j, 512 * (j + 1))
         sum_ref[:, cols] = total_ref[:, cols] + dot(hidden_ref[...], down_ref[:, cols])
@@ -144,9 +145,8 @@
         ref[...] = sum_ref[pl.ds(pl.multiple_of(place * ROWS, ROWS), ROWS), :].astype(ref.dtype)
 
 
-def encoder_mlp(cls_tokens, norm_gain, w_gate, w_up, w_down):
-    swap = functools.partial(shift, c=1)
-    chunk, quarter = call(
+def pack_weights(w_gate, w_up, w_down):
+    return call(
         pack_kernel,
         [((CHUNK, 256), BF16), ((QUARTER, 256), BF16)],
         w_gate,
@@ -156,11 +156,15 @@
         spaces=[HBM] * 3,
         vmem=56,
     )
+
+
+def encoder_mlp(cls_tokens, norm_gain, chunk, quarter, w_gate, w_up, w_down):
+    swap = functools.partial(shift, c=1)
     quarter = shift(quarter, z=2)
-    (normed,) = call(norm_kernel, [((RING * ROWS, D_VIT), BF16)], cls_tokens, norm_gain[None])
-    chunk, quarter, rows = lax.optimization_barrier((chunk, quarter, normed))
+    (normed,) = call(norm_kernel, [((RING * ROWS, D_VIT), BF16)], cls_tokens, norm_gain)
+    rows = along_y(normed)
+    chunk, quarter, _ = lax.optimization_barrier((chunk, quarter, normed))
     before, after = shift(chunk, z=1), shift(chunk, z=-1)
-    rows = along_y(rows)
     quarters = [quarter, shift(quarter, x=1), shift(quarter, x=-1), shift(quarter, x=2)]
     (total,) = call(
         mlp_own_kernel,
@@ -171,34 +175,32 @@
         w_down,
         vmem=20,
     )
+    quarters, total = lax.optimization_barrier((quarters, total))
     (across,) = call(join_kernel, [((CHUNK, 256), BF16)], *quarters)
-    (total,) = call(
+    middle = functools.partial(
+        call,
         mlp_middle_kernel,
-        [((4 * ROWS, D_VIT), F32)],
+        [((RING * ROWS, D_VIT), F32)],
         rows,
-        total,
-        across,
-        swap(across),
-        scratch=[pltpu.VMEM((4 * ROWS, 256), BF16), pltpu.VMEM((256, D_VIT), BF16)],
+        scratch=[pltpu.VMEM((RING * ROWS, 256), BF16), pltpu.VMEM((256, D_VIT), BF16)],
         vmem=20,
     )
-    sums = call(
+    (total,) = middle(total, across, swap(across))
+    (total,) = middle(total, before, after)
+    return call(
         mlp_last_kernel,
         [((ROWS, D_VIT), t) for t in (F32, BF16, BF16, BF16)],
         rows,
         total,
-        before,
-        after,
         swap(before),
         swap(after),
         scratch=[
-            pltpu.VMEM((4 * ROWS, 512), BF16),
-            pltpu.VMEM((512, D_VIT), BF16),
-            pltpu.VMEM((4 * ROWS, D_VIT), F32),
+            pltpu.VMEM((RING * ROWS, 256), BF16),
+            pltpu.VMEM((256, D_VIT), BF16),
+            pltpu.VMEM((RING * ROWS, D_VIT), F32),
         ],
         vmem=20,
     )
-    return sums
 
 
 def route_kernel(dest_ref, coords_ref, pack_ref, meta_ref):
@@ -242,19 +244,10 @@
     return copies
 
 
-def embed_kernel(
-    tokens, own, a, b, c, scale_ref, gain_ref, w, pack, out_ref, tokens_ref, own_ref, a_ref, b_ref, c_ref, w_ref, pack_ref, sems
-):
-    copies = load_all(
-        (tokens, own, a, b, c, w, pack), (tokens_ref, own_ref, a_ref, b_ref, c_ref, w_ref, pack_ref), sems
-    )
-    for copy in copies[:5]:
-        copy.wait()
-    total = own_ref[...] + a_ref[...].astype(F32) + b_ref[...].astype(F32) + c_ref[...].astype(F32)
+def embed_kernel(tokens_ref, own_ref, a, b, c, scale_ref, gain_ref, w_ref, pack_ref, out_ref):
+    total = own_ref[...] + a[...].astype(F32) + b[...].astype(F32) + c[...].astype(F32)
     mixed = tokens_ref[...].astype(F32) + scale_ref[...] * total
     final_rows = layer_norm(mixed, gain_ref[...]).astype(BF16)
-    for copy in copies[5:]:
-        copy.wait()
     embedded = dot(final_rows, w_ref[...]).astype(BF16)
     out_ref[...] = dot(pack_ref[...], embedded).astype(BF16)
 
@@ -405,43 +398,38 @@
 ):
     swap = functools.partial(shift, c=1)
     devices = lax.axis_size("tile") * lax.axis_size("seq")
-    own, back_1, fore_1, back_2 = encoder_mlp(cls_tokens, norm_gain, w_gate, w_up, w_down)
+    chunk, quarter = pack_weights(w_gate, w_up, w_down)
+    raw = (offsets, layer_scale, final_gain, attn_gain, norm_gain)
+    chunk, quarter, raw = lax.optimization_barrier((chunk, quarter, raw))
+    offsets, layer_scale, final_gain, attn_gain, norm_gain = raw
+    frequency = 1.0 / 10000.0 ** (jnp.arange(D // 4).astype(F32) / (D // 4))
+    frequency = jnp.tile(frequency, 4)[None]
+    offset_columns = jnp.repeat(offsets, HEAD_WIDTH)[None]
+    vectors = (frequency, offset_columns, layer_scale[None], final_gain[None], attn_gain[None], norm_gain[None])
+    cls_tokens, vectors = lax.optimization_barrier((cls_tokens, vectors))
+    frequency, offset_columns, layer_scale, final_gain, attn_gain, norm_gain = vectors
+    own, back_1, fore_1, back_2 = encoder_mlp(cls_tokens, norm_gain, chunk, quarter, w_gate, w_up, w_down)
     dest_pos, own = lax.optimization_barrier((dest_pos, own))
     terms = (own, shift(back_1, y=-1), shift(fore_1, y=1), shift(back_2, y=2))
     pack, meta = call(
         route_kernel, [((2 * ROWS, ROWS), BF16), ((ROWS, ROWS), F32)], dest_pos[None], tile_coords
     )
     meta = lax.all_to_all(meta.reshape(devices, 1, ROWS), AXES, split_axis=0, concat_axis=0, tiled=True)
-    frequency = 1.0 / 10000.0 ** (jnp.arange(D // 4).astype(F32) / (D // 4))
-    frequency = jnp.tile(frequency, 4)[None]
     (plan,) = call(plan_kernel, [((ROWS, D + 2 * ROWS), F32)], meta.reshape(ROWS, ROWS), frequency)
-    offset_columns = jnp.repeat(offsets, HEAD_WIDTH)[None]
     (payload,) = call(
         embed_kernel,
         [((2 * ROWS, D), BF16)],
         cls_tokens,
         *terms,
-        layer_scale[None],
-        final_gain[None],
+        layer_scale,
+        final_gain,
         w_embed,
         pack,
-        scratch=[
-            pltpu.VMEM((ROWS, D_VIT), BF16),
-            pltpu.VMEM((ROWS, D_VIT), F32),
-            pltpu.VMEM((ROWS, D_VIT), BF16),
-            pltpu.VMEM((ROWS, D_VIT), BF16),
-            pltpu.VMEM((ROWS, D_VIT), BF16),
-            pltpu.VMEM((D_VIT, D), BF16),
-            pltpu.VMEM((2 * ROWS, ROWS), BF16),
-            pltpu.SemaphoreType.DMA((7,)),
-        ],
-        spaces=[HBM] * 5 + [VMEM] * 2 + [HBM] * 2,
-        vmem=56,
     )
     payload, plan = lax.optimization_barrier((payload, plan))
     payload = lax.all_to_all(payload.reshape(2, devices, D), AXES, split_axis=1, concat_axis=1, tiled=True)
     payload = payload.reshape(2 * ROWS, D)
-    (normed,) = call(place_kernel, [((ROWS, D), BF16)], payload, plan, attn_gain[None])
+    (normed,) = call(place_kernel, [((ROWS, D), BF16)], payload, plan, attn_gain)
     held = [normed, shift(normed, x=1), shift(normed, x=-1), shift(normed, x=2)]
     (far_kv,) = call(far_keys_kernel, [((ROWS, 2 * D), BF16)], normed, w_qkv, offset_columns)
     far_kv = lax.all_to_all(far_kv, "tile", split_axis=0, concat_axis=0, tiled=True)
@@ -486,7 +474,7 @@
             pltpu.SemaphoreType.DMA((3,)),
         ],
         spaces=[HBM, HBM, VMEM, HBM],
-        vmem=56,
+        vmem=60,
     )
     return out
 

time: 160 us -> 143 us (0.89)
  blocking collectives: 0 us -> 39.1 us
  waiting for transfers between devices: 36.1 us -> 16.6 us
  local copies, waits for them, and re-layouts: 26.8 us -> 11.2 us
  starting transfers between devices: 56.8 us -> 41.2 us
  Pallas kernels: 38.7 us -> 33.9 us
    all_to_all x0 -> x2, blocking collectives: none -> 39.1 us  [the longest x1 19.6 us: body(): lax.all_to_all(payload.reshape(2, devices, D), AXES, split_axis=1, concat...]
    all_to_all x2 -> x0, waiting for transfers between devices: 21.6 us -> none  [the longest x1 12 us: body(): lax.all_to_all(payload.reshape(2, devices, D), AXES, split_axis=1, concat...]
    all_to_all x2 -> x0, starting transfers between devices: 15.1 us -> none  [the longest x1 7.91 us: body(): lax.all_to_all(payload.reshape(2, devices, D), AXES, split_axis=1, concat...]
    all_to_all x1, waiting for transfers between devices: 0.01 us -> 12.4 us  [along_y(): lax.all_to_all(value, 'tile', split_axis=0, concat_axis=0, axis_index_gro...]
    unnamed x76 -> x54, local copies, waits for them, and re-layouts: 22.1 us -> 9.91 us
    ppermute x19, waiting for transfers between devices: 14.5 us -> 4.18 us  [shift(): return lax.ppermute(value, AXES, pairs)]
    pallas_call x15 -> x16, Pallas kernels: 38.7 us -> 33.9 us  [call(): pl.pallas_call(kernel, out_shape=outs, in_specs=spaces or [VMEM] * len(ar...]
    reshape x1, local copies, waits for them, and re-layouts: 2.15 us -> 0.41 us  [body(): payload.reshape(2, devices, D)]
  transfers between devices with their start and end apart: 24 -> 22, of which waited for: 8 -> 6; matrix products, arithmetic and copies ran while one was open for 1% -> 1% of each run, Pallas kernels for 12% -> 15%
where the time goes in v4:
time: 143 us; the launch traced here: 142 us
  starting transfers between devices  41.2 us (29%)
  blocking collectives  39.1 us (27%)
  Pallas kernels  33.9 us (24%)
  waiting for transfers between devices  16.6 us (12%)
  local copies, waits for them, and re-layouts  11.2 us (8%)
    pallas_call x16, Pallas kernels, call(): pl.pallas_call(kernel, out_shape=outs, in_specs=spaces or [VMEM] * len(ar...  33.9 us
    ppermute x19, starting transfers between devices, shift(): return lax.ppermute(value, AXES, pairs)  27.6 us
    all_to_all x1, blocking collectives, body(): lax.all_to_all(payload.reshape(2, devices, D), AXES, split_axis=1, concat...  19.6 us
    all_to_all x1, blocking collectives, body(): lax.all_to_all(meta.reshape(devices, 1, ROWS), AXES, split_axis=0, concat...  19.4 us
    all_to_all x1, waiting for transfers between devices, along_y(): lax.all_to_all(value, 'tile', split_axis=0, concat_axis=0, axis_index_gro...  12.4 us
    unnamed x54, local copies, waits for them, and re-layouts  9.91 us
    all_to_all x1, starting transfers between devices, body(): lax.all_to_all(far_parts, 'seq', split_axis=0, concat_axis=0, tiled=True)  5 us
    all_to_all x1, starting transfers between devices, along_y(): lax.all_to_all(value, 'tile', split_axis=0, concat_axis=0, axis_index_gro...  4.31 us
  transfers between devices with their start and end apart: 22, of which 6 were waited for; matrix products, arithmetic and copies ran while one was open for 1% of the time, Pallas kernels for 15%

profile of v4, /device:TPU:1, one launch (start us, length us, event | category | flops | bytes accessed | tf_op | source)
XLA Modules:
  0.0 142.4 jit_solution(8469470564527844014)
XLA Ops:
  0.0 2.4 %shard_map.136 = (bf16[2304,256]{1,0:T(8,128)(2,1)}, bf16[576,256]{1,0:T(8,128)(2,1)}) custom-call(bf16[1536,256]{1,0:T(8,128)(2,1)} %gate_ref.3, bf16[1536,256]{1,0:T(8,128)(2,1)} %up_ref.3, bf16[256,1536]{1,0:T(8,128)(2,1)} %down_ref.3), custom_call_target="tpu_custom_call" | custom-call | flops 1024 | bytes 3833856 | tf_op jit(solution)/shard_map/pallas_call | solution.py:54
  2.5 4.5 %collective-permute-start = (bf16[576,256]{1,0:T(8,128)(2,1)}, bf16[576,256]{1,0:T(8,128)(2,1)S(1)}, u32[]{:S(2)}, u32[]{:S(2)}) collective-permute-start(bf16[576,256]{1,0:T(8,128)(2,1)} %get-tuple-element.50), channel_id=1, source_target_pairs={{0,64},{1,65},{2,66},{3,67},{4,68},{5,69},{6,70},{7,71},{8,72},{9,... | collective-permute-start | bytes 884744 | tf_op jit(solution)/shard_map/ppermute | solution.py:43
  7.9 1.5 %shard_map.137 = bf16[512,1536]{1,0:T(8,128)(2,1)} custom-call(bf16[128,1536]{1,0:T(8,128)(2,1)S(1)} %copy-done.12, f32[1,1536]{1,0:T(1,128)S(1)} %broadcast_in_dim.22.gain_ref), custom_call_target="tpu_custom_call" | custom-call | flops 1024 | bytes 1972224 | tf_op jit(solution)/shard_map/pallas_call | solution.py:54
  9.4 4.3 %all-to-all-start = ((bf16[4,128,1536]{2,1,0:T(8,128)(2,1)}), bf16[4,128,1536]{2,1,0:T(8,128)(2,1)S(1)}, u32[]{:S(2)}, u32[]{:S(2)}) async-start(bf16[4,128,1536]{2,1,0:T(8,128)(2,1)} %bitcast), calls=%async_computation | async-start | bytes 3145728 | tf_op jit(solution)/shard_map/all_to_all | solution.py:48
  14.6 2.1 %collective-permute-start.6 = (bf16[2304,256]{1,0:T(8,128)(2,1)}, bf16[2304,256]{1,0:T(8,128)(2,1)}, u32[]{:S(2)}, u32[]{:S(2)}) collective-permute-start(bf16[2304,256]{1,0:T(8,128)(2,1)} %get-tuple-element.57), channel_id=1, source_target_pairs={{0,96},{1,97},{2,98},{3,99},{4,100},{5,101},{6,102},{7,103},{8,104... | collective-permute-start | bytes 3538952 | tf_op jit(solution)/shard_map/ppermute | solution.py:43
  18.0 1.5 %collective-permute-start.2 = (bf16[576,256]{1,0:T(8,128)(2,1)S(1)}, bf16[576,256]{1,0:T(8,128)(2,1)}, u32[]{:S(2)}, u32[]{:S(2)}) collective-permute-start(bf16[576,256]{1,0:T(8,128)(2,1)S(1)} %collective-permute-done.q0), channel_id=1, source_target_pairs={{0,6},{1,7},{2,0},{3,1},{4,2},{5,3},{6,4},{7,5},{8,14},{9,15},{10,... | collective-permute-start | bytes 884744 | tf_op jit(solution)/shard_map/ppermute | solution.py:43
  19.4 1.5 %collective-permute-start.3 = (bf16[576,256]{1,0:T(8,128)(2,1)S(1)}, bf16[576,256]{1,0:T(8,128)(2,1)}, u32[]{:S(2)}, u32[]{:S(2)}) collective-permute-start(bf16[576,256]{1,0:T(8,128)(2,1)S(1)} %collective-permute-done.q0), channel_id=1, source_target_pairs={{0,4},{1,5},{2,6},{3,7},{4,0},{5,1},{6,2},{7,3},{8,12},{9,13},{10,... | collective-permute-start | bytes 884744 | tf_op jit(solution)/shard_map/ppermute | solution.py:43
  21.0 12.4 %all-to-all-done = bf16[4,128,1536]{2,1,0:T(8,128)(2,1)S(1)} async-done(((bf16[4,128,1536]{2,1,0:T(8,128)(2,1)}), bf16[4,128,1536]{2,1,0:T(8,128)(2,1)S(1)}, u32[]{:S(2)}, u32[]{:S(2)}) %all-to-all-start) | async-done | bytes 1572896 | tf_op jit(solution)/shard_map/all_to_all | solution.py:48
  34.5 1.4 shard_map.138.total_ref
  35.9 1.2 shard_map.139.a
  37.1 2.1 %collective-permute-start.4 = (bf16[2304,256]{1,0:T(8,128)(2,1)S(1)}, bf16[2304,256]{1,0:T(8,128)(2,1)S(1)}, u32[]{:S(2)}, u32[]{:S(2)}) collective-permute-start(bf16[2304,256]{1,0:T(8,128)(2,1)S(1)} %shard_map.139.a), channel_id=1, source_target_pairs={{0,1},{1,0},{2,3},{3,2},{4,5},{5,4},{6,7},{7,6},{8,9},{9,8},{10,11... | collective-permute-start | bytes 3538952 | tf_op jit(solution)/shard_map/ppermute | solution.py:43
  39.3 2.5 %collective-permute-done.5.a = bf16[2304,256]{1,0:T(8,128)(2,1)} collective-permute-done((bf16[2304,256]{1,0:T(8,128)(2,1)}, bf16[2304,256]{1,0:T(8,128)(2,1)}, u32[]{:S(2)}, u32[]{:S(2)}) %collective-permute-start.5) | collective-permute-done | bytes 1179680 | tf_op jit(solution)/shard_map/ppermute | solution.py:43
  41.8 2.2 %collective-permute-start.7 = (bf16[2304,256]{1,0:T(8,128)(2,1)}, bf16[2304,256]{1,0:T(8,128)(2,1)S(1)}, u32[]{:S(2)}, u32[]{:S(2)}) collective-permute-start(bf16[2304,256]{1,0:T(8,128)(2,1)} %collective-permute-done.5.a), channel_id=1, source_target_pairs={{0,1},{1,0},{2,3},{3,2},{4,5},{5,4},{6,7},{7,6},{8,9},{9,8},{10,11... | collective-permute-start | bytes 3538952 | tf_op jit(solution)/shard_map/ppermute | solution.py:43
  44.0 1.5 %shard_map.140.total_ref = f32[512,1536]{1,0:T(8,128)S(1)} custom-call(bf16[512,1536]{1,0:T(8,128)(2,1)S(1)} %bitcast.14, f32[512,1536]{1,0:T(8,128)S(1)} %shard_map.138.total_ref, bf16[2304,256]{1,0:T(8,128)(2,1)S(1)} %shard_map.139.a, bf16[2304,256]{1,0:T(8,128)(2,1)S(1)} %collective-permute-done.4.b), custom_call_target="tpu_custom_call" | custom-call | flops 1024 | bytes 10223616 | tf_op jit(solution)/shard_map/pallas_call | solution.py:54
  45.5 3.1 %shard_map.141.total_ref = f32[512,1536]{1,0:T(8,128)S(1)} custom-call(bf16[512,1536]{1,0:T(8,128)(2,1)S(1)} %bitcast.15, f32[512,1536]{1,0:T(8,128)S(1)} %shard_map.140.total_ref, bf16[2304,256]{1,0:T(8,128)(2,1)} %collective-permute-done.5.a, bf16[2304,256]{1,0:T(8,128)(2,1)} %collective-permute-done.6.b), custom_call_target="tpu_custom_call" | custom-call | flops 1024 | bytes 10223616 | tf_op jit(solution)/shard_map/pallas_call | solution.py:54
  48.6 1.7 %shard_map.142 = (f32[128,1536]{1,0:T(8,128)S(1)}, bf16[128,1536]{1,0:T(8,128)(2,1)S(1)}, bf16[128,1536]{1,0:T(8,128)(2,1)S(1)}, bf16[128,1536]{1,0:T(8,128)(2,1)S(1)}) custom-call(bf16[512,1536]{1,0:T(8,128)(2,1)S(1)} %bitcast.16, f32[512,1536]{1,0:T(8,128)S(1)} %shard_map.141.total_ref, bf16[2304,256]{1,0:T(8,128)(2,1)S(1)} %collective-permute-done.7.a, ...), custom_call_target="tpu_custom_call" | custom-call | flops 1024 | bytes 9043968 | tf_op jit(solution)/shard_map/pallas_call | solution.py:54
  50.4 1.4 collective-permute-start.10
  51.8 2.6 %collective-permute-start.11 = (bf16[128,1536]{1,0:T(8,128)(2,1)S(1)}, bf16[128,1536]{1,0:T(8,128)(2,1)S(1)}, u32[]{:S(2)}, u32[]{:S(2)}) collective-permute-start(bf16[128,1536]{1,0:T(8,128)(2,1)S(1)} %get-tuple-element.62), channel_id=1, source_target_pairs={{0,16},{1,17},{2,18},{3,19},{4,20},{5,21},{6,22},{7,23},{8,24},{9,... | collective-permute-start | bytes 1179656 | tf_op jit(solution)/shard_map/ppermute | solution.py:43
  55.8 19.4 %all_to_all.43 = f32[128,1,128]{2,1,0:T(1,128)S(1)} all-to-all(f32[128,1,128]{2,1,0:T(1,128)S(1)} %bitcast.23), channel_id=1, replica_groups=mesh['tile'=16,'seq'=8] {'tile','seq'}, dimensions={0} | all-to-all | bytes 131072 | tf_op jit(solution)/shard_map/all_to_all | solution.py:417
  75.2 1.5 %shard_map.145.plan_ref = f32[128,1024]{1,0:T(8,128)S(1)} custom-call(f32[128,128]{1,0:T(8,128)S(1)} %bitcast.22, f32[1,768]{1,0:T(1,128)S(1)} %broadcast_in_dim_tile.3.frequency_ref), custom_call_target="tpu_custom_call" | custom-call | flops 1024 | bytes 592896 | tf_op jit(solution)/shard_map/pallas_call | solution.py:54
  78.4 19.6 %all_to_all.44 = bf16[2,128,768]{2,0,1:T(2,128)(2,1)S(1)} all-to-all(bf16[2,128,768]{2,0,1:T(2,128)(2,1)S(1)} %copy.16), channel_id=1, replica_groups=mesh['tile'=16,'seq'=8] {'tile','seq'}, dimensions={1} | all-to-all | bytes 786432 | tf_op jit(solution)/shard_map/all_to_all | solution.py:430
  99.2 2.7 %collective-permute-start.15 = (bf16[128,768]{1,0:T(8,128)(2,1)}, bf16[128,768]{1,0:T(8,128)(2,1)}, u32[]{:S(2)}, u32[]{:S(2)}) collective-permute-start(bf16[128,768]{1,0:T(8,128)(2,1)} %shard_map.146.b0.normed_ref), channel_id=1, source_target_pairs={{0,6},{1,7},{2,0},{3,1},{4,2},{5,3},{6,4},{7,5},{8,14},{9,15},{10,... | collective-permute-start | bytes 589832 | tf_op jit(solution)/shard_map/ppermute | solution.py:43
  101.9 1.8 %shard_map.149 = bf16[128,1536]{1,0:T(8,128)(2,1)S(1)} custom-call(bf16[128,768]{1,0:T(8,128)(2,1)} %shard_map.146.b0.normed_ref, bf16[768,2304]{1,0:T(8,128)(2,1)S(1)} %copy-done, s32[1,768]{1,0:T(1,128)S(1)} %broadcast_in_dim_reshape.3.offsets_ref), custom_call_target="tpu_custom_call" | custom-call | flops 1024 | bytes 4131840 | tf_op jit(solution)/shard_map/pallas_call | solution.py:54
  104.5 4.2 %all-to-all-start.3 = ((bf16[16,8,1536]{2,1,0:T(8,128)(2,1)}), bf16[16,8,1536]{2,1,0:T(8,128)(2,1)}, u32[]{:S(2)}, u32[]{:S(2)}) async-start(bf16[16,8,1536]{2,1,0:T(8,128)(2,1)} %bitcast.19), calls=%async_computation.3 | async-start | bytes 786432 | tf_op jit(solution)/shard_map/all_to_all | solution.py:435
  108.7 1.5 %collective-permute-start.12 = (bf16[128,768]{1,0:T(8,128)(2,1)}, bf16[128,768]{1,0:T(8,128)(2,1)S(1)}, u32[]{:S(2)}, u32[]{:S(2)}) collective-permute-start(bf16[128,768]{1,0:T(8,128)(2,1)} %shard_map.146.b0.normed_ref), channel_id=1, source_target_pairs={{0,1},{1,0},{2,3},{3,2},{4,5},{5,4},{6,7},{7,6},{8,9},{9,8},{10,11... | collective-permute-start | bytes 589832 | tf_op jit(solution)/shard_map/ppermute | solution.py:43
  110.2 2.0 %collective-permute-start.14 = (bf16[128,768]{1,0:T(8,128)(2,1)}, bf16[128,768]{1,0:T(8,128)(2,1)S(1)}, u32[]{:S(2)}, u32[]{:S(2)}) collective-permute-start(bf16[128,768]{1,0:T(8,128)(2,1)} %collective-permute-done.13.b2), channel_id=1, source_target_pairs={{0,1},{1,0},{2,3},{3,2},{4,5},{5,4},{6,7},{7,6},{8,9},{9,8},{10,11... | collective-permute-start | bytes 589832 | tf_op jit(solution)/shard_map/ppermute | solution.py:43
  114.2 3.3 %shard_map.147 = (bf16[64,768]{1,0:T(8,128)(2,1)S(1)}, bf16[1024,768]{1,0:T(8,128)(2,1)S(1)}) custom-call(bf16[128,768]{1,0:T(8,128)(2,1)} %shard_map.146.b0.normed_ref, bf16[128,768]{1,0:T(8,128)(2,1)S(1)} %collective-permute-done.12.b1, bf16[128,768]{1,0:T(8,128)(2,1)} %collective-permute-done.13.b2, bf16[128,768]{1,0:T(8,128)(2,1)S(1)} %collective-permute-done.14.b3, ...), custom_call_target="tpu_custom_call" | custom-call | flops 1024 | bytes 6786048 | tf_op jit(solution)/shard_map/pallas_call | solution.py:54
  120.2 2.5 %shard_map.150 = f32[64,896]{1,0:T(8,128)S(1)} custom-call(bf16[64,768]{1,0:T(8,128)(2,1)S(1)} %copy-done.17, bf16[128,1536]{1,0:T(8,128)(2,1)} %bitcast.9.kv_ref), custom_call_target="tpu_custom_call" | custom-call | flops 1024 | bytes 720896 | tf_op jit(solution)/shard_map/pallas_call | solution.py:54
  123.5 5.0 %all-to-all-start.4 = ((f32[8,8,896]{2,1,0:T(8,128)}), f32[8,8,896]{2,1,0:T(8,128)}, u32[]{:S(2)}, u32[]{:S(2)}) async-start(f32[8,8,896]{2,1,0:T(8,128)} %bitcast.21), calls=%async_computation.4 | async-start | bytes 458752 | tf_op jit(solution)/shard_map/all_to_all | solution.py:448
  130.5 1.4 copy-done.11
  131.9 5.8 %shard_map.148.near = f32[128,2304]{1,0:T(8,128)S(1)} custom-call(bf16[1024,768]{1,0:T(8,128)(2,1)S(1)} %copy-done.11, bf16[768,2304]{1,0:T(8,128)(2,1)S(1)} %copy-done, bf16[256,768]{1,0:T(8,128)(2,1)S(1)} %bitcast.18, f32[128,1024]{1,0:T(8,128)S(1)} %copy-done.3), custom_call_target="tpu_custom_call" | custom-call | flops 1024 | bytes 7208960 | tf_op jit(solution)/shard_map/pallas_call | solution.py:54
  138.8 3.5 %shard_map.151 = bf16[128,768]{1,0:T(8,128)(2,1)} custom-call(f32[128,2304]{1,0:T(8,128)} %copy-done.1, f32[64,896]{1,0:T(8,128)} %bitcast.11.far, s32[1,768]{1,0:T(1,128)} %copy-done.18, bf16[768,768]{1,0:T(8,128)(2,1)} %w.1), custom_call_target="tpu_custom_call" | custom-call | flops 1024 | bytes 2788352 | tf_op jit(solution)/shard_map/pallas_call | solution.py:54
  (95 shorter events, 17.6 us)
Async XLA Ops:
  0.0 7.8 %copy-start.25 = (f32[768]{0:T(1024)S(1)}, f32[768]{0:T(1024)}, u32[]{:S(2)}) copy-start(f32[768]{0:T(1024)} %param.24) | copy-start | bytes 9220
  0.0 7.9 %copy-start.12 = (bf16[128,1536]{1,0:T(8,128)(2,1)S(1)}, bf16[128,1536]{1,0:T(8,128)(2,1)}, u32[]{:S(2)}) copy-start(bf16[128,1536]{1,0:T(8,128)(2,1)} %tokens_ref) | copy-start | bytes 1179652
  2.5 11.4 %collective-permute-start = (bf16[576,256]{1,0:T(8,128)(2,1)}, bf16[576,256]{1,0:T(8,128)(2,1)S(1)}, u32[]{:S(2)}, u32[]{:S(2)}) collective-permute-start(bf16[576,256]{1,0:T(8,128)(2,1)} %get-tuple-element.50), channel_id=1, source_target_pairs={{0,64},{1,65},{2,66},{3,67},{4,68},{5,69},{6,70},{7,71},{8,72},{9,... | collective-permute-start | bytes 884744 | tf_op jit(solution)/shard_map/ppermute | solution.py:43
  7.2 107.0 %copy-start.18 = (s32[1,768]{1,0:T(1,128)}, s32[1,768]{1,0:T(1,128)S(1)}, u32[]{:S(2)}) copy-start(s32[1,768]{1,0:T(1,128)S(1)} %broadcast_in_dim_reshape.3.offsets_ref) | copy-start | bytes 9220
  9.4 23.9 %copy-start.6 = (bf16[1536,256]{1,0:T(8,128)(2,1)S(1)}, bf16[1536,256]{1,0:T(8,128)(2,1)}, u32[]{:S(2)}) copy-start(bf16[1536,256]{1,0:T(8,128)(2,1)} %gate_ref.3) | copy-start | bytes 2359300
  9.4 23.9 %copy-start.7 = (bf16[1536,256]{1,0:T(8,128)(2,1)S(1)}, bf16[1536,256]{1,0:T(8,128)(2,1)}, u32[]{:S(2)}) copy-start(bf16[1536,256]{1,0:T(8,128)(2,1)} %up_ref.3) | copy-start | bytes 2359300
  9.4 23.9 %all-to-all-start = ((bf16[4,128,1536]{2,1,0:T(8,128)(2,1)}), bf16[4,128,1536]{2,1,0:T(8,128)(2,1)S(1)}, u32[]{:S(2)}, u32[]{:S(2)}) async-start(bf16[4,128,1536]{2,1,0:T(8,128)(2,1)} %bitcast), calls=%async_computation | async-start | bytes 3145728 | tf_op jit(solution)/shard_map/all_to_all | solution.py:48
  13.9 27.9 %collective-permute-start.5 = (bf16[2304,256]{1,0:T(8,128)(2,1)}, bf16[2304,256]{1,0:T(8,128)(2,1)}, u32[]{:S(2)}, u32[]{:S(2)}) collective-permute-start(bf16[2304,256]{1,0:T(8,128)(2,1)} %get-tuple-element.57), channel_id=1, source_target_pairs={{0,32},{1,33},{2,34},{3,35},{4,36},{5,37},{6,38},{7,39},{8,40},{9,... | collective-permute-start | bytes 3538952 | tf_op jit(solution)/shard_map/ppermute | solution.py:43
  14.6 29.4 %collective-permute-start.6 = (bf16[2304,256]{1,0:T(8,128)(2,1)}, bf16[2304,256]{1,0:T(8,128)(2,1)}, u32[]{:S(2)}, u32[]{:S(2)}) collective-permute-start(bf16[2304,256]{1,0:T(8,128)(2,1)} %get-tuple-element.57), channel_id=1, source_target_pairs={{0,96},{1,97},{2,98},{3,99},{4,100},{5,101},{6,102},{7,103},{8,104... | collective-permute-start | bytes 3538952 | tf_op jit(solution)/shard_map/ppermute | solution.py:43
  16.8 19.1 %collective-permute-start.1 = (bf16[576,256]{1,0:T(8,128)(2,1)S(1)}, bf16[576,256]{1,0:T(8,128)(2,1)}, u32[]{:S(2)}, u32[]{:S(2)}) collective-permute-start(bf16[576,256]{1,0:T(8,128)(2,1)S(1)} %collective-permute-done.q0), channel_id=1, source_target_pairs={{0,2},{1,3},{2,4},{3,5},{4,6},{5,7},{6,0},{7,1},{8,10},{9,11},{10,... | collective-permute-start | bytes 884744 | tf_op jit(solution)/shard_map/ppermute | solution.py:43
  18.0 17.9 %collective-permute-start.2 = (bf16[576,256]{1,0:T(8,128)(2,1)S(1)}, bf16[576,256]{1,0:T(8,128)(2,1)}, u32[]{:S(2)}, u32[]{:S(2)}) collective-permute-start(bf16[576,256]{1,0:T(8,128)(2,1)S(1)} %collective-permute-done.q0), channel_id=1, source_target_pairs={{0,6},{1,7},{2,0},{3,1},{4,2},{5,3},{6,4},{7,5},{8,14},{9,15},{10,... | collective-permute-start | bytes 884744 | tf_op jit(solution)/shard_map/ppermute | solution.py:43
  19.4 16.5 %collective-permute-start.3 = (bf16[576,256]{1,0:T(8,128)(2,1)S(1)}, bf16[576,256]{1,0:T(8,128)(2,1)}, u32[]{:S(2)}, u32[]{:S(2)}) collective-permute-start(bf16[576,256]{1,0:T(8,128)(2,1)S(1)} %collective-permute-done.q0), channel_id=1, source_target_pairs={{0,4},{1,5},{2,6},{3,7},{4,0},{5,1},{6,2},{7,3},{8,12},{9,13},{10,... | collective-permute-start | bytes 884744 | tf_op jit(solution)/shard_map/ppermute | solution.py:43
  37.1 6.9 %collective-permute-start.4 = (bf16[2304,256]{1,0:T(8,128)(2,1)S(1)}, bf16[2304,256]{1,0:T(8,128)(2,1)S(1)}, u32[]{:S(2)}, u32[]{:S(2)}) collective-permute-start(bf16[2304,256]{1,0:T(8,128)(2,1)S(1)} %shard_map.139.a), channel_id=1, source_target_pairs={{0,1},{1,0},{2,3},{3,2},{4,5},{5,4},{6,7},{7,6},{8,9},{9,8},{10,11... | collective-permute-start | bytes 3538952 | tf_op jit(solution)/shard_map/ppermute | solution.py:43
  41.8 6.8 %collective-permute-start.7 = (bf16[2304,256]{1,0:T(8,128)(2,1)}, bf16[2304,256]{1,0:T(8,128)(2,1)S(1)}, u32[]{:S(2)}, u32[]{:S(2)}) collective-permute-start(bf16[2304,256]{1,0:T(8,128)(2,1)} %collective-permute-done.5.a), channel_id=1, source_target_pairs={{0,1},{1,0},{2,3},{3,2},{4,5},{5,4},{6,7},{7,6},{8,9},{9,8},{10,11... | collective-permute-start | bytes 3538952 | tf_op jit(solution)/shard_map/ppermute | solution.py:43
  44.0 4.6 %collective-permute-start.8 = (bf16[2304,256]{1,0:T(8,128)(2,1)}, bf16[2304,256]{1,0:T(8,128)(2,1)S(1)}, u32[]{:S(2)}, u32[]{:S(2)}) collective-permute-start(bf16[2304,256]{1,0:T(8,128)(2,1)} %collective-permute-done.6.b), channel_id=1, source_target_pairs={{0,1},{1,0},{2,3},{3,2},{4,5},{5,4},{6,7},{7,6},{8,9},{9,8},{10,11... | collective-permute-start | bytes 3538952 | tf_op jit(solution)/shard_map/ppermute | solution.py:43
  48.6 28.2 %copy-start.13 = (bf16[128,1536]{1,0:T(8,128)(2,1)S(1)}, bf16[128,1536]{1,0:T(8,128)(2,1)}, u32[]{:S(2)}) copy-start(bf16[128,1536]{1,0:T(8,128)(2,1)} %tokens_ref) | copy-start | bytes 1179652
  48.6 28.2 %copy-start.19 = (f32[1,1536]{1,0:T(1,128)S(1)}, f32[1,1536]{1,0:T(1,128)}, u32[]{:S(2)}) copy-start(f32[1,1536]{1,0:T(1,128)} %broadcast_in_dim.20.gain_ref) | copy-start | bytes 18436
  48.6 28.1 %copy-start.9 = (bf16[1536,768]{1,0:T(8,128)(2,1)S(1)}, bf16[1536,768]{1,0:T(8,128)(2,1)}, u32[]{:S(2)}) copy-start(bf16[1536,768]{1,0:T(8,128)(2,1)} %w_ref.4) | copy-start | bytes 7077892
  50.4 26.3 %collective-permute-start.10 = (bf16[128,1536]{1,0:T(8,128)(2,1)S(1)}, bf16[128,1536]{1,0:T(8,128)(2,1)S(1)}, u32[]{:S(2)}, u32[]{:S(2)}) collective-permute-start(bf16[128,1536]{1,0:T(8,128)(2,1)S(1)} %get-tuple-element.61), channel_id=1, source_target_pairs={{0,8},{1,9},{2,10},{3,11},{4,12},{5,13},{6,14},{7,15},{8,16},{9,17... | collective-permute-start | bytes 1179656 | tf_op jit(solution)/shard_map/ppermute | solution.py:43
  51.8 25.0 %collective-permute-start.11 = (bf16[128,1536]{1,0:T(8,128)(2,1)S(1)}, bf16[128,1536]{1,0:T(8,128)(2,1)S(1)}, u32[]{:S(2)}, u32[]{:S(2)}) collective-permute-start(bf16[128,1536]{1,0:T(8,128)(2,1)S(1)} %get-tuple-element.62), channel_id=1, source_target_pairs={{0,16},{1,17},{2,18},{3,19},{4,20},{5,21},{6,22},{7,23},{8,24},{9,... | collective-permute-start | bytes 1179656 | tf_op jit(solution)/shard_map/ppermute | solution.py:43
  54.4 22.4 %collective-permute-start.9 = (bf16[128,1536]{1,0:T(8,128)(2,1)S(1)}, bf16[128,1536]{1,0:T(8,128)(2,1)S(1)}, u32[]{:S(2)}, u32[]{:S(2)}) collective-permute-start(bf16[128,1536]{1,0:T(8,128)(2,1)S(1)} %get-tuple-element.60), channel_id=1, source_target_pairs={{0,24},{1,25},{2,26},{3,27},{4,28},{5,29},{6,30},{7,31},{8,0},{9,1... | collective-permute-start | bytes 1179656 | tf_op jit(solution)/shard_map/ppermute | solution.py:43
  76.7 21.4 %copy-start.2 = (f32[128,1024]{1,0:T(8,128)}, f32[128,1024]{1,0:T(8,128)S(1)}, u32[]{:S(2)}) copy-start(f32[128,1024]{1,0:T(8,128)S(1)} %shard_map.145.plan_ref) | copy-start | bytes 1572868
  76.8 25.1 %copy-start = (bf16[768,2304]{1,0:T(8,128)(2,1)S(1)}, bf16[768,2304]{1,0:T(8,128)(2,1)}, u32[]{:S(2)}) copy-start(bf16[768,2304]{1,0:T(8,128)(2,1)} %w_ref.7) | copy-start | bytes 10616836
  99.2 11.0 %collective-permute-start.13 = (bf16[128,768]{1,0:T(8,128)(2,1)}, bf16[128,768]{1,0:T(8,128)(2,1)}, u32[]{:S(2)}, u32[]{:S(2)}) collective-permute-start(bf16[128,768]{1,0:T(8,128)(2,1)} %shard_map.146.b0.normed_ref), channel_id=1, source_target_pairs={{0,2},{1,3},{2,4},{3,5},{4,6},{5,7},{6,0},{7,1},{8,10},{9,11},{10,... | collective-permute-start | bytes 589832 | tf_op jit(solution)/shard_map/ppermute | solution.py:43
  99.2 13.1 %collective-permute-start.15 = (bf16[128,768]{1,0:T(8,128)(2,1)}, bf16[128,768]{1,0:T(8,128)(2,1)}, u32[]{:S(2)}, u32[]{:S(2)}) collective-permute-start(bf16[128,768]{1,0:T(8,128)(2,1)} %shard_map.146.b0.normed_ref), channel_id=1, source_target_pairs={{0,6},{1,7},{2,0},{3,1},{4,2},{5,3},{6,4},{7,5},{8,14},{9,15},{10,... | collective-permute-start | bytes 589832 | tf_op jit(solution)/shard_map/ppermute | solution.py:43
  101.9 10.4 %collective-permute-start.17 = (bf16[128,768]{1,0:T(8,128)(2,1)}, bf16[128,768]{1,0:T(8,128)(2,1)}, u32[]{:S(2)}, u32[]{:S(2)}) collective-permute-start(bf16[128,768]{1,0:T(8,128)(2,1)} %shard_map.146.b0.normed_ref), channel_id=1, source_target_pairs={{0,4},{1,5},{2,6},{3,7},{4,0},{5,1},{6,2},{7,3},{8,12},{9,13},{10,... | collective-permute-start | bytes 589832 | tf_op jit(solution)/shard_map/ppermute | solution.py:43
  104.5 14.8 %all-to-all-start.3 = ((bf16[16,8,1536]{2,1,0:T(8,128)(2,1)}), bf16[16,8,1536]{2,1,0:T(8,128)(2,1)}, u32[]{:S(2)}, u32[]{:S(2)}) async-start(bf16[16,8,1536]{2,1,0:T(8,128)(2,1)} %bitcast.19), calls=%async_computation.3 | async-start | bytes 786432 | tf_op jit(solution)/shard_map/all_to_all | solution.py:435
  108.7 4.1 %collective-permute-start.12 = (bf16[128,768]{1,0:T(8,128)(2,1)}, bf16[128,768]{1,0:T(8,128)(2,1)S(1)}, u32[]{:S(2)}, u32[]{:S(2)}) collective-permute-start(bf16[128,768]{1,0:T(8,128)(2,1)} %shard_map.146.b0.normed_ref), channel_id=1, source_target_pairs={{0,1},{1,0},{2,3},{3,2},{4,5},{5,4},{6,7},{7,6},{8,9},{9,8},{10,11... | collective-permute-start | bytes 589832 | tf_op jit(solution)/shard_map/ppermute | solution.py:43
  110.2 3.3 %collective-permute-start.14 = (bf16[128,768]{1,0:T(8,128)(2,1)}, bf16[128,768]{1,0:T(8,128)(2,1)S(1)}, u32[]{:S(2)}, u32[]{:S(2)}) collective-permute-start(bf16[128,768]{1,0:T(8,128)(2,1)} %collective-permute-done.13.b2), channel_id=1, source_target_pairs={{0,1},{1,0},{2,3},{3,2},{4,5},{5,4},{6,7},{7,6},{8,9},{9,8},{10,11... | collective-permute-start | bytes 589832 | tf_op jit(solution)/shard_map/ppermute | solution.py:43
  112.3 1.7 %collective-permute-start.16 = (bf16[128,768]{1,0:T(8,128)(2,1)}, bf16[128,768]{1,0:T(8,128)(2,1)S(1)}, u32[]{:S(2)}, u32[]{:S(2)}) collective-permute-start(bf16[128,768]{1,0:T(8,128)(2,1)} %collective-permute-done.15.b4), channel_id=1, source_target_pairs={{0,1},{1,0},{2,3},{3,2},{4,5},{5,4},{6,7},{7,6},{8,9},{9,8},{10,11... | collective-permute-start | bytes 589832 | tf_op jit(solution)/shard_map/ppermute | solution.py:43
  112.3 1.9 %collective-permute-start.18 = (bf16[128,768]{1,0:T(8,128)(2,1)}, bf16[128,768]{1,0:T(8,128)(2,1)S(1)}, u32[]{:S(2)}, u32[]{:S(2)}) collective-permute-start(bf16[128,768]{1,0:T(8,128)(2,1)} %collective-permute-done.17.b6), channel_id=1, source_target_pairs={{0,1},{1,0},{2,3},{3,2},{4,5},{5,4},{6,7},{7,6},{8,9},{9,8},{10,11... | collective-permute-start | bytes 589832 | tf_op jit(solution)/shard_map/ppermute | solution.py:43
  123.5 15.3 %all-to-all-start.4 = ((f32[8,8,896]{2,1,0:T(8,128)}), f32[8,8,896]{2,1,0:T(8,128)}, u32[]{:S(2)}, u32[]{:S(2)}) async-start(f32[8,8,896]{2,1,0:T(8,128)} %bitcast.21), calls=%async_computation.4 | async-start | bytes 458752 | tf_op jit(solution)/shard_map/all_to_all | solution.py:448
  (17 other events, 53.8 us)

commit v5 on v4

--- a/solution.py
+++ b/solution.py
@@ -48,14 +48,14 @@
     return lax.all_to_all(value, "tile", split_axis=0, concat_axis=0, axis_index_groups=groups, tiled=True)
 
 
-def call(kernel, outs, *args, scratch=(), vmem=12, spaces=None, cost=1):
+def call(kernel, outs, *args, scratch=(), vmem=12, spaces=None, out_spaces=None, cost=1):
     outs = [jax.ShapeDtypeStruct(shape, dtype) for shape, dtype in outs]
     nbytes = cost * sum(a.size * a.dtype.itemsize for a in (*args, *outs))
     return pl.pallas_call(
         kernel,
         out_shape=outs,
         in_specs=spaces or [VMEM] * len(args),
-        out_specs=tuple(VMEM for _ in outs),
+        out_specs=tuple(out_spaces or [VMEM] * len(outs)),
         scratch_shapes=scratch,
         compiler_params=pltpu.CompilerParams(vmem_limit_bytes=vmem * MIB),
         cost_estimate=pl.CostEstimate(flops=1024, bytes_accessed=nbytes, transcendentals=0),
@@ -96,7 +96,7 @@
 
 def join_kernel(q0, q1, q2, q3, out_ref):
     x = lax.div(lax.axis_index("seq"), CORES)
-    for dx, q in ((0, q0), (1, q1), (3, q2), (2, q3)):
+    for dx, q in ((0, q0), (2, q1), (1, q2), (3, q3)):
         place = lax.rem(x - dx + RING, RING)
         out_ref[pl.ds(pl.multiple_of(place * QUARTER, QUARTER), QUARTER), :] = q[...]
 
@@ -165,7 +165,7 @@
     rows = along_y(normed)
     chunk, quarter, _ = lax.optimization_barrier((chunk, quarter, normed))
     before, after = shift(chunk, z=1), shift(chunk, z=-1)
-    quarters = [quarter, shift(quarter, x=1), shift(quarter, x=-1), shift(quarter, x=2)]
+    quarters = [quarter, shift(quarter, x=2), shift(quarter, x=1), shift(quarter, x=-1)]
     (total,) = call(
         mlp_own_kernel,
         [((RING * ROWS, D_VIT), F32)],
@@ -203,38 +203,35 @@
     )
 
 
-def route_kernel(dest_ref, coords_ref, pack_ref, meta_ref):
+def route_kernel(dest_ref, coords_ref, pack_ref, fields_ref):
     dest = jnp.broadcast_to(dest_ref[...], (ROWS, ROWS))
     target = lax.shift_right_logical(dest, 7).astype(F32)
     here = lax.broadcasted_iota(I32, (ROWS, ROWS), 1)
     peer = lax.broadcasted_iota(I32, (ROWS, ROWS), 0)
     earlier = jnp.where((target == target.T) & (peer < here), 1.0, 0.0)
     slot = jnp.sum(earlier, axis=0, keepdims=True)
-    fields = (dest_ref[...] & 127, coords_ref[0:1, :], coords_ref[1:2, :])
-    meta = jnp.full((ROWS, ROWS), -1.0, F32)
     for s in range(2):
         taken = (target == peer.astype(F32)) & (slot == float(s))
         pack_ref[ROWS * s : ROWS * (s + 1), :] = jnp.where(taken, 1.0, 0.0).astype(BF16)
-        for k, field in enumerate(fields):
-            column = jnp.sum(jnp.where(taken, field.astype(F32) + 1.0, 0.0), axis=1, keepdims=True) - 1.0
-            meta = jnp.where(here == 3 * s + k, column, meta)
-    meta_ref[...] = meta
-
-
-def plan_kernel(meta_ref, frequency_ref, out_ref):
-    fields = meta_ref[...].T
-    row = lax.broadcasted_iota(I32, (ROWS, ROWS), 0)
-    coords = [0.0, 0.0]
-    for s in range(2):
-        taken = row.astype(F32) == fields[3 * s : 3 * s + 1, :]
-        out_ref[:, D + ROWS * s : D + ROWS * (s + 1)] = jnp.where(taken, 1.0, 0.0)
-        for k in range(2):
-            value = fields[3 * s + 1 + k : 3 * s + 2 + k, :]
-            coords[k] = coords[k] + jnp.sum(jnp.where(taken, value, 0.0), axis=1, keepdims=True)
+    fields = [(dest_ref[...] & 127) + 1]
+    for k in range(2):
+        fields += [lax.shift_right_logical(coords_ref[k : k + 1, :], 5), coords_ref[k : k + 1, :] & 31]
+    table = jnp.zeros((ROWS, ROWS), F32)
+    for k, field in enumerate(fields):
+        table = jnp.where(peer == k, field.astype(F32), table)
+    fields_ref[...] = table.T.astype(BF16)
+
+
+def slide_rows(payload_ref, frequency_ref):
+    sent = payload_ref[:, D:]
+    row = lax.broadcasted_iota(I32, (ROWS, 2 * ROWS), 0) + 1
+    place = jnp.where(row.astype(F32) == sent.astype(F32).T[0:1, :], 1.0, 0.0).astype(BF16)
+    fields = dot(place, sent)
+    along = [32.0 * fields[:, 1 + 2 * k : 2 + 2 * k] + fields[:, 2 + 2 * k : 3 + 2 * k] for k in range(2)]
     lane = lax.broadcasted_iota(I32, (ROWS, D), 1)
-    angle = jnp.where(lane < D // 2, coords[0], coords[1]) * frequency_ref[...]
     sine = (lane < D // 4) | ((lane >= D // 2) & (lane < 3 * D // 4))
-    out_ref[:, :D] = jnp.where(sine, jnp.sin(angle), jnp.cos(angle))
+    angle = jnp.where(lane < D // 2, along[0], along[1]) * frequency_ref[...]
+    return dot(place, payload_ref[:, :D]) + jnp.sin(angle + jnp.where(sine, 0.0, jnp.pi / 2))
 
 
 def load_all(sources, targets, sems):
@@ -244,12 +241,13 @@
     return copies
 
 
-def embed_kernel(tokens_ref, own_ref, a, b, c, scale_ref, gain_ref, w_ref, pack_ref, out_ref):
+def embed_kernel(tokens_ref, own_ref, a, b, c, scale_ref, gain_ref, w_ref, pack_ref, fields_ref, out_ref):
     total = own_ref[...] + a[...].astype(F32) + b[...].astype(F32) + c[...].astype(F32)
     mixed = tokens_ref[...].astype(F32) + scale_ref[...] * total
     final_rows = layer_norm(mixed, gain_ref[...]).astype(BF16)
     embedded = dot(final_rows, w_ref[...]).astype(BF16)
-    out_ref[...] = dot(pack_ref[...], embedded).astype(BF16)
+    out_ref[:, :D] = dot(pack_ref[...], embedded).astype(BF16)
+    out_ref[:, D:] = dot(pack_ref[...], fields_ref[...]).astype(BF16)
 
 
 def kept_columns(rows, offsets_ref):
@@ -263,12 +261,9 @@
     return jnp.where(lax.shift_right_logical(row, 4) == group, 1.0, 0.0).astype(BF16)
 
 
-def slide_rows(payload_ref, plan_ref):
-    return dot(plan_ref[:, D:].astype(BF16), payload_ref[...]) + plan_ref[:, :D]
-
-
-def place_kernel(payload_ref, plan_ref, gain_ref, normed_ref):
-    seq_in = slide_rows(payload_ref, plan_ref)
+def place_kernel(payload_ref, frequency_ref, gain_ref, normed_ref, seq_ref):
+    seq_in = slide_rows(payload_ref, frequency_ref)
+    seq_ref[...] = seq_in
     normed_ref[...] = layer_norm(seq_in, gain_ref[...]).astype(BF16)
 
 
@@ -329,8 +324,7 @@
             out_ref[where, 128 * j : 128 * (j + 1)] = block[KEPT * n : KEPT * (n + 1), :]
 
 
-def near_kernel(rows_ref, w_ref, payload_ref, plan_ref, out_ref, q_ref, k_ref, v_ref):
-    out_ref[:, 2 * D :] = slide_rows(payload_ref, plan_ref)
+def near_kernel(rows_ref, w_ref, out_ref, q_ref, k_ref, v_ref):
     q_ref[...] = (dot(rows_ref[:ROWS, :], w_ref[:, :D]) * (HEAD_WIDTH ** -0.5)).astype(BF16)
     for n in range(2):
         part = slice(512 * n, 512 * (n + 1))
@@ -340,8 +334,8 @@
     for j in range(PAIRS):
         cols = slice(PAIR * j, PAIR * (j + 1))
         mixed, even, odd = attend_pair(q_ref[:, cols], k_ref[:, cols], v_ref[:, cols])
-        out_ref[:, cols] = mixed
-        out_ref[:, D + PAIR * j : D + PAIR * (j + 1)] = jnp.where(lane < HEAD_WIDTH, even, odd)
+        out_ref[j, :, :PAIR] = mixed
+        out_ref[j, :, PAIR:] = jnp.where(lane < HEAD_WIDTH, even, odd)
 
 
 def spread(rows):
@@ -349,8 +343,8 @@
     return jnp.broadcast_to(rows[:, None, :], (n, SEGMENT_SPACING, width)).reshape(n * SEGMENT_SPACING, width)
 
 
-def final_kernel(near, far, offsets_ref, w, out_ref, near_ref, far_ref, w_ref, sems):
-    copies = load_all((far, near, w), (far_ref, near_ref, w_ref), sems)
+def final_kernel(near, far, seq, offsets_ref, w, out_ref, near_ref, far_ref, seq_ref, w_ref, sems):
+    copies = load_all((far, near, seq, w), (far_ref, near_ref, seq_ref, w_ref), sems)
     copies[0].wait()
     copies[1].wait()
     parts = [slice(KEPT * n, KEPT * (n + 1)) for n in range(SEGMENT_DEVICES)]
@@ -371,13 +365,14 @@
         far = functools.reduce(jnp.add, [over_lanes(s, j) * far_ref[part, cols] for s, part in zip(shares, parts)])
         far = spread(far / over_lanes(totals, j))
         kept = place == offsets_ref[:, cols]
-        share = jnp.where(kept, 1.0 / (1.0 + jnp.exp(near_ref[:, D + PAIR * j : D + PAIR * (j + 1)] - spread(over_lanes(far_lse, j)))), 0.0)
-        combined.append(((1.0 - share) * near_ref[:, cols] + share * far).astype(BF16))
+        share = jnp.where(kept, 1.0 / (1.0 + jnp.exp(near_ref[j, :, PAIR:] - spread(over_lanes(far_lse, j)))), 0.0)
+        combined.append(((1.0 - share) * near_ref[j, :, :PAIR] + share * far).astype(BF16))
     copies[2].wait()
-    out_ref[...] = (near_ref[:, 2 * D :] + dot(jnp.concatenate(combined, axis=1), w_ref[...])).astype(BF16)
-
-
-BLOCKS = ((0, 0), (0, 1), (1, 0), (1, 1), (-1, 0), (-1, 1), (2, 0), (2, 1))
+    copies[3].wait()
+    out_ref[...] = (seq_ref[...] + dot(jnp.concatenate(combined, axis=1), w_ref[...])).astype(BF16)
+
+
+BLOCKS = ((0, 0), (0, 1), (2, 0), (2, 1), (1, 0), (1, 1), (-1, 0), (-1, 1))
 
 
 def body(
@@ -410,27 +405,29 @@
     frequency, offset_columns, layer_scale, final_gain, attn_gain, norm_gain = vectors
     own, back_1, fore_1, back_2 = encoder_mlp(cls_tokens, norm_gain, chunk, quarter, w_gate, w_up, w_down)
     dest_pos, own = lax.optimization_barrier((dest_pos, own))
-    terms = (own, shift(back_1, y=-1), shift(fore_1, y=1), shift(back_2, y=2))
-    pack, meta = call(
-        route_kernel, [((2 * ROWS, ROWS), BF16), ((ROWS, ROWS), F32)], dest_pos[None], tile_coords
-    )
-    meta = lax.all_to_all(meta.reshape(devices, 1, ROWS), AXES, split_axis=0, concat_axis=0, tiled=True)
-    (plan,) = call(plan_kernel, [((ROWS, D + 2 * ROWS), F32)], meta.reshape(ROWS, ROWS), frequency)
+    terms = (own, shift(back_1, y=-1), shift(back_2, y=2), shift(fore_1, y=1))
+    pack, fields = call(route_kernel, [((2 * ROWS, ROWS), BF16), ((ROWS, ROWS), BF16)], dest_pos[None], tile_coords)
     (payload,) = call(
         embed_kernel,
-        [((2 * ROWS, D), BF16)],
+        [((2 * ROWS, D + ROWS), BF16)],
         cls_tokens,
         *terms,
         layer_scale,
         final_gain,
         w_embed,
         pack,
-    )
-    payload, plan = lax.optimization_barrier((payload, plan))
-    payload = lax.all_to_all(payload.reshape(2, devices, D), AXES, split_axis=1, concat_axis=1, tiled=True)
-    payload = payload.reshape(2 * ROWS, D)
-    (normed,) = call(place_kernel, [((ROWS, D), BF16)], payload, plan, attn_gain)
-    held = [normed, shift(normed, x=1), shift(normed, x=-1), shift(normed, x=2)]
+        fields,
+    )
+    payload = payload.reshape(2, devices, D + ROWS)
+    payload = lax.all_to_all(payload, AXES, split_axis=1, concat_axis=1, tiled=True)
+    normed, seq_in = call(
+        place_kernel,
+        [((ROWS, D), BF16), ((ROWS, D), F32)],
+        payload.reshape(2 * ROWS, D + ROWS),
+        frequency,
+        attn_gain,
+    )
+    held = [normed, shift(normed, x=2), shift(normed, x=1), shift(normed, x=-1)]
     (far_kv,) = call(far_keys_kernel, [((ROWS, 2 * D), BF16)], normed, w_qkv, offset_columns)
     far_kv = lax.all_to_all(far_kv, "tile", split_axis=0, concat_axis=0, tiled=True)
     blocks = []
@@ -448,11 +445,9 @@
     far_parts = lax.all_to_all(far_parts, "seq", split_axis=0, concat_axis=0, tiled=True)
     (near,) = call(
         near_kernel,
-        [((ROWS, 3 * D), F32)],
+        [((PAIRS, ROWS, 2 * PAIR), F32)],
         rows,
         w_qkv,
-        payload,
-        plan,
         scratch=[
             pltpu.VMEM((ROWS, D), BF16),
             pltpu.VMEM((segment, D), BF16),
@@ -465,15 +460,17 @@
         [((ROWS, D), BF16)],
         near,
         far_parts,
+        seq_in,
         offset_columns,
         w_out,
         scratch=[
-            pltpu.VMEM((ROWS, 3 * D), F32),
+            pltpu.VMEM((PAIRS, ROWS, 2 * PAIR), F32),
             pltpu.VMEM((SEGMENT_DEVICES * KEPT, D + 128), F32),
+            pltpu.VMEM((ROWS, D), F32),
             pltpu.VMEM((D, D), BF16),
-            pltpu.SemaphoreType.DMA((3,)),
+            pltpu.SemaphoreType.DMA((4,)),
         ],
-        spaces=[HBM, HBM, VMEM, HBM],
+        spaces=[HBM, HBM, HBM, VMEM, HBM],
         vmem=60,
     )
     return out

time: 143 us -> 141 us (0.986)
  blocking collectives: 39.1 us -> 22 us
  waiting for transfers between devices: 16.6 us -> 31.4 us
    all_to_all x2 -> x1, blocking collectives: 39.1 us -> 22 us  [body(): lax.all_to_all(payload, AXES, split_axis=1, concat_axis=1, tiled=True)]
    ppermute x19, waiting for transfers between devices: 4.18 us -> 20 us  [shift(): return lax.ppermute(value, AXES, pairs)]
    unnamed x54 -> x50, local copies, waits for them, and re-layouts: 9.91 us -> 8.38 us
    pallas_call x16 -> x15, Pallas kernels: 33.9 us -> 33.6 us  [call(): pl.pallas_call(kernel, out_shape=outs, in_specs=spaces or [VMEM] * len(ar...]
  transfers between devices with their start and end apart: 22 -> 22, of which waited for: 6 -> 8; matrix products, arithmetic and copies ran while one was open for 1% -> 1% of each run, Pallas kernels for 15% -> 14%
where the time goes in v5:
time: 141 us; the launch traced here: 140 us
  starting transfers between devices  42.3 us (30%)
  Pallas kernels  33.6 us (24%)
  waiting for transfers between devices  31.4 us (22%)
  blocking collectives  22 us (16%)
  local copies, waits for them, and re-layouts  10.3 us (7%)
    pallas_call x15, Pallas kernels, call(): pl.pallas_call(kernel, out_shape=outs, in_specs=spaces or [VMEM] * len(ar...  33.6 us
    ppermute x19, starting transfers between devices, shift(): return lax.ppermute(value, AXES, pairs)  28.4 us
    all_to_all x1, blocking collectives, body(): lax.all_to_all(payload, AXES, split_axis=1, concat_axis=1, tiled=True)  22 us
    ppermute x19, waiting for transfers between devices, shift(): return lax.ppermute(value, AXES, pairs)  20 us
    all_to_all x1, waiting for transfers between devices, along_y(): lax.all_to_all(value, 'tile', split_axis=0, concat_axis=0, axis_index_gro...  11.4 us
    unnamed x50, local copies, waits for them, and re-layouts  8.38 us
    all_to_all x1, starting transfers between devices, body(): lax.all_to_all(far_parts, 'seq', split_axis=0, concat_axis=0, tiled=True)  5.39 us
    all_to_all x1, starting transfers between devices, along_y(): lax.all_to_all(value, 'tile', split_axis=0, concat_axis=0, axis_index_gro...  4.31 us
  transfers between devices with their start and end apart: 22, of which 8 were waited for; matrix products, arithmetic and copies ran while one was open for 1% of the time, Pallas kernels for 14%

profile of v5, /device:TPU:1, one launch (start us, length us, event | category | flops | bytes accessed | tf_op | source)
XLA Modules:
  0.0 140.2 jit_solution(6157228368968152404)
XLA Ops:
  0.0 2.4 %shard_map.136 = (bf16[2304,256]{1,0:T(8,128)(2,1)}, bf16[576,256]{1,0:T(8,128)(2,1)}) custom-call(bf16[1536,256]{1,0:T(8,128)(2,1)} %gate_ref.3, bf16[1536,256]{1,0:T(8,128)(2,1)} %up_ref.3, bf16[256,1536]{1,0:T(8,128)(2,1)} %down_ref.3), custom_call_target="tpu_custom_call" | custom-call | flops 1024 | bytes 3833856 | tf_op jit(solution)/shard_map/pallas_call | solution.py:54
  2.5 4.5 %collective-permute-start = (bf16[576,256]{1,0:T(8,128)(2,1)}, bf16[576,256]{1,0:T(8,128)(2,1)S(1)}, u32[]{:S(2)}, u32[]{:S(2)}) collective-permute-start(bf16[576,256]{1,0:T(8,128)(2,1)} %get-tuple-element.50), channel_id=1, source_target_pairs={{0,64},{1,65},{2,66},{3,67},{4,68},{5,69},{6,70},{7,71},{8,72},{9,... | collective-permute-start | bytes 884744 | tf_op jit(solution)/shard_map/ppermute | solution.py:43
  8.5 1.5 %shard_map.137 = bf16[512,1536]{1,0:T(8,128)(2,1)} custom-call(bf16[128,1536]{1,0:T(8,128)(2,1)S(1)} %copy-done.6, f32[1,1536]{1,0:T(1,128)S(1)} %broadcast_in_dim.22.gain_ref), custom_call_target="tpu_custom_call" | custom-call | flops 1024 | bytes 1972224 | tf_op jit(solution)/shard_map/pallas_call | solution.py:54
  10.0 4.3 %all-to-all-start = ((bf16[4,128,1536]{2,1,0:T(8,128)(2,1)}), bf16[4,128,1536]{2,1,0:T(8,128)(2,1)S(1)}, u32[]{:S(2)}, u32[]{:S(2)}) async-start(bf16[4,128,1536]{2,1,0:T(8,128)(2,1)} %bitcast), calls=%async_computation | async-start | bytes 3145728 | tf_op jit(solution)/shard_map/all_to_all | solution.py:48
  15.1 1.9 %collective-permute-start.6 = (bf16[2304,256]{1,0:T(8,128)(2,1)}, bf16[2304,256]{1,0:T(8,128)(2,1)}, u32[]{:S(2)}, u32[]{:S(2)}) collective-permute-start(bf16[2304,256]{1,0:T(8,128)(2,1)} %get-tuple-element.57), channel_id=1, source_target_pairs={{0,96},{1,97},{2,98},{3,99},{4,100},{5,101},{6,102},{7,103},{8,104... | collective-permute-start | bytes 3538952 | tf_op jit(solution)/shard_map/ppermute | solution.py:43
  17.0 2.7 %collective-permute-start.1 = (bf16[576,256]{1,0:T(8,128)(2,1)S(1)}, bf16[576,256]{1,0:T(8,128)(2,1)}, u32[]{:S(2)}, u32[]{:S(2)}) collective-permute-start(bf16[576,256]{1,0:T(8,128)(2,1)S(1)} %collective-permute-done.q0), channel_id=1, source_target_pairs={{0,4},{1,5},{2,6},{3,7},{4,0},{5,1},{6,2},{7,3},{8,12},{9,13},{10,... | collective-permute-start | bytes 884744 | tf_op jit(solution)/shard_map/ppermute | solution.py:43
  20.1 2.4 %collective-permute-start.3 = (bf16[576,256]{1,0:T(8,128)(2,1)S(1)}, bf16[576,256]{1,0:T(8,128)(2,1)}, u32[]{:S(2)}, u32[]{:S(2)}) collective-permute-start(bf16[576,256]{1,0:T(8,128)(2,1)S(1)} %collective-permute-done.q0), channel_id=1, source_target_pairs={{0,6},{1,7},{2,0},{3,1},{4,2},{5,3},{6,4},{7,5},{8,14},{9,15},{10,... | collective-permute-start | bytes 884744 | tf_op jit(solution)/shard_map/ppermute | solution.py:43
  22.4 11.4 %all-to-all-done = bf16[4,128,1536]{2,1,0:T(8,128)(2,1)S(1)} async-done(((bf16[4,128,1536]{2,1,0:T(8,128)(2,1)}), bf16[4,128,1536]{2,1,0:T(8,128)(2,1)S(1)}, u32[]{:S(2)}, u32[]{:S(2)}) %all-to-all-start) | async-done | bytes 1572896 | tf_op jit(solution)/shard_map/all_to_all | solution.py:48
  35.0 1.4 shard_map.138.total_ref
  36.4 1.2 shard_map.139.a
  37.6 2.2 %collective-permute-start.4 = (bf16[2304,256]{1,0:T(8,128)(2,1)S(1)}, bf16[2304,256]{1,0:T(8,128)(2,1)S(1)}, u32[]{:S(2)}, u32[]{:S(2)}) collective-permute-start(bf16[2304,256]{1,0:T(8,128)(2,1)S(1)} %shard_map.139.a), channel_id=1, source_target_pairs={{0,1},{1,0},{2,3},{3,2},{4,5},{5,4},{6,7},{7,6},{8,9},{9,8},{10,11... | collective-permute-start | bytes 3538952 | tf_op jit(solution)/shard_map/ppermute | solution.py:43
  39.9 2.2 %collective-permute-done.5.a = bf16[2304,256]{1,0:T(8,128)(2,1)} collective-permute-done((bf16[2304,256]{1,0:T(8,128)(2,1)}, bf16[2304,256]{1,0:T(8,128)(2,1)}, u32[]{:S(2)}, u32[]{:S(2)}) %collective-permute-start.5) | collective-permute-done | bytes 1179680 | tf_op jit(solution)/shard_map/ppermute | solution.py:43
  42.1 2.2 %collective-permute-start.7 = (bf16[2304,256]{1,0:T(8,128)(2,1)}, bf16[2304,256]{1,0:T(8,128)(2,1)S(1)}, u32[]{:S(2)}, u32[]{:S(2)}) collective-permute-start(bf16[2304,256]{1,0:T(8,128)(2,1)} %collective-permute-done.5.a), channel_id=1, source_target_pairs={{0,1},{1,0},{2,3},{3,2},{4,5},{5,4},{6,7},{7,6},{8,9},{9,8},{10,11... | collective-permute-start | bytes 3538952 | tf_op jit(solution)/shard_map/ppermute | solution.py:43
  44.2 1.5 %shard_map.140.total_ref = f32[512,1536]{1,0:T(8,128)S(1)} custom-call(bf16[512,1536]{1,0:T(8,128)(2,1)S(1)} %bitcast.10, f32[512,1536]{1,0:T(8,128)S(1)} %shard_map.138.total_ref, bf16[2304,256]{1,0:T(8,128)(2,1)S(1)} %shard_map.139.a, bf16[2304,256]{1,0:T(8,128)(2,1)S(1)} %collective-permute-done.4.b), custom_call_target="tpu_custom_call" | custom-call | flops 1024 | bytes 10223616 | tf_op jit(solution)/shard_map/pallas_call | solution.py:54
  45.7 3.1 %shard_map.141.total_ref = f32[512,1536]{1,0:T(8,128)S(1)} custom-call(bf16[512,1536]{1,0:T(8,128)(2,1)S(1)} %bitcast.11, f32[512,1536]{1,0:T(8,128)S(1)} %shard_map.140.total_ref, bf16[2304,256]{1,0:T(8,128)(2,1)} %collective-permute-done.5.a, bf16[2304,256]{1,0:T(8,128)(2,1)} %collective-permute-done.6.b), custom_call_target="tpu_custom_call" | custom-call | flops 1024 | bytes 10223616 | tf_op jit(solution)/shard_map/pallas_call | solution.py:54
  48.9 1.8 %shard_map.142 = (f32[128,1536]{1,0:T(8,128)S(1)}, bf16[128,1536]{1,0:T(8,128)(2,1)S(1)}, bf16[128,1536]{1,0:T(8,128)(2,1)S(1)}, bf16[128,1536]{1,0:T(8,128)(2,1)S(1)}) custom-call(bf16[512,1536]{1,0:T(8,128)(2,1)S(1)} %bitcast.12, f32[512,1536]{1,0:T(8,128)S(1)} %shard_map.141.total_ref, bf16[2304,256]{1,0:T(8,128)(2,1)S(1)} %collective-permute-done.7.a, ...), custom_call_target="tpu_custom_call" | custom-call | flops 1024 | bytes 9043968 | tf_op jit(solution)/shard_map/pallas_call | solution.py:54
  50.7 3.0 %collective-permute-start.10 = (bf16[128,1536]{1,0:T(8,128)(2,1)S(1)}, bf16[128,1536]{1,0:T(8,128)(2,1)S(1)}, u32[]{:S(2)}, u32[]{:S(2)}) collective-permute-start(bf16[128,1536]{1,0:T(8,128)(2,1)S(1)} %get-tuple-element.61), channel_id=1, source_target_pairs={{0,16},{1,17},{2,18},{3,19},{4,20},{5,21},{6,22},{7,23},{8,24},{9,... | collective-permute-start | bytes 1179656 | tf_op jit(solution)/shard_map/ppermute | solution.py:43
  54.0 2.4 %collective-permute-start.9 = (bf16[128,1536]{1,0:T(8,128)(2,1)S(1)}, bf16[128,1536]{1,0:T(8,128)(2,1)S(1)}, u32[]{:S(2)}, u32[]{:S(2)}) collective-permute-start(bf16[128,1536]{1,0:T(8,128)(2,1)S(1)} %get-tuple-element.60), channel_id=1, source_target_pairs={{0,24},{1,25},{2,26},{3,27},{4,28},{5,29},{6,30},{7,31},{8,0},{9,1... | collective-permute-start | bytes 1179656 | tf_op jit(solution)/shard_map/ppermute | solution.py:43
  56.5 6.0 %collective-permute-done.10.b = bf16[128,1536]{1,0:T(8,128)(2,1)S(1)} collective-permute-done((bf16[128,1536]{1,0:T(8,128)(2,1)S(1)}, bf16[128,1536]{1,0:T(8,128)(2,1)S(1)}, u32[]{:S(2)}, u32[]{:S(2)}) %collective-permute-start.10) | collective-permute-done | bytes 393248 | tf_op jit(solution)/shard_map/ppermute | solution.py:43
  62.5 9.2 %collective-permute-done.11.c = bf16[128,1536]{1,0:T(8,128)(2,1)S(1)} collective-permute-done((bf16[128,1536]{1,0:T(8,128)(2,1)S(1)}, bf16[128,1536]{1,0:T(8,128)(2,1)S(1)}, u32[]{:S(2)}, u32[]{:S(2)}) %collective-permute-start.11) | collective-permute-done | bytes 393248 | tf_op jit(solution)/shard_map/ppermute | solution.py:43
  73.5 22.0 %all_to_all.38 = bf16[2,128,896]{2,0,1:T(2,128)(2,1)S(1)} all-to-all(bf16[2,128,896]{2,0,1:T(2,128)(2,1)S(1)} %copy.15), channel_id=1, replica_groups=mesh['tile'=16,'seq'=8] {'tile','seq'}, dimensions={1} | all-to-all | bytes 917504 | tf_op jit(solution)/shard_map/all_to_all | solution.py:422
  95.5 2.5 %shard_map.145 = (bf16[128,768]{1,0:T(8,128)(2,1)}, f32[128,768]{1,0:T(8,128)S(1)}) custom-call(bf16[256,896]{1,0:T(8,128)(2,1)S(1)} %bitcast.14, f32[1,768]{1,0:T(1,128)S(1)} %copy-done.17, f32[1,768]{1,0:T(1,128)S(1)} %broadcast_in_dim.21.gain_ref), custom_call_target="tpu_custom_call" | custom-call | flops 1024 | bytes 1054720 | tf_op jit(solution)/shard_map/pallas_call | solution.py:54
  100.4 2.2 %collective-permute-start.17 = (bf16[128,768]{1,0:T(8,128)(2,1)}, bf16[128,768]{1,0:T(8,128)(2,1)}, u32[]{:S(2)}, u32[]{:S(2)}) collective-permute-start(bf16[128,768]{1,0:T(8,128)(2,1)} %get-tuple-element.70.b0.normed_ref), channel_id=1, source_target_pairs={{0,6},{1,7},{2,0},{3,1},{4,2},{5,3},{6,4},{7,5},{8,14},{9,15},{10,... | collective-permute-start | bytes 589832 | tf_op jit(solution)/shard_map/ppermute | solution.py:43
  102.6 1.8 %shard_map.148 = bf16[128,1536]{1,0:T(8,128)(2,1)S(1)} custom-call(bf16[128,768]{1,0:T(8,128)(2,1)} %get-tuple-element.70.b0.normed_ref, bf16[768,2304]{1,0:T(8,128)(2,1)S(1)} %copy-done, s32[1,768]{1,0:T(1,128)S(1)} %broadcast_in_dim_reshape.3.offsets_ref), custom_call_target="tpu_custom_call" | custom-call | flops 1024 | bytes 4131840 | tf_op jit(solution)/shard_map/pallas_call | solution.py:54
  105.1 4.2 %all-to-all-start.2 = ((bf16[16,8,1536]{2,1,0:T(8,128)(2,1)}), bf16[16,8,1536]{2,1,0:T(8,128)(2,1)}, u32[]{:S(2)}, u32[]{:S(2)}) async-start(bf16[16,8,1536]{2,1,0:T(8,128)(2,1)} %bitcast.15), calls=%async_computation.2 | async-start | bytes 786432 | tf_op jit(solution)/shard_map/all_to_all | solution.py:432
  109.3 1.3 collective-permute-start.12
  113.8 3.3 %shard_map.146 = (bf16[64,768]{1,0:T(8,128)(2,1)S(1)}, bf16[1024,768]{1,0:T(8,128)(2,1)S(1)}) custom-call(bf16[128,768]{1,0:T(8,128)(2,1)} %get-tuple-element.70.b0.normed_ref, bf16[128,768]{1,0:T(8,128)(2,1)S(1)} %collective-permute-done.12.b1, bf16[128,768]{1,0:T(8,128)(2,1)} %collective-permute-done.13.b2, ...), custom_call_target="tpu_custom_call" | custom-call | flops 1024 | bytes 6786048 | tf_op jit(solution)/shard_map/pallas_call | solution.py:54
  119.8 2.6 %shard_map.149 = f32[64,896]{1,0:T(8,128)S(1)} custom-call(bf16[64,768]{1,0:T(8,128)(2,1)S(1)} %copy-done.14, bf16[128,1536]{1,0:T(8,128)(2,1)} %bitcast.6.kv_ref), custom_call_target="tpu_custom_call" | custom-call | flops 1024 | bytes 720896 | tf_op jit(solution)/shard_map/pallas_call | solution.py:54
  123.1 5.4 %all-to-all-start.3 = ((f32[8,8,896]{2,1,0:T(8,128)}), f32[8,8,896]{2,1,0:T(8,128)}, u32[]{:S(2)}, u32[]{:S(2)}) async-start(f32[8,8,896]{2,1,0:T(8,128)} %bitcast.16), calls=%async_computation.3 | async-start | bytes 458752 | tf_op jit(solution)/shard_map/all_to_all | solution.py:445
  128.5 1.4 %copy-done.10 = bf16[1024,768]{1,0:T(8,128)(2,1)S(1)} copy-done((bf16[1024,768]{1,0:T(8,128)(2,1)S(1)}, bf16[1024,768]{1,0:T(8,128)(2,1)}, u32[]{:S(2)}) %copy-start.10) | copy-done | bytes 1572888
  129.9 5.7 %shard_map.147.near = f32[6,128,256]{2,1,0:T(8,128)S(1)} custom-call(bf16[1024,768]{1,0:T(8,128)(2,1)S(1)} %copy-done.10, bf16[768,2304]{1,0:T(8,128)(2,1)S(1)} %copy-done), custom_call_target="tpu_custom_call" | custom-call | flops 1024 | bytes 5898240 | tf_op jit(solution)/shard_map/pallas_call | solution.py:54
  136.5 3.5 %shard_map.150 = bf16[128,768]{1,0:T(8,128)(2,1)} custom-call(f32[6,128,256]{2,1,0:T(8,128)} %copy-done.4, f32[64,896]{1,0:T(8,128)} %bitcast.8.far, f32[128,768]{1,0:T(8,128)} %copy-done.12, s32[1,768]{1,0:T(1,128)} %copy-done.15, bf16[768,768]{1,0:T(8,128)(2,1)} %w.1), custom_call_target="tpu_custom_call" | custom-call | flops 1024 | bytes 2788352 | tf_op jit(solution)/shard_map/pallas_call | solution.py:54
  (89 shorter events, 16.4 us)
Async XLA Ops:
  0.0 7.8 %copy-start.23 = (f32[768]{0:T(1024)S(1)}, f32[768]{0:T(1024)}, u32[]{:S(2)}) copy-start(f32[768]{0:T(1024)} %param.24) | copy-start | bytes 9220
  0.0 8.5 %copy-start.6 = (bf16[128,1536]{1,0:T(8,128)(2,1)S(1)}, bf16[128,1536]{1,0:T(8,128)(2,1)}, u32[]{:S(2)}) copy-start(bf16[128,1536]{1,0:T(8,128)(2,1)} %tokens_ref) | copy-start | bytes 1179652
  2.5 11.8 %collective-permute-start = (bf16[576,256]{1,0:T(8,128)(2,1)}, bf16[576,256]{1,0:T(8,128)(2,1)S(1)}, u32[]{:S(2)}, u32[]{:S(2)}) collective-permute-start(bf16[576,256]{1,0:T(8,128)(2,1)} %get-tuple-element.50), channel_id=1, source_target_pairs={{0,64},{1,65},{2,66},{3,67},{4,68},{5,69},{6,70},{7,71},{8,72},{9,... | collective-permute-start | bytes 884744 | tf_op jit(solution)/shard_map/ppermute | solution.py:43
  7.2 106.7 %copy-start.15 = (s32[1,768]{1,0:T(1,128)}, s32[1,768]{1,0:T(1,128)S(1)}, u32[]{:S(2)}) copy-start(s32[1,768]{1,0:T(1,128)S(1)} %broadcast_in_dim_reshape.3.offsets_ref) | copy-start | bytes 9220
  10.0 23.8 %copy-start.1 = (bf16[1536,256]{1,0:T(8,128)(2,1)S(1)}, bf16[1536,256]{1,0:T(8,128)(2,1)}, u32[]{:S(2)}) copy-start(bf16[1536,256]{1,0:T(8,128)(2,1)} %gate_ref.3) | copy-start | bytes 2359300
  10.0 23.8 %copy-start.2 = (bf16[1536,256]{1,0:T(8,128)(2,1)S(1)}, bf16[1536,256]{1,0:T(8,128)(2,1)}, u32[]{:S(2)}) copy-start(bf16[1536,256]{1,0:T(8,128)(2,1)} %up_ref.3) | copy-start | bytes 2359300
  10.0 23.8 %all-to-all-start = ((bf16[4,128,1536]{2,1,0:T(8,128)(2,1)}), bf16[4,128,1536]{2,1,0:T(8,128)(2,1)S(1)}, u32[]{:S(2)}, u32[]{:S(2)}) async-start(bf16[4,128,1536]{2,1,0:T(8,128)(2,1)} %bitcast), calls=%async_computation | async-start | bytes 3145728 | tf_op jit(solution)/shard_map/all_to_all | solution.py:48
  14.3 27.7 %collective-permute-start.5 = (bf16[2304,256]{1,0:T(8,128)(2,1)}, bf16[2304,256]{1,0:T(8,128)(2,1)}, u32[]{:S(2)}, u32[]{:S(2)}) collective-permute-start(bf16[2304,256]{1,0:T(8,128)(2,1)} %get-tuple-element.57), channel_id=1, source_target_pairs={{0,32},{1,33},{2,34},{3,35},{4,36},{5,37},{6,38},{7,39},{8,40},{9,... | collective-permute-start | bytes 3538952 | tf_op jit(solution)/shard_map/ppermute | solution.py:43
  15.1 29.2 %collective-permute-start.6 = (bf16[2304,256]{1,0:T(8,128)(2,1)}, bf16[2304,256]{1,0:T(8,128)(2,1)}, u32[]{:S(2)}, u32[]{:S(2)}) collective-permute-start(bf16[2304,256]{1,0:T(8,128)(2,1)} %get-tuple-element.57), channel_id=1, source_target_pairs={{0,96},{1,97},{2,98},{3,99},{4,100},{5,101},{6,102},{7,103},{8,104... | collective-permute-start | bytes 3538952 | tf_op jit(solution)/shard_map/ppermute | solution.py:43
  17.0 19.4 %collective-permute-start.1 = (bf16[576,256]{1,0:T(8,128)(2,1)S(1)}, bf16[576,256]{1,0:T(8,128)(2,1)}, u32[]{:S(2)}, u32[]{:S(2)}) collective-permute-start(bf16[576,256]{1,0:T(8,128)(2,1)S(1)} %collective-permute-done.q0), channel_id=1, source_target_pairs={{0,4},{1,5},{2,6},{3,7},{4,0},{5,1},{6,2},{7,3},{8,12},{9,13},{10,... | collective-permute-start | bytes 884744 | tf_op jit(solution)/shard_map/ppermute | solution.py:43
  19.7 16.6 %collective-permute-start.2 = (bf16[576,256]{1,0:T(8,128)(2,1)S(1)}, bf16[576,256]{1,0:T(8,128)(2,1)}, u32[]{:S(2)}, u32[]{:S(2)}) collective-permute-start(bf16[576,256]{1,0:T(8,128)(2,1)S(1)} %collective-permute-done.q0), channel_id=1, source_target_pairs={{0,2},{1,3},{2,4},{3,5},{4,6},{5,7},{6,0},{7,1},{8,10},{9,11},{10,... | collective-permute-start | bytes 884744 | tf_op jit(solution)/shard_map/ppermute | solution.py:43
  20.1 16.3 %collective-permute-start.3 = (bf16[576,256]{1,0:T(8,128)(2,1)S(1)}, bf16[576,256]{1,0:T(8,128)(2,1)}, u32[]{:S(2)}, u32[]{:S(2)}) collective-permute-start(bf16[576,256]{1,0:T(8,128)(2,1)S(1)} %collective-permute-done.q0), channel_id=1, source_target_pairs={{0,6},{1,7},{2,0},{3,1},{4,2},{5,3},{6,4},{7,5},{8,14},{9,15},{10,... | collective-permute-start | bytes 884744 | tf_op jit(solution)/shard_map/ppermute | solution.py:43
  37.6 6.6 %collective-permute-start.4 = (bf16[2304,256]{1,0:T(8,128)(2,1)S(1)}, bf16[2304,256]{1,0:T(8,128)(2,1)S(1)}, u32[]{:S(2)}, u32[]{:S(2)}) collective-permute-start(bf16[2304,256]{1,0:T(8,128)(2,1)S(1)} %shard_map.139.a), channel_id=1, source_target_pairs={{0,1},{1,0},{2,3},{3,2},{4,5},{5,4},{6,7},{7,6},{8,9},{9,8},{10,11... | collective-permute-start | bytes 3538952 | tf_op jit(solution)/shard_map/ppermute | solution.py:43
  42.1 6.8 %collective-permute-start.7 = (bf16[2304,256]{1,0:T(8,128)(2,1)}, bf16[2304,256]{1,0:T(8,128)(2,1)S(1)}, u32[]{:S(2)}, u32[]{:S(2)}) collective-permute-start(bf16[2304,256]{1,0:T(8,128)(2,1)} %collective-permute-done.5.a), channel_id=1, source_target_pairs={{0,1},{1,0},{2,3},{3,2},{4,5},{5,4},{6,7},{7,6},{8,9},{9,8},{10,11... | collective-permute-start | bytes 3538952 | tf_op jit(solution)/shard_map/ppermute | solution.py:43
  44.2 4.7 %collective-permute-start.8 = (bf16[2304,256]{1,0:T(8,128)(2,1)}, bf16[2304,256]{1,0:T(8,128)(2,1)S(1)}, u32[]{:S(2)}, u32[]{:S(2)}) collective-permute-start(bf16[2304,256]{1,0:T(8,128)(2,1)} %collective-permute-done.6.b), channel_id=1, source_target_pairs={{0,1},{1,0},{2,3},{3,2},{4,5},{5,4},{6,7},{7,6},{8,9},{9,8},{10,11... | collective-permute-start | bytes 3538952 | tf_op jit(solution)/shard_map/ppermute | solution.py:43
  48.8 22.9 %copy-start.7 = (bf16[128,1536]{1,0:T(8,128)(2,1)S(1)}, bf16[128,1536]{1,0:T(8,128)(2,1)}, u32[]{:S(2)}) copy-start(bf16[128,1536]{1,0:T(8,128)(2,1)} %tokens_ref) | copy-start | bytes 1179652
  48.9 22.9 %copy-start.16 = (f32[1,1536]{1,0:T(1,128)S(1)}, f32[1,1536]{1,0:T(1,128)}, u32[]{:S(2)}) copy-start(f32[1,1536]{1,0:T(1,128)} %broadcast_in_dim.20.gain_ref) | copy-start | bytes 18436
  48.9 22.9 %copy-start.5 = (bf16[1536,768]{1,0:T(8,128)(2,1)S(1)}, bf16[1536,768]{1,0:T(8,128)(2,1)}, u32[]{:S(2)}) copy-start(bf16[1536,768]{1,0:T(8,128)(2,1)} %w_ref.4) | copy-start | bytes 7077892
  50.7 11.8 %collective-permute-start.10 = (bf16[128,1536]{1,0:T(8,128)(2,1)S(1)}, bf16[128,1536]{1,0:T(8,128)(2,1)S(1)}, u32[]{:S(2)}, u32[]{:S(2)}) collective-permute-start(bf16[128,1536]{1,0:T(8,128)(2,1)S(1)} %get-tuple-element.61), channel_id=1, source_target_pairs={{0,16},{1,17},{2,18},{3,19},{4,20},{5,21},{6,22},{7,23},{8,24},{9,... | collective-permute-start | bytes 1179656 | tf_op jit(solution)/shard_map/ppermute | solution.py:43
  53.7 18.0 %collective-permute-start.11 = (bf16[128,1536]{1,0:T(8,128)(2,1)S(1)}, bf16[128,1536]{1,0:T(8,128)(2,1)S(1)}, u32[]{:S(2)}, u32[]{:S(2)}) collective-permute-start(bf16[128,1536]{1,0:T(8,128)(2,1)S(1)} %get-tuple-element.62), channel_id=1, source_target_pairs={{0,8},{1,9},{2,10},{3,11},{4,12},{5,13},{6,14},{7,15},{8,16},{9,17... | collective-permute-start | bytes 1179656 | tf_op jit(solution)/shard_map/ppermute | solution.py:43
  54.0 17.7 %collective-permute-start.9 = (bf16[128,1536]{1,0:T(8,128)(2,1)S(1)}, bf16[128,1536]{1,0:T(8,128)(2,1)S(1)}, u32[]{:S(2)}, u32[]{:S(2)}) collective-permute-start(bf16[128,1536]{1,0:T(8,128)(2,1)S(1)} %get-tuple-element.60), channel_id=1, source_target_pairs={{0,24},{1,25},{2,26},{3,27},{4,28},{5,29},{6,30},{7,31},{8,0},{9,1... | collective-permute-start | bytes 1179656 | tf_op jit(solution)/shard_map/ppermute | solution.py:43
  71.8 30.8 %copy-start = (bf16[768,2304]{1,0:T(8,128)(2,1)S(1)}, bf16[768,2304]{1,0:T(8,128)(2,1)}, u32[]{:S(2)}) copy-start(bf16[768,2304]{1,0:T(8,128)(2,1)} %w_ref.7) | copy-start | bytes 10616836
  73.0 22.5 %copy-start.17 = (f32[1,768]{1,0:T(1,128)S(1)}, f32[1,768]{1,0:T(1,128)}, u32[]{:S(2)}) copy-start(f32[1,768]{1,0:T(1,128)} %broadcast_in_dim_tile.3.frequency_ref) | copy-start | bytes 9220
  98.8 11.8 %collective-permute-start.13 = (bf16[128,768]{1,0:T(8,128)(2,1)}, bf16[128,768]{1,0:T(8,128)(2,1)}, u32[]{:S(2)}, u32[]{:S(2)}) collective-permute-start(bf16[128,768]{1,0:T(8,128)(2,1)} %get-tuple-element.70.b0.normed_ref), channel_id=1, source_target_pairs={{0,4},{1,5},{2,6},{3,7},{4,0},{5,1},{6,2},{7,3},{8,12},{9,13},{10,... | collective-permute-start | bytes 589832 | tf_op jit(solution)/shard_map/ppermute | solution.py:43
  99.9 11.8 %collective-permute-start.15 = (bf16[128,768]{1,0:T(8,128)(2,1)}, bf16[128,768]{1,0:T(8,128)(2,1)}, u32[]{:S(2)}, u32[]{:S(2)}) collective-permute-start(bf16[128,768]{1,0:T(8,128)(2,1)} %get-tuple-element.70.b0.normed_ref), channel_id=1, source_target_pairs={{0,2},{1,3},{2,4},{3,5},{4,6},{5,7},{6,0},{7,1},{8,10},{9,11},{10,... | collective-permute-start | bytes 589832 | tf_op jit(solution)/shard_map/ppermute | solution.py:43
  100.4 11.8 %collective-permute-start.17 = (bf16[128,768]{1,0:T(8,128)(2,1)}, bf16[128,768]{1,0:T(8,128)(2,1)}, u32[]{:S(2)}, u32[]{:S(2)}) collective-permute-start(bf16[128,768]{1,0:T(8,128)(2,1)} %get-tuple-element.70.b0.normed_ref), channel_id=1, source_target_pairs={{0,6},{1,7},{2,0},{3,1},{4,2},{5,3},{6,4},{7,5},{8,14},{9,15},{10,... | collective-permute-start | bytes 589832 | tf_op jit(solution)/shard_map/ppermute | solution.py:43
  105.1 13.8 %all-to-all-start.2 = ((bf16[16,8,1536]{2,1,0:T(8,128)(2,1)}), bf16[16,8,1536]{2,1,0:T(8,128)(2,1)}, u32[]{:S(2)}, u32[]{:S(2)}) async-start(bf16[16,8,1536]{2,1,0:T(8,128)(2,1)} %bitcast.15), calls=%async_computation.2 | async-start | bytes 786432 | tf_op jit(solution)/shard_map/all_to_all | solution.py:432
  109.3 2.8 %collective-permute-start.12 = (bf16[128,768]{1,0:T(8,128)(2,1)}, bf16[128,768]{1,0:T(8,128)(2,1)S(1)}, u32[]{:S(2)}, u32[]{:S(2)}) collective-permute-start(bf16[128,768]{1,0:T(8,128)(2,1)} %get-tuple-element.70.b0.normed_ref), channel_id=1, source_target_pairs={{0,1},{1,0},{2,3},{3,2},{4,5},{5,4},{6,7},{7,6},{8,9},{9,8},{10,11... | collective-permute-start | bytes 589832 | tf_op jit(solution)/shard_map/ppermute | solution.py:43
  110.7 1.7 %collective-permute-start.14 = (bf16[128,768]{1,0:T(8,128)(2,1)}, bf16[128,768]{1,0:T(8,128)(2,1)S(1)}, u32[]{:S(2)}, u32[]{:S(2)}) collective-permute-start(bf16[128,768]{1,0:T(8,128)(2,1)} %collective-permute-done.13.b2), channel_id=1, source_target_pairs={{0,1},{1,0},{2,3},{3,2},{4,5},{5,4},{6,7},{7,6},{8,9},{9,8},{10,11... | collective-permute-start | bytes 589832 | tf_op jit(solution)/shard_map/ppermute | solution.py:43
  111.7 1.8 %collective-permute-start.16 = (bf16[128,768]{1,0:T(8,128)(2,1)}, bf16[128,768]{1,0:T(8,128)(2,1)S(1)}, u32[]{:S(2)}, u32[]{:S(2)}) collective-permute-start(bf16[128,768]{1,0:T(8,128)(2,1)} %collective-permute-done.15.b4), channel_id=1, source_target_pairs={{0,1},{1,0},{2,3},{3,2},{4,5},{5,4},{6,7},{7,6},{8,9},{9,8},{10,11... | collective-permute-start | bytes 589832 | tf_op jit(solution)/shard_map/ppermute | solution.py:43
  112.2 1.7 %collective-permute-start.18 = (bf16[128,768]{1,0:T(8,128)(2,1)}, bf16[128,768]{1,0:T(8,128)(2,1)S(1)}, u32[]{:S(2)}, u32[]{:S(2)}) collective-permute-start(bf16[128,768]{1,0:T(8,128)(2,1)} %collective-permute-done.17.b6), channel_id=1, source_target_pairs={{0,1},{1,0},{2,3},{3,2},{4,5},{5,4},{6,7},{7,6},{8,9},{9,8},{10,11... | collective-permute-start | bytes 589832 | tf_op jit(solution)/shard_map/ppermute | solution.py:43
  123.1 13.4 %all-to-all-start.3 = ((f32[8,8,896]{2,1,0:T(8,128)}), f32[8,8,896]{2,1,0:T(8,128)}, u32[]{:S(2)}, u32[]{:S(2)}) async-start(f32[8,8,896]{2,1,0:T(8,128)} %bitcast.16), calls=%async_computation.3 | async-start | bytes 458752 | tf_op jit(solution)/shard_map/all_to_all | solution.py:445
  (15 other events, 52.6 us)

commit v6 on v5

--- a/solution.py
+++ b/solution.py
@@ -261,32 +261,29 @@
     return jnp.where(lax.shift_right_logical(row, 4) == group, 1.0, 0.0).astype(BF16)
 
 
-def place_kernel(payload_ref, frequency_ref, gain_ref, normed_ref, seq_ref):
+def place_kernel(payload_ref, frequency_ref, gain_ref, w_ref, offsets_ref, block_ref, far_ref, seq_ref):
     seq_in = slide_rows(payload_ref, frequency_ref)
     seq_ref[...] = seq_in
-    normed_ref[...] = layer_norm(seq_in, gain_ref[...]).astype(BF16)
-
-
-def far_keys_kernel(normed_ref, w_ref, offsets_ref, far_ref):
+    normed = layer_norm(seq_in, gain_ref[...]).astype(BF16)
+    block_ref[:ROWS, :] = normed
     kept = kept_columns(ROWS, offsets_ref)
     groups = group_matrix(KEPT)
-    for part in range(2):
-        cols = slice(D * (part + 1), D * (part + 2))
-        rows = jnp.where(kept, dot(normed_ref[...], w_ref[:, cols]), 0.0).astype(BF16)
-        chosen = dot(groups, rows).astype(BF16)
-        for n in range(16):
-            far_ref[KEPT * n : KEPT * (n + 1), D * part : D * (part + 1)] = chosen
-
-
-def far_queries_kernel(b0, b1, b2, b3, b4, b5, b6, b7, w_ref, offsets_ref, q_ref, rows_ref):
+    for part in range(3):
+        rows = dot(normed, w_ref[:, D * part : D * (part + 1)])
+        if part == 0:
+            rows = rows * (HEAD_WIDTH ** -0.5)
+        chosen = dot(groups, jnp.where(kept, rows, 0.0).astype(BF16)).astype(BF16)
+        if part == 0:
+            block_ref[ROWS:, :] = chosen
+        else:
+            for n in range(16):
+                far_ref[KEPT * n : KEPT * (n + 1), D * (part - 1) : D * part] = chosen
+
+
+def join_blocks_kernel(b0, b1, b2, b3, b4, b5, b6, b7, q_ref, rows_ref):
     for n, b in enumerate((b0, b1, b2, b3, b4, b5, b6, b7)):
-        rows_ref[ROWS * n : ROWS * (n + 1), :] = b[...]
-    kept = kept_columns(512, offsets_ref)
-    groups = group_matrix(4 * KEPT)
-    for n in range(2):
-        rows = dot(rows_ref[512 * n : 512 * (n + 1), :], w_ref[:, :D]) * (HEAD_WIDTH ** -0.5)
-        chosen = dot(groups, jnp.where(kept, rows, 0.0).astype(BF16))
-        q_ref[4 * KEPT * n : 4 * KEPT * (n + 1), :] = chosen.astype(BF16)
+        rows_ref[ROWS * n : ROWS * (n + 1), :] = b[:ROWS, :]
+        q_ref[KEPT * n : KEPT * (n + 1), :] = b[ROWS:, :]
 
 
 def attend_pair(queries, keys, values):
@@ -420,26 +417,23 @@
     )
     payload = payload.reshape(2, devices, D + ROWS)
     payload = lax.all_to_all(payload, AXES, split_axis=1, concat_axis=1, tiled=True)
-    normed, seq_in = call(
+    block, far_kv, seq_in = call(
         place_kernel,
-        [((ROWS, D), BF16), ((ROWS, D), F32)],
+        [((ROWS + KEPT, D), BF16), ((ROWS, 2 * D), BF16), ((ROWS, D), F32)],
         payload.reshape(2 * ROWS, D + ROWS),
         frequency,
         attn_gain,
-    )
-    held = [normed, shift(normed, x=2), shift(normed, x=1), shift(normed, x=-1)]
-    (far_kv,) = call(far_keys_kernel, [((ROWS, 2 * D), BF16)], normed, w_qkv, offset_columns)
+        w_qkv,
+        offset_columns,
+    )
+    held = [block, shift(block, x=2), shift(block, x=1), shift(block, x=-1)]
     far_kv = lax.all_to_all(far_kv, "tile", split_axis=0, concat_axis=0, tiled=True)
     blocks = []
     for block in held:
         blocks += [block, swap(block)]
     segment = SEGMENT_DEVICES * ROWS
     far_queries, rows = call(
-        far_queries_kernel,
-        [((SEGMENT_DEVICES * KEPT, D), BF16), ((segment, D), BF16)],
-        *blocks,
-        w_qkv,
-        offset_columns,
+        join_blocks_kernel, [((SEGMENT_DEVICES * KEPT, D), BF16), ((segment, D), BF16)], *blocks
     )
     (far_parts,) = call(far_kernel, [((SEGMENT_DEVICES * KEPT, D + 128), F32)], far_queries, far_kv)
     far_parts = lax.all_to_all(far_parts, "seq", split_axis=0, concat_axis=0, tiled=True)

time: 141 us -> 140 us (level)
  Pallas kernels: 33.6 us -> 30.3 us
  waiting for transfers between devices: 31.4 us -> 33.1 us
    pallas_call x15 -> x14, Pallas kernels: 33.6 us -> 30.3 us  [call(): pl.pallas_call(kernel, out_shape=outs, in_specs=spaces or [VMEM] * len(ar...]
    ppermute x19, waiting for transfers between devices: 20 us -> 21.6 us  [shift(): return lax.ppermute(value, AXES, pairs)]
    ppermute x19, starting transfers between devices: 28.4 us -> 29.8 us  [shift(): return lax.ppermute(value, AXES, pairs)]
  transfers between devices with their start and end apart: 22 -> 22, of which waited for: 8 -> 7; matrix products, arithmetic and copies ran while one was open for 1% -> 1% of each run, Pallas kernels for 14% -> 11%
where the time goes in v6:
time: 140 us; the launch traced here: 139 us
  starting transfers between devices  42.6 us (30%)
  waiting for transfers between devices  33.1 us (24%)
  Pallas kernels  30.3 us (22%)
  blocking collectives  22 us (16%)
  local copies, waits for them, and re-layouts  10.4 us (7%)
    pallas_call x14, Pallas kernels, call(): pl.pallas_call(kernel, out_shape=outs, in_specs=spaces or [VMEM] * len(ar...  30.3 us
    ppermute x19, starting transfers between devices, shift(): return lax.ppermute(value, AXES, pairs)  29.8 us
    all_to_all x1, blocking collectives, body(): lax.all_to_all(payload, AXES, split_axis=1, concat_axis=1, tiled=True)  22 us
    ppermute x19, waiting for transfers between devices, shift(): return lax.ppermute(value, AXES, pairs)  21.6 us
    all_to_all x1, waiting for transfers between devices, along_y(): lax.all_to_all(value, 'tile', split_axis=0, concat_axis=0, axis_index_gro...  11.4 us
    unnamed x50, local copies, waits for them, and re-layouts  8.41 us
    all_to_all x1, starting transfers between devices, along_y(): lax.all_to_all(value, 'tile', split_axis=0, concat_axis=0, axis_index_gro...  4.31 us
    all_to_all x1, starting transfers between devices, body(): lax.all_to_all(far_parts, 'seq', split_axis=0, concat_axis=0, tiled=True)  4.23 us
  transfers between devices with their start and end apart: 22, of which 7 were waited for; matrix products, arithmetic and copies ran while one was open for 1% of the time, Pallas kernels for 11%

profile of v6, /device:TPU:1, one launch (start us, length us, event | category | flops | bytes accessed | tf_op | source)
XLA Modules:
  0.0 138.8 jit_solution(3171736726661270250)
XLA Ops:
  0.0 2.4 %shard_map.136 = (bf16[2304,256]{1,0:T(8,128)(2,1)}, bf16[576,256]{1,0:T(8,128)(2,1)}) custom-call(bf16[1536,256]{1,0:T(8,128)(2,1)} %gate_ref.3, bf16[1536,256]{1,0:T(8,128)(2,1)} %up_ref.3, bf16[256,1536]{1,0:T(8,128)(2,1)} %down_ref.3), custom_call_target="tpu_custom_call" | custom-call | flops 1024 | bytes 3833856 | tf_op jit(solution)/shard_map/pallas_call | solution.py:54
  2.5 4.5 %collective-permute-start = (bf16[576,256]{1,0:T(8,128)(2,1)}, bf16[576,256]{1,0:T(8,128)(2,1)S(1)}, u32[]{:S(2)}, u32[]{:S(2)}) collective-permute-start(bf16[576,256]{1,0:T(8,128)(2,1)} %get-tuple-element.51), channel_id=1, source_target_pairs={{0,64},{1,65},{2,66},{3,67},{4,68},{5,69},{6,70},{7,71},{8,72},{9,... | collective-permute-start | bytes 884744 | tf_op jit(solution)/shard_map/ppermute | solution.py:43
  8.5 1.5 %shard_map.137 = bf16[512,1536]{1,0:T(8,128)(2,1)} custom-call(bf16[128,1536]{1,0:T(8,128)(2,1)S(1)} %copy-done.6, f32[1,1536]{1,0:T(1,128)S(1)} %broadcast_in_dim.22.gain_ref), custom_call_target="tpu_custom_call" | custom-call | flops 1024 | bytes 1972224 | tf_op jit(solution)/shard_map/pallas_call | solution.py:54
  10.0 4.3 %all-to-all-start = ((bf16[4,128,1536]{2,1,0:T(8,128)(2,1)}), bf16[4,128,1536]{2,1,0:T(8,128)(2,1)S(1)}, u32[]{:S(2)}, u32[]{:S(2)}) async-start(bf16[4,128,1536]{2,1,0:T(8,128)(2,1)} %bitcast), calls=%async_computation | async-start | bytes 3145728 | tf_op jit(solution)/shard_map/all_to_all | solution.py:48
  15.1 1.9 %collective-permute-start.6 = (bf16[2304,256]{1,0:T(8,128)(2,1)}, bf16[2304,256]{1,0:T(8,128)(2,1)}, u32[]{:S(2)}, u32[]{:S(2)}) collective-permute-start(bf16[2304,256]{1,0:T(8,128)(2,1)} %get-tuple-element.58), channel_id=1, source_target_pairs={{0,96},{1,97},{2,98},{3,99},{4,100},{5,101},{6,102},{7,103},{8,104... | collective-permute-start | bytes 3538952 | tf_op jit(solution)/shard_map/ppermute | solution.py:43
  17.0 2.7 %collective-permute-start.1 = (bf16[576,256]{1,0:T(8,128)(2,1)S(1)}, bf16[576,256]{1,0:T(8,128)(2,1)}, u32[]{:S(2)}, u32[]{:S(2)}) collective-permute-start(bf16[576,256]{1,0:T(8,128)(2,1)S(1)} %collective-permute-done.q0), channel_id=1, source_target_pairs={{0,4},{1,5},{2,6},{3,7},{4,0},{5,1},{6,2},{7,3},{8,12},{9,13},{10,... | collective-permute-start | bytes 884744 | tf_op jit(solution)/shard_map/ppermute | solution.py:43
  20.1 2.4 %collective-permute-start.3 = (bf16[576,256]{1,0:T(8,128)(2,1)S(1)}, bf16[576,256]{1,0:T(8,128)(2,1)}, u32[]{:S(2)}, u32[]{:S(2)}) collective-permute-start(bf16[576,256]{1,0:T(8,128)(2,1)S(1)} %collective-permute-done.q0), channel_id=1, source_target_pairs={{0,6},{1,7},{2,0},{3,1},{4,2},{5,3},{6,4},{7,5},{8,14},{9,15},{10,... | collective-permute-start | bytes 884744 | tf_op jit(solution)/shard_map/ppermute | solution.py:43
  22.4 11.4 %all-to-all-done = bf16[4,128,1536]{2,1,0:T(8,128)(2,1)S(1)} async-done(((bf16[4,128,1536]{2,1,0:T(8,128)(2,1)}), bf16[4,128,1536]{2,1,0:T(8,128)(2,1)S(1)}, u32[]{:S(2)}, u32[]{:S(2)}) %all-to-all-start) | async-done | bytes 1572896 | tf_op jit(solution)/shard_map/all_to_all | solution.py:48
  35.0 1.4 shard_map.138.total_ref
  37.6 2.2 %collective-permute-start.4 = (bf16[2304,256]{1,0:T(8,128)(2,1)S(1)}, bf16[2304,256]{1,0:T(8,128)(2,1)S(1)}, u32[]{:S(2)}, u32[]{:S(2)}) collective-permute-start(bf16[2304,256]{1,0:T(8,128)(2,1)S(1)} %shard_map.139.a), channel_id=1, source_target_pairs={{0,1},{1,0},{2,3},{3,2},{4,5},{5,4},{6,7},{7,6},{8,9},{9,8},{10,11... | collective-permute-start | bytes 3538952 | tf_op jit(solution)/shard_map/ppermute | solution.py:43
  39.9 2.2 %collective-permute-done.5.a = bf16[2304,256]{1,0:T(8,128)(2,1)} collective-permute-done((bf16[2304,256]{1,0:T(8,128)(2,1)}, bf16[2304,256]{1,0:T(8,128)(2,1)}, u32[]{:S(2)}, u32[]{:S(2)}) %collective-permute-start.5) | collective-permute-done | bytes 1179680 | tf_op jit(solution)/shard_map/ppermute | solution.py:43
  42.1 2.2 %collective-permute-start.7 = (bf16[2304,256]{1,0:T(8,128)(2,1)}, bf16[2304,256]{1,0:T(8,128)(2,1)S(1)}, u32[]{:S(2)}, u32[]{:S(2)}) collective-permute-start(bf16[2304,256]{1,0:T(8,128)(2,1)} %collective-permute-done.5.a), channel_id=1, source_target_pairs={{0,1},{1,0},{2,3},{3,2},{4,5},{5,4},{6,7},{7,6},{8,9},{9,8},{10,11... | collective-permute-start | bytes 3538952 | tf_op jit(solution)/shard_map/ppermute | solution.py:43
  44.2 1.5 %shard_map.140.total_ref = f32[512,1536]{1,0:T(8,128)S(1)} custom-call(bf16[512,1536]{1,0:T(8,128)(2,1)S(1)} %bitcast.10, f32[512,1536]{1,0:T(8,128)S(1)} %shard_map.138.total_ref, bf16[2304,256]{1,0:T(8,128)(2,1)S(1)} %shard_map.139.a, bf16[2304,256]{1,0:T(8,128)(2,1)S(1)} %collective-permute-done.4.b), custom_call_target="tpu_custom_call" | custom-call | flops 1024 | bytes 10223616 | tf_op jit(solution)/shard_map/pallas_call | solution.py:54
  45.7 3.1 %shard_map.141.total_ref = f32[512,1536]{1,0:T(8,128)S(1)} custom-call(bf16[512,1536]{1,0:T(8,128)(2,1)S(1)} %bitcast.11, f32[512,1536]{1,0:T(8,128)S(1)} %shard_map.140.total_ref, bf16[2304,256]{1,0:T(8,128)(2,1)} %collective-permute-done.5.a, bf16[2304,256]{1,0:T(8,128)(2,1)} %collective-permute-done.6.b), custom_call_target="tpu_custom_call" | custom-call | flops 1024 | bytes 10223616 | tf_op jit(solution)/shard_map/pallas_call | solution.py:54
  48.9 1.8 %shard_map.142 = (f32[128,1536]{1,0:T(8,128)S(1)}, bf16[128,1536]{1,0:T(8,128)(2,1)S(1)}, bf16[128,1536]{1,0:T(8,128)(2,1)S(1)}, bf16[128,1536]{1,0:T(8,128)(2,1)S(1)}) custom-call(bf16[512,1536]{1,0:T(8,128)(2,1)S(1)} %bitcast.12, f32[512,1536]{1,0:T(8,128)S(1)} %shard_map.141.total_ref, bf16[2304,256]{1,0:T(8,128)(2,1)S(1)} %collective-permute-done.7.a, ...), custom_call_target="tpu_custom_call" | custom-call | flops 1024 | bytes 9043968 | tf_op jit(solution)/shard_map/pallas_call | solution.py:54
  50.7 3.0 %collective-permute-start.10 = (bf16[128,1536]{1,0:T(8,128)(2,1)S(1)}, bf16[128,1536]{1,0:T(8,128)(2,1)S(1)}, u32[]{:S(2)}, u32[]{:S(2)}) collective-permute-start(bf16[128,1536]{1,0:T(8,128)(2,1)S(1)} %get-tuple-element.62), channel_id=1, source_target_pairs={{0,16},{1,17},{2,18},{3,19},{4,20},{5,21},{6,22},{7,23},{8,24},{9,... | collective-permute-start | bytes 1179656 | tf_op jit(solution)/shard_map/ppermute | solution.py:43
  54.0 2.4 %collective-permute-start.9 = (bf16[128,1536]{1,0:T(8,128)(2,1)S(1)}, bf16[128,1536]{1,0:T(8,128)(2,1)S(1)}, u32[]{:S(2)}, u32[]{:S(2)}) collective-permute-start(bf16[128,1536]{1,0:T(8,128)(2,1)S(1)} %get-tuple-element.61), channel_id=1, source_target_pairs={{0,24},{1,25},{2,26},{3,27},{4,28},{5,29},{6,30},{7,31},{8,0},{9,1... | collective-permute-start | bytes 1179656 | tf_op jit(solution)/shard_map/ppermute | solution.py:43
  56.5 6.0 %collective-permute-done.10.b = bf16[128,1536]{1,0:T(8,128)(2,1)S(1)} collective-permute-done((bf16[128,1536]{1,0:T(8,128)(2,1)S(1)}, bf16[128,1536]{1,0:T(8,128)(2,1)S(1)}, u32[]{:S(2)}, u32[]{:S(2)}) %collective-permute-start.10) | collective-permute-done | bytes 393248 | tf_op jit(solution)/shard_map/ppermute | solution.py:43
  62.5 9.2 %collective-permute-done.11.c = bf16[128,1536]{1,0:T(8,128)(2,1)S(1)} collective-permute-done((bf16[128,1536]{1,0:T(8,128)(2,1)S(1)}, bf16[128,1536]{1,0:T(8,128)(2,1)S(1)}, u32[]{:S(2)}, u32[]{:S(2)}) %collective-permute-start.11) | collective-permute-done | bytes 393248 | tf_op jit(solution)/shard_map/ppermute | solution.py:43
  73.5 22.0 %all_to_all.38 = bf16[2,128,896]{2,0,1:T(2,128)(2,1)S(1)} all-to-all(bf16[2,128,896]{2,0,1:T(2,128)(2,1)S(1)} %copy.15), channel_id=1, replica_groups=mesh['tile'=16,'seq'=8] {'tile','seq'}, dimensions={1} | all-to-all | bytes 917504 | tf_op jit(solution)/shard_map/all_to_all | solution.py:419
  95.5 3.0 %shard_map.145 = (bf16[136,768]{1,0:T(8,128)(2,1)}, bf16[128,1536]{1,0:T(8,128)(2,1)S(1)}, f32[128,768]{1,0:T(8,128)S(1)}) custom-call(bf16[256,896]{1,0:T(8,128)(2,1)S(1)} %bitcast.14, f32[1,768]{1,0:T(1,128)S(1)} %copy-done.17, f32[1,768]{1,0:T(1,128)S(1)} %broadcast_in_dim.21.gain_ref, bf16[768,2304]{1,0:T(8,128)(2,1)S(1)} %copy-done, ...), custom_call_target="tpu_custom_call" | custom-call | flops 1024 | bytes 5002240 | tf_op jit(solution)/shard_map/pallas_call | solution.py:54
  101.6 2.2 %collective-permute-start.17 = (bf16[136,768]{1,0:T(8,128)(2,1)}, bf16[136,768]{1,0:T(8,128)(2,1)}, u32[]{:S(2)}, u32[]{:S(2)}) collective-permute-start(bf16[136,768]{1,0:T(8,128)(2,1)} %get-tuple-element.72.b0), channel_id=1, source_target_pairs={{0,6},{1,7},{2,0},{3,1},{4,2},{5,3},{6,4},{7,5},{8,14},{9,15},{10,... | collective-permute-start | bytes 626696 | tf_op jit(solution)/shard_map/ppermute | solution.py:43
  103.8 4.2 %all-to-all-start.2 = ((bf16[16,8,1536]{2,1,0:T(8,128)(2,1)}), bf16[16,8,1536]{2,1,0:T(8,128)(2,1)}, u32[]{:S(2)}, u32[]{:S(2)}) async-start(bf16[16,8,1536]{2,1,0:T(8,128)(2,1)} %bitcast.16), calls=%async_computation.2 | async-start | bytes 786432 | tf_op jit(solution)/shard_map/all_to_all | solution.py:430
  108.0 1.3 collective-permute-start.12
  109.4 1.5 %collective-permute-start.14 = (bf16[136,768]{1,0:T(8,128)(2,1)}, bf16[136,768]{1,0:T(8,128)(2,1)S(1)}, u32[]{:S(2)}, u32[]{:S(2)}) collective-permute-start(bf16[136,768]{1,0:T(8,128)(2,1)} %collective-permute-done.13.b2), channel_id=1, source_target_pairs={{0,1},{1,0},{2,3},{3,2},{4,5},{5,4},{6,7},{7,6},{8,9},{9,8},{10,11... | collective-permute-start | bytes 626696 | tf_op jit(solution)/shard_map/ppermute | solution.py:43
  110.9 2.6 %collective-permute-done.15.b4 = bf16[136,768]{1,0:T(8,128)(2,1)} collective-permute-done((bf16[136,768]{1,0:T(8,128)(2,1)}, bf16[136,768]{1,0:T(8,128)(2,1)}, u32[]{:S(2)}, u32[]{:S(2)}) %collective-permute-start.15) | collective-permute-done | bytes 208928 | tf_op jit(solution)/shard_map/ppermute | solution.py:43
  115.6 1.3 shard_map.146
  119.7 2.6 %shard_map.148 = f32[64,896]{1,0:T(8,128)S(1)} custom-call(bf16[64,768]{1,0:T(8,128)(2,1)S(1)} %copy-done.14, bf16[128,1536]{1,0:T(8,128)(2,1)} %bitcast.6.kv_ref), custom_call_target="tpu_custom_call" | custom-call | flops 1024 | bytes 720896 | tf_op jit(solution)/shard_map/pallas_call | solution.py:54
  122.9 4.2 %all-to-all-start.3 = ((f32[8,8,896]{2,1,0:T(8,128)}), f32[8,8,896]{2,1,0:T(8,128)}, u32[]{:S(2)}, u32[]{:S(2)}) async-start(f32[8,8,896]{2,1,0:T(8,128)} %bitcast.15), calls=%async_computation.3 | async-start | bytes 458752 | tf_op jit(solution)/shard_map/all_to_all | solution.py:439
  127.2 1.4 %copy-done.9 = bf16[1024,768]{1,0:T(8,128)(2,1)S(1)} copy-done((bf16[1024,768]{1,0:T(8,128)(2,1)S(1)}, bf16[1024,768]{1,0:T(8,128)(2,1)}, u32[]{:S(2)}) %copy-start.9) | copy-done | bytes 1572888
  128.6 5.7 %shard_map.147.near = f32[6,128,256]{2,1,0:T(8,128)S(1)} custom-call(bf16[1024,768]{1,0:T(8,128)(2,1)S(1)} %copy-done.9, bf16[768,2304]{1,0:T(8,128)(2,1)S(1)} %copy-done), custom_call_target="tpu_custom_call" | custom-call | flops 1024 | bytes 5898240 | tf_op jit(solution)/shard_map/pallas_call | solution.py:54
  135.2 3.5 %shard_map.149 = bf16[128,768]{1,0:T(8,128)(2,1)} custom-call(f32[6,128,256]{2,1,0:T(8,128)} %copy-done.4, f32[64,896]{1,0:T(8,128)} %bitcast.8.far, f32[128,768]{1,0:T(8,128)} %copy-done.12, s32[1,768]{1,0:T(1,128)} %copy-done.15, bf16[768,768]{1,0:T(8,128)(2,1)} %w.1), custom_call_target="tpu_custom_call" | custom-call | flops 1024 | bytes 2788352 | tf_op jit(solution)/shard_map/pallas_call | solution.py:54
  (88 shorter events, 16.6 us)
Async XLA Ops:
  0.0 7.8 %copy-start.23 = (f32[768]{0:T(1024)S(1)}, f32[768]{0:T(1024)}, u32[]{:S(2)}) copy-start(f32[768]{0:T(1024)} %param.24) | copy-start | bytes 9220
  0.0 8.5 %copy-start.6 = (bf16[128,1536]{1,0:T(8,128)(2,1)S(1)}, bf16[128,1536]{1,0:T(8,128)(2,1)}, u32[]{:S(2)}) copy-start(bf16[128,1536]{1,0:T(8,128)(2,1)} %tokens_ref) | copy-start | bytes 1179652
  2.5 11.8 %collective-permute-start = (bf16[576,256]{1,0:T(8,128)(2,1)}, bf16[576,256]{1,0:T(8,128)(2,1)S(1)}, u32[]{:S(2)}, u32[]{:S(2)}) collective-permute-start(bf16[576,256]{1,0:T(8,128)(2,1)} %get-tuple-element.51), channel_id=1, source_target_pairs={{0,64},{1,65},{2,66},{3,67},{4,68},{5,69},{6,70},{7,71},{8,72},{9,... | collective-permute-start | bytes 884744 | tf_op jit(solution)/shard_map/ppermute | solution.py:43
  7.2 88.3 %copy-start.15 = (s32[1,768]{1,0:T(1,128)}, s32[1,768]{1,0:T(1,128)S(1)}, u32[]{:S(2)}) copy-start(s32[1,768]{1,0:T(1,128)S(1)} %broadcast_in_dim_reshape.3.offsets_ref) | copy-start | bytes 9220
  10.0 23.8 %copy-start.1 = (bf16[1536,256]{1,0:T(8,128)(2,1)S(1)}, bf16[1536,256]{1,0:T(8,128)(2,1)}, u32[]{:S(2)}) copy-start(bf16[1536,256]{1,0:T(8,128)(2,1)} %gate_ref.3) | copy-start | bytes 2359300
  10.0 23.8 %copy-start.2 = (bf16[1536,256]{1,0:T(8,128)(2,1)S(1)}, bf16[1536,256]{1,0:T(8,128)(2,1)}, u32[]{:S(2)}) copy-start(bf16[1536,256]{1,0:T(8,128)(2,1)} %up_ref.3) | copy-start | bytes 2359300
  10.0 23.8 %all-to-all-start = ((bf16[4,128,1536]{2,1,0:T(8,128)(2,1)}), bf16[4,128,1536]{2,1,0:T(8,128)(2,1)S(1)}, u32[]{:S(2)}, u32[]{:S(2)}) async-start(bf16[4,128,1536]{2,1,0:T(8,128)(2,1)} %bitcast), calls=%async_computation | async-start | bytes 3145728 | tf_op jit(solution)/shard_map/all_to_all | solution.py:48
  14.3 27.7 %collective-permute-start.5 = (bf16[2304,256]{1,0:T(8,128)(2,1)}, bf16[2304,256]{1,0:T(8,128)(2,1)}, u32[]{:S(2)}, u32[]{:S(2)}) collective-permute-start(bf16[2304,256]{1,0:T(8,128)(2,1)} %get-tuple-element.58), channel_id=1, source_target_pairs={{0,32},{1,33},{2,34},{3,35},{4,36},{5,37},{6,38},{7,39},{8,40},{9,... | collective-permute-start | bytes 3538952 | tf_op jit(solution)/shard_map/ppermute | solution.py:43
  15.1 29.2 %collective-permute-start.6 = (bf16[2304,256]{1,0:T(8,128)(2,1)}, bf16[2304,256]{1,0:T(8,128)(2,1)}, u32[]{:S(2)}, u32[]{:S(2)}) collective-permute-start(bf16[2304,256]{1,0:T(8,128)(2,1)} %get-tuple-element.58), channel_id=1, source_target_pairs={{0,96},{1,97},{2,98},{3,99},{4,100},{5,101},{6,102},{7,103},{8,104... | collective-permute-start | bytes 3538952 | tf_op jit(solution)/shard_map/ppermute | solution.py:43
  17.0 19.4 %collective-permute-start.1 = (bf16[576,256]{1,0:T(8,128)(2,1)S(1)}, bf16[576,256]{1,0:T(8,128)(2,1)}, u32[]{:S(2)}, u32[]{:S(2)}) collective-permute-start(bf16[576,256]{1,0:T(8,128)(2,1)S(1)} %collective-permute-done.q0), channel_id=1, source_target_pairs={{0,4},{1,5},{2,6},{3,7},{4,0},{5,1},{6,2},{7,3},{8,12},{9,13},{10,... | collective-permute-start | bytes 884744 | tf_op jit(solution)/shard_map/ppermute | solution.py:43
  19.7 16.6 %collective-permute-start.2 = (bf16[576,256]{1,0:T(8,128)(2,1)S(1)}, bf16[576,256]{1,0:T(8,128)(2,1)}, u32[]{:S(2)}, u32[]{:S(2)}) collective-permute-start(bf16[576,256]{1,0:T(8,128)(2,1)S(1)} %collective-permute-done.q0), channel_id=1, source_target_pairs={{0,2},{1,3},{2,4},{3,5},{4,6},{5,7},{6,0},{7,1},{8,10},{9,11},{10,... | collective-permute-start | bytes 884744 | tf_op jit(solution)/shard_map/ppermute | solution.py:43
  20.1 16.3 %collective-permute-start.3 = (bf16[576,256]{1,0:T(8,128)(2,1)S(1)}, bf16[576,256]{1,0:T(8,128)(2,1)}, u32[]{:S(2)}, u32[]{:S(2)}) collective-permute-start(bf16[576,256]{1,0:T(8,128)(2,1)S(1)} %collective-permute-done.q0), channel_id=1, source_target_pairs={{0,6},{1,7},{2,0},{3,1},{4,2},{5,3},{6,4},{7,5},{8,14},{9,15},{10,... | collective-permute-start | bytes 884744 | tf_op jit(solution)/shard_map/ppermute | solution.py:43
  37.6 6.6 %collective-permute-start.4 = (bf16[2304,256]{1,0:T(8,128)(2,1)S(1)}, bf16[2304,256]{1,0:T(8,128)(2,1)S(1)}, u32[]{:S(2)}, u32[]{:S(2)}) collective-permute-start(bf16[2304,256]{1,0:T(8,128)(2,1)S(1)} %shard_map.139.a), channel_id=1, source_target_pairs={{0,1},{1,0},{2,3},{3,2},{4,5},{5,4},{6,7},{7,6},{8,9},{9,8},{10,11... | collective-permute-start | bytes 3538952 | tf_op jit(solution)/shard_map/ppermute | solution.py:43
  42.1 6.8 %collective-permute-start.7 = (bf16[2304,256]{1,0:T(8,128)(2,1)}, bf16[2304,256]{1,0:T(8,128)(2,1)S(1)}, u32[]{:S(2)}, u32[]{:S(2)}) collective-permute-start(bf16[2304,256]{1,0:T(8,128)(2,1)} %collective-permute-done.5.a), channel_id=1, source_target_pairs={{0,1},{1,0},{2,3},{3,2},{4,5},{5,4},{6,7},{7,6},{8,9},{9,8},{10,11... | collective-permute-start | bytes 3538952 | tf_op jit(solution)/shard_map/ppermute | solution.py:43
  44.2 4.7 %collective-permute-start.8 = (bf16[2304,256]{1,0:T(8,128)(2,1)}, bf16[2304,256]{1,0:T(8,128)(2,1)S(1)}, u32[]{:S(2)}, u32[]{:S(2)}) collective-permute-start(bf16[2304,256]{1,0:T(8,128)(2,1)} %collective-permute-done.6.b), channel_id=1, source_target_pairs={{0,1},{1,0},{2,3},{3,2},{4,5},{5,4},{6,7},{7,6},{8,9},{9,8},{10,11... | collective-permute-start | bytes 3538952 | tf_op jit(solution)/shard_map/ppermute | solution.py:43
  48.8 22.9 %copy-start.7 = (bf16[128,1536]{1,0:T(8,128)(2,1)S(1)}, bf16[128,1536]{1,0:T(8,128)(2,1)}, u32[]{:S(2)}) copy-start(bf16[128,1536]{1,0:T(8,128)(2,1)} %tokens_ref) | copy-start | bytes 1179652
  48.9 22.9 %copy-start.16 = (f32[1,1536]{1,0:T(1,128)S(1)}, f32[1,1536]{1,0:T(1,128)}, u32[]{:S(2)}) copy-start(f32[1,1536]{1,0:T(1,128)} %broadcast_in_dim.20.gain_ref) | copy-start | bytes 18436
  48.9 22.9 %copy-start.5 = (bf16[1536,768]{1,0:T(8,128)(2,1)S(1)}, bf16[1536,768]{1,0:T(8,128)(2,1)}, u32[]{:S(2)}) copy-start(bf16[1536,768]{1,0:T(8,128)(2,1)} %w_ref.3) | copy-start | bytes 7077892
  50.7 11.8 %collective-permute-start.10 = (bf16[128,1536]{1,0:T(8,128)(2,1)S(1)}, bf16[128,1536]{1,0:T(8,128)(2,1)S(1)}, u32[]{:S(2)}, u32[]{:S(2)}) collective-permute-start(bf16[128,1536]{1,0:T(8,128)(2,1)S(1)} %get-tuple-element.62), channel_id=1, source_target_pairs={{0,16},{1,17},{2,18},{3,19},{4,20},{5,21},{6,22},{7,23},{8,24},{9,... | collective-permute-start | bytes 1179656 | tf_op jit(solution)/shard_map/ppermute | solution.py:43
  53.7 18.0 %collective-permute-start.11 = (bf16[128,1536]{1,0:T(8,128)(2,1)S(1)}, bf16[128,1536]{1,0:T(8,128)(2,1)S(1)}, u32[]{:S(2)}, u32[]{:S(2)}) collective-permute-start(bf16[128,1536]{1,0:T(8,128)(2,1)S(1)} %get-tuple-element.63), channel_id=1, source_target_pairs={{0,8},{1,9},{2,10},{3,11},{4,12},{5,13},{6,14},{7,15},{8,16},{9,17... | collective-permute-start | bytes 1179656 | tf_op jit(solution)/shard_map/ppermute | solution.py:43
  54.0 17.7 %collective-permute-start.9 = (bf16[128,1536]{1,0:T(8,128)(2,1)S(1)}, bf16[128,1536]{1,0:T(8,128)(2,1)S(1)}, u32[]{:S(2)}, u32[]{:S(2)}) collective-permute-start(bf16[128,1536]{1,0:T(8,128)(2,1)S(1)} %get-tuple-element.61), channel_id=1, source_target_pairs={{0,24},{1,25},{2,26},{3,27},{4,28},{5,29},{6,30},{7,31},{8,0},{9,1... | collective-permute-start | bytes 1179656 | tf_op jit(solution)/shard_map/ppermute | solution.py:43
  71.8 23.8 %copy-start = (bf16[768,2304]{1,0:T(8,128)(2,1)S(1)}, bf16[768,2304]{1,0:T(8,128)(2,1)}, u32[]{:S(2)}) copy-start(bf16[768,2304]{1,0:T(8,128)(2,1)} %w_ref.5) | copy-start | bytes 10616836
  73.0 22.5 %copy-start.17 = (f32[1,768]{1,0:T(1,128)S(1)}, f32[1,768]{1,0:T(1,128)}, u32[]{:S(2)}) copy-start(f32[1,768]{1,0:T(1,128)} %broadcast_in_dim_tile.3.frequency_ref) | copy-start | bytes 9220
  100.1 9.3 %collective-permute-start.13 = (bf16[136,768]{1,0:T(8,128)(2,1)}, bf16[136,768]{1,0:T(8,128)(2,1)}, u32[]{:S(2)}, u32[]{:S(2)}) collective-permute-start(bf16[136,768]{1,0:T(8,128)(2,1)} %get-tuple-element.72.b0), channel_id=1, source_target_pairs={{0,4},{1,5},{2,6},{3,7},{4,0},{5,1},{6,2},{7,3},{8,12},{9,13},{10,... | collective-permute-start | bytes 626696 | tf_op jit(solution)/shard_map/ppermute | solution.py:43
  101.1 12.3 %collective-permute-start.15 = (bf16[136,768]{1,0:T(8,128)(2,1)}, bf16[136,768]{1,0:T(8,128)(2,1)}, u32[]{:S(2)}, u32[]{:S(2)}) collective-permute-start(bf16[136,768]{1,0:T(8,128)(2,1)} %get-tuple-element.72.b0), channel_id=1, source_target_pairs={{0,2},{1,3},{2,4},{3,5},{4,6},{5,7},{6,0},{7,1},{8,10},{9,11},{10,... | collective-permute-start | bytes 626696 | tf_op jit(solution)/shard_map/ppermute | solution.py:43
  101.6 12.3 %collective-permute-start.17 = (bf16[136,768]{1,0:T(8,128)(2,1)}, bf16[136,768]{1,0:T(8,128)(2,1)}, u32[]{:S(2)}, u32[]{:S(2)}) collective-permute-start(bf16[136,768]{1,0:T(8,128)(2,1)} %get-tuple-element.72.b0), channel_id=1, source_target_pairs={{0,6},{1,7},{2,0},{3,1},{4,2},{5,3},{6,4},{7,5},{8,14},{9,15},{10,... | collective-permute-start | bytes 626696 | tf_op jit(solution)/shard_map/ppermute | solution.py:43
  103.8 15.0 %all-to-all-start.2 = ((bf16[16,8,1536]{2,1,0:T(8,128)(2,1)}), bf16[16,8,1536]{2,1,0:T(8,128)(2,1)}, u32[]{:S(2)}, u32[]{:S(2)}) async-start(bf16[16,8,1536]{2,1,0:T(8,128)(2,1)} %bitcast.16), calls=%async_computation.2 | async-start | bytes 786432 | tf_op jit(solution)/shard_map/all_to_all | solution.py:430
  108.0 5.9 %collective-permute-start.12 = (bf16[136,768]{1,0:T(8,128)(2,1)}, bf16[136,768]{1,0:T(8,128)(2,1)S(1)}, u32[]{:S(2)}, u32[]{:S(2)}) collective-permute-start(bf16[136,768]{1,0:T(8,128)(2,1)} %get-tuple-element.72.b0), channel_id=1, source_target_pairs={{0,1},{1,0},{2,3},{3,2},{4,5},{5,4},{6,7},{7,6},{8,9},{9,8},{10,11... | collective-permute-start | bytes 626696 | tf_op jit(solution)/shard_map/ppermute | solution.py:43
  109.4 4.6 %collective-permute-start.14 = (bf16[136,768]{1,0:T(8,128)(2,1)}, bf16[136,768]{1,0:T(8,128)(2,1)S(1)}, u32[]{:S(2)}, u32[]{:S(2)}) collective-permute-start(bf16[136,768]{1,0:T(8,128)(2,1)} %collective-permute-done.13.b2), channel_id=1, source_target_pairs={{0,1},{1,0},{2,3},{3,2},{4,5},{5,4},{6,7},{7,6},{8,9},{9,8},{10,11... | collective-permute-start | bytes 626696 | tf_op jit(solution)/shard_map/ppermute | solution.py:43
  113.4 1.8 %collective-permute-start.16 = (bf16[136,768]{1,0:T(8,128)(2,1)}, bf16[136,768]{1,0:T(8,128)(2,1)S(1)}, u32[]{:S(2)}, u32[]{:S(2)}) collective-permute-start(bf16[136,768]{1,0:T(8,128)(2,1)} %collective-permute-done.15.b4), channel_id=1, source_target_pairs={{0,1},{1,0},{2,3},{3,2},{4,5},{5,4},{6,7},{7,6},{8,9},{9,8},{10,11... | collective-permute-start | bytes 626696 | tf_op jit(solution)/shard_map/ppermute | solution.py:43
  113.9 1.7 %collective-permute-start.18 = (bf16[136,768]{1,0:T(8,128)(2,1)}, bf16[136,768]{1,0:T(8,128)(2,1)S(1)}, u32[]{:S(2)}, u32[]{:S(2)}) collective-permute-start(bf16[136,768]{1,0:T(8,128)(2,1)} %collective-permute-done.17.b6), channel_id=1, source_target_pairs={{0,1},{1,0},{2,3},{3,2},{4,5},{5,4},{6,7},{7,6},{8,9},{9,8},{10,11... | collective-permute-start | bytes 626696 | tf_op jit(solution)/shard_map/ppermute | solution.py:43
  122.9 12.3 %all-to-all-start.3 = ((f32[8,8,896]{2,1,0:T(8,128)}), f32[8,8,896]{2,1,0:T(8,128)}, u32[]{:S(2)}, u32[]{:S(2)}) async-start(f32[8,8,896]{2,1,0:T(8,128)} %bitcast.15), calls=%async_computation.3 | async-start | bytes 458752 | tf_op jit(solution)/shard_map/all_to_all | solution.py:439
  (15 other events, 52.6 us)

commit v7 on v6

--- a/solution.py
+++ b/solution.py
@@ -222,6 +222,17 @@
     fields_ref[...] = table.T.astype(BF16)
 
 
+def sine_of(v):
+    n = jnp.floor(v * (1.0 / jnp.pi) + 0.5)
+    r = ((v - n * 3.140625) - n * 0.0009676218032836914) - n * 3.178650954705639e-08
+    square = r * r
+    series = jnp.full_like(v, -1.0 / 39916800.0)
+    for term in (1.0 / 362880.0, -1.0 / 5040.0, 1.0 / 120.0, -1.0 / 6.0):
+        series = series * square + term
+    value = r + r * square * series
+    return jnp.where(n - 2.0 * jnp.floor(0.5 * n) == 0.0, value, -value)
+
+
 def slide_rows(payload_ref, frequency_ref):
     sent = payload_ref[:, D:]
     row = lax.broadcasted_iota(I32, (ROWS, 2 * ROWS), 0) + 1
@@ -231,7 +242,7 @@
     lane = lax.broadcasted_iota(I32, (ROWS, D), 1)
     sine = (lane < D // 4) | ((lane >= D // 2) & (lane < 3 * D // 4))
     angle = jnp.where(lane < D // 2, along[0], along[1]) * frequency_ref[...]
-    return dot(place, payload_ref[:, :D]) + jnp.sin(angle + jnp.where(sine, 0.0, jnp.pi / 2))
+    return dot(place, payload_ref[:, :D]) + sine_of(angle + jnp.where(sine, 0.0, jnp.pi / 2))
 
 
 def load_all(sources, targets, sems):

time: 140 us -> 139 us (level)
  transfers between devices with their start and end apart: 22 -> 22, of which waited for: 7 -> 7; matrix products, arithmetic and copies ran while one was open for 1% -> 1% of each run, Pallas kernels for 11% -> 12%
where the time goes in v7:
time: 139 us; the launch traced here: 138 us
  starting transfers between devices  42.6 us (31%)
  waiting for transfers between devices  33.1 us (24%)
  Pallas kernels  29.4 us (21%)
  blocking collectives  22 us (16%)
  local copies, waits for them, and re-layouts  10.4 us (7%)
    ppermute x19, starting transfers between devices, shift(): return lax.ppermute(value, AXES, pairs)  29.8 us
    pallas_call x14, Pallas kernels, call(): pl.pallas_call(kernel, out_shape=outs, in_specs=spaces or [VMEM] * len(ar...  29.4 us
    all_to_all x1, blocking collectives, body(): lax.all_to_all(payload, AXES, split_axis=1, concat_axis=1, tiled=True)  22 us
    ppermute x19, waiting for transfers between devices, shift(): return lax.ppermute(value, AXES, pairs)  21.6 us
    all_to_all x1, waiting for transfers between devices, along_y(): lax.all_to_all(value, 'tile', split_axis=0, concat_axis=0, axis_index_gro...  11.4 us
    unnamed x50, local copies, waits for them, and re-layouts  8.41 us
    all_to_all x1, starting transfers between devices, along_y(): lax.all_to_all(value, 'tile', split_axis=0, concat_axis=0, axis_index_gro...  4.31 us
    all_to_all x1, starting transfers between devices, body(): lax.all_to_all(far_parts, 'seq', split_axis=0, concat_axis=0, tiled=True)  4.23 us
  transfers between devices with their start and end apart: 22, of which 7 were waited for; matrix products, arithmetic and copies ran while one was open for 1% of the time, Pallas kernels for 12%

profile of v7, /device:TPU:1, one launch (start us, length us, event | category | flops | bytes accessed | tf_op | source)
XLA Modules:
  0.0 137.9 jit_solution(5380968390337682611)
XLA Ops:
  0.0 2.4 %shard_map.136 = (bf16[2304,256]{1,0:T(8,128)(2,1)}, bf16[576,256]{1,0:T(8,128)(2,1)}) custom-call(bf16[1536,256]{1,0:T(8,128)(2,1)} %gate_ref.3, bf16[1536,256]{1,0:T(8,128)(2,1)} %up_ref.3, bf16[256,1536]{1,0:T(8,128)(2,1)} %down_ref.3), custom_call_target="tpu_custom_call" | custom-call | flops 1024 | bytes 3833856 | tf_op jit(solution)/shard_map/pallas_call | solution.py:54
  2.5 4.5 %collective-permute-start = (bf16[576,256]{1,0:T(8,128)(2,1)}, bf16[576,256]{1,0:T(8,128)(2,1)S(1)}, u32[]{:S(2)}, u32[]{:S(2)}) collective-permute-start(bf16[576,256]{1,0:T(8,128)(2,1)} %get-tuple-element.51), channel_id=1, source_target_pairs={{0,64},{1,65},{2,66},{3,67},{4,68},{5,69},{6,70},{7,71},{8,72},{9,... | collective-permute-start | bytes 884744 | tf_op jit(solution)/shard_map/ppermute | solution.py:43
  8.5 1.5 %shard_map.137 = bf16[512,1536]{1,0:T(8,128)(2,1)} custom-call(bf16[128,1536]{1,0:T(8,128)(2,1)S(1)} %copy-done.6, f32[1,1536]{1,0:T(1,128)S(1)} %broadcast_in_dim.22.gain_ref), custom_call_target="tpu_custom_call" | custom-call | flops 1024 | bytes 1972224 | tf_op jit(solution)/shard_map/pallas_call | solution.py:54
  10.0 4.3 %all-to-all-start = ((bf16[4,128,1536]{2,1,0:T(8,128)(2,1)}), bf16[4,128,1536]{2,1,0:T(8,128)(2,1)S(1)}, u32[]{:S(2)}, u32[]{:S(2)}) async-start(bf16[4,128,1536]{2,1,0:T(8,128)(2,1)} %bitcast), calls=%async_computation | async-start | bytes 3145728 | tf_op jit(solution)/shard_map/all_to_all | solution.py:48
  15.1 1.9 %collective-permute-start.6 = (bf16[2304,256]{1,0:T(8,128)(2,1)}, bf16[2304,256]{1,0:T(8,128)(2,1)}, u32[]{:S(2)}, u32[]{:S(2)}) collective-permute-start(bf16[2304,256]{1,0:T(8,128)(2,1)} %get-tuple-element.58), channel_id=1, source_target_pairs={{0,96},{1,97},{2,98},{3,99},{4,100},{5,101},{6,102},{7,103},{8,104... | collective-permute-start | bytes 3538952 | tf_op jit(solution)/shard_map/ppermute | solution.py:43
  17.0 2.7 %collective-permute-start.1 = (bf16[576,256]{1,0:T(8,128)(2,1)S(1)}, bf16[576,256]{1,0:T(8,128)(2,1)}, u32[]{:S(2)}, u32[]{:S(2)}) collective-permute-start(bf16[576,256]{1,0:T(8,128)(2,1)S(1)} %collective-permute-done.q0), channel_id=1, source_target_pairs={{0,4},{1,5},{2,6},{3,7},{4,0},{5,1},{6,2},{7,3},{8,12},{9,13},{10,... | collective-permute-start | bytes 884744 | tf_op jit(solution)/shard_map/ppermute | solution.py:43
  20.1 2.4 %collective-permute-start.3 = (bf16[576,256]{1,0:T(8,128)(2,1)S(1)}, bf16[576,256]{1,0:T(8,128)(2,1)}, u32[]{:S(2)}, u32[]{:S(2)}) collective-permute-start(bf16[576,256]{1,0:T(8,128)(2,1)S(1)} %collective-permute-done.q0), channel_id=1, source_target_pairs={{0,6},{1,7},{2,0},{3,1},{4,2},{5,3},{6,4},{7,5},{8,14},{9,15},{10,... | collective-permute-start | bytes 884744 | tf_op jit(solution)/shard_map/ppermute | solution.py:43
  22.4 11.4 %all-to-all-done = bf16[4,128,1536]{2,1,0:T(8,128)(2,1)S(1)} async-done(((bf16[4,128,1536]{2,1,0:T(8,128)(2,1)}), bf16[4,128,1536]{2,1,0:T(8,128)(2,1)S(1)}, u32[]{:S(2)}, u32[]{:S(2)}) %all-to-all-start) | async-done | bytes 1572896 | tf_op jit(solution)/shard_map/all_to_all | solution.py:48
  35.0 1.4 %shard_map.138.total_ref = f32[512,1536]{1,0:T(8,128)S(1)} custom-call(bf16[512,1536]{1,0:T(8,128)(2,1)S(1)} %bitcast.9, bf16[1536,256]{1,0:T(8,128)(2,1)S(1)} %copy-done.1, bf16[1536,256]{1,0:T(8,128)(2,1)S(1)} %copy-done.2, bf16[256,1536]{1,0:T(8,128)(2,1)S(1)} %copy-done.3), custom_call_target="tpu_custom_call" | custom-call | flops 1024 | bytes 7077888 | tf_op jit(solution)/shard_map/pallas_call | solution.py:54
  37.6 2.2 %collective-permute-start.4 = (bf16[2304,256]{1,0:T(8,128)(2,1)S(1)}, bf16[2304,256]{1,0:T(8,128)(2,1)S(1)}, u32[]{:S(2)}, u32[]{:S(2)}) collective-permute-start(bf16[2304,256]{1,0:T(8,128)(2,1)S(1)} %shard_map.139.a), channel_id=1, source_target_pairs={{0,1},{1,0},{2,3},{3,2},{4,5},{5,4},{6,7},{7,6},{8,9},{9,8},{10,11... | collective-permute-start | bytes 3538952 | tf_op jit(solution)/shard_map/ppermute | solution.py:43
  39.9 2.2 %collective-permute-done.5.a = bf16[2304,256]{1,0:T(8,128)(2,1)} collective-permute-done((bf16[2304,256]{1,0:T(8,128)(2,1)}, bf16[2304,256]{1,0:T(8,128)(2,1)}, u32[]{:S(2)}, u32[]{:S(2)}) %collective-permute-start.5) | collective-permute-done | bytes 1179680 | tf_op jit(solution)/shard_map/ppermute | solution.py:43
  42.1 2.2 %collective-permute-start.7 = (bf16[2304,256]{1,0:T(8,128)(2,1)}, bf16[2304,256]{1,0:T(8,128)(2,1)S(1)}, u32[]{:S(2)}, u32[]{:S(2)}) collective-permute-start(bf16[2304,256]{1,0:T(8,128)(2,1)} %collective-permute-done.5.a), channel_id=1, source_target_pairs={{0,1},{1,0},{2,3},{3,2},{4,5},{5,4},{6,7},{7,6},{8,9},{9,8},{10,11... | collective-permute-start | bytes 3538952 | tf_op jit(solution)/shard_map/ppermute | solution.py:43
  44.2 1.5 %shard_map.140.total_ref = f32[512,1536]{1,0:T(8,128)S(1)} custom-call(bf16[512,1536]{1,0:T(8,128)(2,1)S(1)} %bitcast.10, f32[512,1536]{1,0:T(8,128)S(1)} %shard_map.138.total_ref, bf16[2304,256]{1,0:T(8,128)(2,1)S(1)} %shard_map.139.a, bf16[2304,256]{1,0:T(8,128)(2,1)S(1)} %collective-permute-done.4.b), custom_call_target="tpu_custom_call" | custom-call | flops 1024 | bytes 10223616 | tf_op jit(solution)/shard_map/pallas_call | solution.py:54
  45.7 3.1 %shard_map.141.total_ref = f32[512,1536]{1,0:T(8,128)S(1)} custom-call(bf16[512,1536]{1,0:T(8,128)(2,1)S(1)} %bitcast.11, f32[512,1536]{1,0:T(8,128)S(1)} %shard_map.140.total_ref, bf16[2304,256]{1,0:T(8,128)(2,1)} %collective-permute-done.5.a, bf16[2304,256]{1,0:T(8,128)(2,1)} %collective-permute-done.6.b), custom_call_target="tpu_custom_call" | custom-call | flops 1024 | bytes 10223616 | tf_op jit(solution)/shard_map/pallas_call | solution.py:54
  48.9 1.8 %shard_map.142 = (f32[128,1536]{1,0:T(8,128)S(1)}, bf16[128,1536]{1,0:T(8,128)(2,1)S(1)}, bf16[128,1536]{1,0:T(8,128)(2,1)S(1)}, bf16[128,1536]{1,0:T(8,128)(2,1)S(1)}) custom-call(bf16[512,1536]{1,0:T(8,128)(2,1)S(1)} %bitcast.12, f32[512,1536]{1,0:T(8,128)S(1)} %shard_map.141.total_ref, bf16[2304,256]{1,0:T(8,128)(2,1)S(1)} %collective-permute-done.7.a, ...), custom_call_target="tpu_custom_call" | custom-call | flops 1024 | bytes 9043968 | tf_op jit(solution)/shard_map/pallas_call | solution.py:54
  50.7 3.0 %collective-permute-start.10 = (bf16[128,1536]{1,0:T(8,128)(2,1)S(1)}, bf16[128,1536]{1,0:T(8,128)(2,1)S(1)}, u32[]{:S(2)}, u32[]{:S(2)}) collective-permute-start(bf16[128,1536]{1,0:T(8,128)(2,1)S(1)} %get-tuple-element.62), channel_id=1, source_target_pairs={{0,16},{1,17},{2,18},{3,19},{4,20},{5,21},{6,22},{7,23},{8,24},{9,... | collective-permute-start | bytes 1179656 | tf_op jit(solution)/shard_map/ppermute | solution.py:43
  54.0 2.4 %collective-permute-start.9 = (bf16[128,1536]{1,0:T(8,128)(2,1)S(1)}, bf16[128,1536]{1,0:T(8,128)(2,1)S(1)}, u32[]{:S(2)}, u32[]{:S(2)}) collective-permute-start(bf16[128,1536]{1,0:T(8,128)(2,1)S(1)} %get-tuple-element.61), channel_id=1, source_target_pairs={{0,24},{1,25},{2,26},{3,27},{4,28},{5,29},{6,30},{7,31},{8,0},{9,1... | collective-permute-start | bytes 1179656 | tf_op jit(solution)/shard_map/ppermute | solution.py:43
  56.5 6.0 %collective-permute-done.10.b = bf16[128,1536]{1,0:T(8,128)(2,1)S(1)} collective-permute-done((bf16[128,1536]{1,0:T(8,128)(2,1)S(1)}, bf16[128,1536]{1,0:T(8,128)(2,1)S(1)}, u32[]{:S(2)}, u32[]{:S(2)}) %collective-permute-start.10) | collective-permute-done | bytes 393248 | tf_op jit(solution)/shard_map/ppermute | solution.py:43
  62.5 9.2 %collective-permute-done.11.c = bf16[128,1536]{1,0:T(8,128)(2,1)S(1)} collective-permute-done((bf16[128,1536]{1,0:T(8,128)(2,1)S(1)}, bf16[128,1536]{1,0:T(8,128)(2,1)S(1)}, u32[]{:S(2)}, u32[]{:S(2)}) %collective-permute-start.11) | collective-permute-done | bytes 393248 | tf_op jit(solution)/shard_map/ppermute | solution.py:43
  73.5 22.0 %all_to_all.38 = bf16[2,128,896]{2,0,1:T(2,128)(2,1)S(1)} all-to-all(bf16[2,128,896]{2,0,1:T(2,128)(2,1)S(1)} %copy.15), channel_id=1, replica_groups=mesh['tile'=16,'seq'=8] {'tile','seq'}, dimensions={1} | all-to-all | bytes 917504 | tf_op jit(solution)/shard_map/all_to_all | solution.py:430
  95.5 2.1 %shard_map.145 = (bf16[136,768]{1,0:T(8,128)(2,1)}, bf16[128,1536]{1,0:T(8,128)(2,1)S(1)}, f32[128,768]{1,0:T(8,128)S(1)}) custom-call(bf16[256,896]{1,0:T(8,128)(2,1)S(1)} %bitcast.14, f32[1,768]{1,0:T(1,128)S(1)} %copy-done.17, f32[1,768]{1,0:T(1,128)S(1)} %broadcast_in_dim.21.gain_ref, bf16[768,2304]{1,0:T(8,128)(2,1)S(1)} %copy-done, ...), custom_call_target="tpu_custom_call" | custom-call | flops 1024 | bytes 5002240 | tf_op jit(solution)/shard_map/pallas_call | solution.py:54
  100.7 2.2 %collective-permute-start.17 = (bf16[136,768]{1,0:T(8,128)(2,1)}, bf16[136,768]{1,0:T(8,128)(2,1)}, u32[]{:S(2)}, u32[]{:S(2)}) collective-permute-start(bf16[136,768]{1,0:T(8,128)(2,1)} %get-tuple-element.72.b0), channel_id=1, source_target_pairs={{0,6},{1,7},{2,0},{3,1},{4,2},{5,3},{6,4},{7,5},{8,14},{9,15},{10,... | collective-permute-start | bytes 626696 | tf_op jit(solution)/shard_map/ppermute | solution.py:43
  102.9 4.2 %all-to-all-start.2 = ((bf16[16,8,1536]{2,1,0:T(8,128)(2,1)}), bf16[16,8,1536]{2,1,0:T(8,128)(2,1)}, u32[]{:S(2)}, u32[]{:S(2)}) async-start(bf16[16,8,1536]{2,1,0:T(8,128)(2,1)} %bitcast.16), calls=%async_computation.2 | async-start | bytes 786432 | tf_op jit(solution)/shard_map/all_to_all | solution.py:441
  107.1 1.3 collective-permute-start.12
  108.4 1.5 %collective-permute-start.14 = (bf16[136,768]{1,0:T(8,128)(2,1)}, bf16[136,768]{1,0:T(8,128)(2,1)S(1)}, u32[]{:S(2)}, u32[]{:S(2)}) collective-permute-start(bf16[136,768]{1,0:T(8,128)(2,1)} %collective-permute-done.13.b2), channel_id=1, source_target_pairs={{0,1},{1,0},{2,3},{3,2},{4,5},{5,4},{6,7},{7,6},{8,9},{9,8},{10,11... | collective-permute-start | bytes 626696 | tf_op jit(solution)/shard_map/ppermute | solution.py:43
  109.9 2.6 %collective-permute-done.15.b4 = bf16[136,768]{1,0:T(8,128)(2,1)} collective-permute-done((bf16[136,768]{1,0:T(8,128)(2,1)}, bf16[136,768]{1,0:T(8,128)(2,1)}, u32[]{:S(2)}, u32[]{:S(2)}) %collective-permute-start.15) | collective-permute-done | bytes 208928 | tf_op jit(solution)/shard_map/ppermute | solution.py:43
  114.7 1.3 shard_map.146
  118.7 2.6 %shard_map.148 = f32[64,896]{1,0:T(8,128)S(1)} custom-call(bf16[64,768]{1,0:T(8,128)(2,1)S(1)} %copy-done.14, bf16[128,1536]{1,0:T(8,128)(2,1)} %bitcast.6.kv_ref), custom_call_target="tpu_custom_call" | custom-call | flops 1024 | bytes 720896 | tf_op jit(solution)/shard_map/pallas_call | solution.py:54
  122.0 4.2 %all-to-all-start.3 = ((f32[8,8,896]{2,1,0:T(8,128)}), f32[8,8,896]{2,1,0:T(8,128)}, u32[]{:S(2)}, u32[]{:S(2)}) async-start(f32[8,8,896]{2,1,0:T(8,128)} %bitcast.15), calls=%async_computation.3 | async-start | bytes 458752 | tf_op jit(solution)/shard_map/all_to_all | solution.py:450
  126.2 1.4 %copy-done.9 = bf16[1024,768]{1,0:T(8,128)(2,1)S(1)} copy-done((bf16[1024,768]{1,0:T(8,128)(2,1)S(1)}, bf16[1024,768]{1,0:T(8,128)(2,1)}, u32[]{:S(2)}) %copy-start.9) | copy-done | bytes 1572888
  127.6 5.7 %shard_map.147.near = f32[6,128,256]{2,1,0:T(8,128)S(1)} custom-call(bf16[1024,768]{1,0:T(8,128)(2,1)S(1)} %copy-done.9, bf16[768,2304]{1,0:T(8,128)(2,1)S(1)} %copy-done), custom_call_target="tpu_custom_call" | custom-call | flops 1024 | bytes 5898240 | tf_op jit(solution)/shard_map/pallas_call | solution.py:54
  134.3 3.5 %shard_map.149 = bf16[128,768]{1,0:T(8,128)(2,1)} custom-call(f32[6,128,256]{2,1,0:T(8,128)} %copy-done.4, f32[64,896]{1,0:T(8,128)} %bitcast.8.far, f32[128,768]{1,0:T(8,128)} %copy-done.12, s32[1,768]{1,0:T(1,128)} %copy-done.15, bf16[768,768]{1,0:T(8,128)(2,1)} %w.1), custom_call_target="tpu_custom_call" | custom-call | flops 1024 | bytes 2788352 | tf_op jit(solution)/shard_map/pallas_call | solution.py:54
  (88 shorter events, 16.6 us)
Async XLA Ops:
  0.0 7.8 %copy-start.23 = (f32[768]{0:T(1024)S(1)}, f32[768]{0:T(1024)}, u32[]{:S(2)}) copy-start(f32[768]{0:T(1024)} %param.24) | copy-start | bytes 9220
  0.0 8.5 %copy-start.6 = (bf16[128,1536]{1,0:T(8,128)(2,1)S(1)}, bf16[128,1536]{1,0:T(8,128)(2,1)}, u32[]{:S(2)}) copy-start(bf16[128,1536]{1,0:T(8,128)(2,1)} %tokens_ref) | copy-start | bytes 1179652
  2.5 11.8 %collective-permute-start = (bf16[576,256]{1,0:T(8,128)(2,1)}, bf16[576,256]{1,0:T(8,128)(2,1)S(1)}, u32[]{:S(2)}, u32[]{:S(2)}) collective-permute-start(bf16[576,256]{1,0:T(8,128)(2,1)} %get-tuple-element.51), channel_id=1, source_target_pairs={{0,64},{1,65},{2,66},{3,67},{4,68},{5,69},{6,70},{7,71},{8,72},{9,... | collective-permute-start | bytes 884744 | tf_op jit(solution)/shard_map/ppermute | solution.py:43
  7.2 88.3 %copy-start.15 = (s32[1,768]{1,0:T(1,128)}, s32[1,768]{1,0:T(1,128)S(1)}, u32[]{:S(2)}) copy-start(s32[1,768]{1,0:T(1,128)S(1)} %broadcast_in_dim_reshape.3.offsets_ref) | copy-start | bytes 9220
  10.0 23.8 %copy-start.1 = (bf16[1536,256]{1,0:T(8,128)(2,1)S(1)}, bf16[1536,256]{1,0:T(8,128)(2,1)}, u32[]{:S(2)}) copy-start(bf16[1536,256]{1,0:T(8,128)(2,1)} %gate_ref.3) | copy-start | bytes 2359300
  10.0 23.8 %copy-start.2 = (bf16[1536,256]{1,0:T(8,128)(2,1)S(1)}, bf16[1536,256]{1,0:T(8,128)(2,1)}, u32[]{:S(2)}) copy-start(bf16[1536,256]{1,0:T(8,128)(2,1)} %up_ref.3) | copy-start | bytes 2359300
  10.0 23.8 %all-to-all-start = ((bf16[4,128,1536]{2,1,0:T(8,128)(2,1)}), bf16[4,128,1536]{2,1,0:T(8,128)(2,1)S(1)}, u32[]{:S(2)}, u32[]{:S(2)}) async-start(bf16[4,128,1536]{2,1,0:T(8,128)(2,1)} %bitcast), calls=%async_computation | async-start | bytes 3145728 | tf_op jit(solution)/shard_map/all_to_all | solution.py:48
  14.3 27.7 %collective-permute-start.5 = (bf16[2304,256]{1,0:T(8,128)(2,1)}, bf16[2304,256]{1,0:T(8,128)(2,1)}, u32[]{:S(2)}, u32[]{:S(2)}) collective-permute-start(bf16[2304,256]{1,0:T(8,128)(2,1)} %get-tuple-element.58), channel_id=1, source_target_pairs={{0,32},{1,33},{2,34},{3,35},{4,36},{5,37},{6,38},{7,39},{8,40},{9,... | collective-permute-start | bytes 3538952 | tf_op jit(solution)/shard_map/ppermute | solution.py:43
  15.1 29.2 %collective-permute-start.6 = (bf16[2304,256]{1,0:T(8,128)(2,1)}, bf16[2304,256]{1,0:T(8,128)(2,1)}, u32[]{:S(2)}, u32[]{:S(2)}) collective-permute-start(bf16[2304,256]{1,0:T(8,128)(2,1)} %get-tuple-element.58), channel_id=1, source_target_pairs={{0,96},{1,97},{2,98},{3,99},{4,100},{5,101},{6,102},{7,103},{8,104... | collective-permute-start | bytes 3538952 | tf_op jit(solution)/shard_map/ppermute | solution.py:43
  17.0 19.4 %collective-permute-start.1 = (bf16[576,256]{1,0:T(8,128)(2,1)S(1)}, bf16[576,256]{1,0:T(8,128)(2,1)}, u32[]{:S(2)}, u32[]{:S(2)}) collective-permute-start(bf16[576,256]{1,0:T(8,128)(2,1)S(1)} %collective-permute-done.q0), channel_id=1, source_target_pairs={{0,4},{1,5},{2,6},{3,7},{4,0},{5,1},{6,2},{7,3},{8,12},{9,13},{10,... | collective-permute-start | bytes 884744 | tf_op jit(solution)/shard_map/ppermute | solution.py:43
  19.7 16.6 %collective-permute-start.2 = (bf16[576,256]{1,0:T(8,128)(2,1)S(1)}, bf16[576,256]{1,0:T(8,128)(2,1)}, u32[]{:S(2)}, u32[]{:S(2)}) collective-permute-start(bf16[576,256]{1,0:T(8,128)(2,1)S(1)} %collective-permute-done.q0), channel_id=1, source_target_pairs={{0,2},{1,3},{2,4},{3,5},{4,6},{5,7},{6,0},{7,1},{8,10},{9,11},{10,... | collective-permute-start | bytes 884744 | tf_op jit(solution)/shard_map/ppermute | solution.py:43
  20.1 16.3 %collective-permute-start.3 = (bf16[576,256]{1,0:T(8,128)(2,1)S(1)}, bf16[576,256]{1,0:T(8,128)(2,1)}, u32[]{:S(2)}, u32[]{:S(2)}) collective-permute-start(bf16[576,256]{1,0:T(8,128)(2,1)S(1)} %collective-permute-done.q0), channel_id=1, source_target_pairs={{0,6},{1,7},{2,0},{3,1},{4,2},{5,3},{6,4},{7,5},{8,14},{9,15},{10,... | collective-permute-start | bytes 884744 | tf_op jit(solution)/shard_map/ppermute | solution.py:43
  37.6 6.6 %collective-permute-start.4 = (bf16[2304,256]{1,0:T(8,128)(2,1)S(1)}, bf16[2304,256]{1,0:T(8,128)(2,1)S(1)}, u32[]{:S(2)}, u32[]{:S(2)}) collective-permute-start(bf16[2304,256]{1,0:T(8,128)(2,1)S(1)} %shard_map.139.a), channel_id=1, source_target_pairs={{0,1},{1,0},{2,3},{3,2},{4,5},{5,4},{6,7},{7,6},{8,9},{9,8},{10,11... | collective-permute-start | bytes 3538952 | tf_op jit(solution)/shard_map/ppermute | solution.py:43
  42.1 6.8 %collective-permute-start.7 = (bf16[2304,256]{1,0:T(8,128)(2,1)}, bf16[2304,256]{1,0:T(8,128)(2,1)S(1)}, u32[]{:S(2)}, u32[]{:S(2)}) collective-permute-start(bf16[2304,256]{1,0:T(8,128)(2,1)} %collective-permute-done.5.a), channel_id=1, source_target_pairs={{0,1},{1,0},{2,3},{3,2},{4,5},{5,4},{6,7},{7,6},{8,9},{9,8},{10,11... | collective-permute-start | bytes 3538952 | tf_op jit(solution)/shard_map/ppermute | solution.py:43
  44.2 4.7 %collective-permute-start.8 = (bf16[2304,256]{1,0:T(8,128)(2,1)}, bf16[2304,256]{1,0:T(8,128)(2,1)S(1)}, u32[]{:S(2)}, u32[]{:S(2)}) collective-permute-start(bf16[2304,256]{1,0:T(8,128)(2,1)} %collective-permute-done.6.b), channel_id=1, source_target_pairs={{0,1},{1,0},{2,3},{3,2},{4,5},{5,4},{6,7},{7,6},{8,9},{9,8},{10,11... | collective-permute-start | bytes 3538952 | tf_op jit(solution)/shard_map/ppermute | solution.py:43
  48.8 22.9 %copy-start.7 = (bf16[128,1536]{1,0:T(8,128)(2,1)S(1)}, bf16[128,1536]{1,0:T(8,128)(2,1)}, u32[]{:S(2)}) copy-start(bf16[128,1536]{1,0:T(8,128)(2,1)} %tokens_ref) | copy-start | bytes 1179652
  48.9 22.9 %copy-start.16 = (f32[1,1536]{1,0:T(1,128)S(1)}, f32[1,1536]{1,0:T(1,128)}, u32[]{:S(2)}) copy-start(f32[1,1536]{1,0:T(1,128)} %broadcast_in_dim.20.gain_ref) | copy-start | bytes 18436
  48.9 22.9 %copy-start.5 = (bf16[1536,768]{1,0:T(8,128)(2,1)S(1)}, bf16[1536,768]{1,0:T(8,128)(2,1)}, u32[]{:S(2)}) copy-start(bf16[1536,768]{1,0:T(8,128)(2,1)} %w_ref.3) | copy-start | bytes 7077892
  50.7 11.8 %collective-permute-start.10 = (bf16[128,1536]{1,0:T(8,128)(2,1)S(1)}, bf16[128,1536]{1,0:T(8,128)(2,1)S(1)}, u32[]{:S(2)}, u32[]{:S(2)}) collective-permute-start(bf16[128,1536]{1,0:T(8,128)(2,1)S(1)} %get-tuple-element.62), channel_id=1, source_target_pairs={{0,16},{1,17},{2,18},{3,19},{4,20},{5,21},{6,22},{7,23},{8,24},{9,... | collective-permute-start | bytes 1179656 | tf_op jit(solution)/shard_map/ppermute | solution.py:43
  53.7 18.0 %collective-permute-start.11 = (bf16[128,1536]{1,0:T(8,128)(2,1)S(1)}, bf16[128,1536]{1,0:T(8,128)(2,1)S(1)}, u32[]{:S(2)}, u32[]{:S(2)}) collective-permute-start(bf16[128,1536]{1,0:T(8,128)(2,1)S(1)} %get-tuple-element.63), channel_id=1, source_target_pairs={{0,8},{1,9},{2,10},{3,11},{4,12},{5,13},{6,14},{7,15},{8,16},{9,17... | collective-permute-start | bytes 1179656 | tf_op jit(solution)/shard_map/ppermute | solution.py:43
  54.0 17.7 %collective-permute-start.9 = (bf16[128,1536]{1,0:T(8,128)(2,1)S(1)}, bf16[128,1536]{1,0:T(8,128)(2,1)S(1)}, u32[]{:S(2)}, u32[]{:S(2)}) collective-permute-start(bf16[128,1536]{1,0:T(8,128)(2,1)S(1)} %get-tuple-element.61), channel_id=1, source_target_pairs={{0,24},{1,25},{2,26},{3,27},{4,28},{5,29},{6,30},{7,31},{8,0},{9,1... | collective-permute-start | bytes 1179656 | tf_op jit(solution)/shard_map/ppermute | solution.py:43
  71.8 23.8 %copy-start = (bf16[768,2304]{1,0:T(8,128)(2,1)S(1)}, bf16[768,2304]{1,0:T(8,128)(2,1)}, u32[]{:S(2)}) copy-start(bf16[768,2304]{1,0:T(8,128)(2,1)} %w_ref.5) | copy-start | bytes 10616836
  73.0 22.5 %copy-start.17 = (f32[1,768]{1,0:T(1,128)S(1)}, f32[1,768]{1,0:T(1,128)}, u32[]{:S(2)}) copy-start(f32[1,768]{1,0:T(1,128)} %broadcast_in_dim_tile.3.frequency_ref) | copy-start | bytes 9220
  99.1 9.3 %collective-permute-start.13 = (bf16[136,768]{1,0:T(8,128)(2,1)}, bf16[136,768]{1,0:T(8,128)(2,1)}, u32[]{:S(2)}, u32[]{:S(2)}) collective-permute-start(bf16[136,768]{1,0:T(8,128)(2,1)} %get-tuple-element.72.b0), channel_id=1, source_target_pairs={{0,4},{1,5},{2,6},{3,7},{4,0},{5,1},{6,2},{7,3},{8,12},{9,13},{10,... | collective-permute-start | bytes 626696 | tf_op jit(solution)/shard_map/ppermute | solution.py:43
  100.2 12.3 %collective-permute-start.15 = (bf16[136,768]{1,0:T(8,128)(2,1)}, bf16[136,768]{1,0:T(8,128)(2,1)}, u32[]{:S(2)}, u32[]{:S(2)}) collective-permute-start(bf16[136,768]{1,0:T(8,128)(2,1)} %get-tuple-element.72.b0), channel_id=1, source_target_pairs={{0,2},{1,3},{2,4},{3,5},{4,6},{5,7},{6,0},{7,1},{8,10},{9,11},{10,... | collective-permute-start | bytes 626696 | tf_op jit(solution)/shard_map/ppermute | solution.py:43
  100.7 12.3 %collective-permute-start.17 = (bf16[136,768]{1,0:T(8,128)(2,1)}, bf16[136,768]{1,0:T(8,128)(2,1)}, u32[]{:S(2)}, u32[]{:S(2)}) collective-permute-start(bf16[136,768]{1,0:T(8,128)(2,1)} %get-tuple-element.72.b0), channel_id=1, source_target_pairs={{0,6},{1,7},{2,0},{3,1},{4,2},{5,3},{6,4},{7,5},{8,14},{9,15},{10,... | collective-permute-start | bytes 626696 | tf_op jit(solution)/shard_map/ppermute | solution.py:43
  102.9 15.0 %all-to-all-start.2 = ((bf16[16,8,1536]{2,1,0:T(8,128)(2,1)}), bf16[16,8,1536]{2,1,0:T(8,128)(2,1)}, u32[]{:S(2)}, u32[]{:S(2)}) async-start(bf16[16,8,1536]{2,1,0:T(8,128)(2,1)} %bitcast.16), calls=%async_computation.2 | async-start | bytes 786432 | tf_op jit(solution)/shard_map/all_to_all | solution.py:441
  107.1 5.9 %collective-permute-start.12 = (bf16[136,768]{1,0:T(8,128)(2,1)}, bf16[136,768]{1,0:T(8,128)(2,1)S(1)}, u32[]{:S(2)}, u32[]{:S(2)}) collective-permute-start(bf16[136,768]{1,0:T(8,128)(2,1)} %get-tuple-element.72.b0), channel_id=1, source_target_pairs={{0,1},{1,0},{2,3},{3,2},{4,5},{5,4},{6,7},{7,6},{8,9},{9,8},{10,11... | collective-permute-start | bytes 626696 | tf_op jit(solution)/shard_map/ppermute | solution.py:43
  108.4 4.6 %collective-permute-start.14 = (bf16[136,768]{1,0:T(8,128)(2,1)}, bf16[136,768]{1,0:T(8,128)(2,1)S(1)}, u32[]{:S(2)}, u32[]{:S(2)}) collective-permute-start(bf16[136,768]{1,0:T(8,128)(2,1)} %collective-permute-done.13.b2), channel_id=1, source_target_pairs={{0,1},{1,0},{2,3},{3,2},{4,5},{5,4},{6,7},{7,6},{8,9},{9,8},{10,11... | collective-permute-start | bytes 626696 | tf_op jit(solution)/shard_map/ppermute | solution.py:43
  112.5 1.8 %collective-permute-start.16 = (bf16[136,768]{1,0:T(8,128)(2,1)}, bf16[136,768]{1,0:T(8,128)(2,1)S(1)}, u32[]{:S(2)}, u32[]{:S(2)}) collective-permute-start(bf16[136,768]{1,0:T(8,128)(2,1)} %collective-permute-done.15.b4), channel_id=1, source_target_pairs={{0,1},{1,0},{2,3},{3,2},{4,5},{5,4},{6,7},{7,6},{8,9},{9,8},{10,11... | collective-permute-start | bytes 626696 | tf_op jit(solution)/shard_map/ppermute | solution.py:43
  113.0 1.7 %collective-permute-start.18 = (bf16[136,768]{1,0:T(8,128)(2,1)}, bf16[136,768]{1,0:T(8,128)(2,1)S(1)}, u32[]{:S(2)}, u32[]{:S(2)}) collective-permute-start(bf16[136,768]{1,0:T(8,128)(2,1)} %collective-permute-done.17.b6), channel_id=1, source_target_pairs={{0,1},{1,0},{2,3},{3,2},{4,5},{5,4},{6,7},{7,6},{8,9},{9,8},{10,11... | collective-permute-start | bytes 626696 | tf_op jit(solution)/shard_map/ppermute | solution.py:43
  122.0 12.3 %all-to-all-start.3 = ((f32[8,8,896]{2,1,0:T(8,128)}), f32[8,8,896]{2,1,0:T(8,128)}, u32[]{:S(2)}, u32[]{:S(2)}) async-start(f32[8,8,896]{2,1,0:T(8,128)} %bitcast.15), calls=%async_computation.3 | async-start | bytes 458752 | tf_op jit(solution)/shard_map/all_to_all | solution.py:450
  (15 other events, 52.6 us)

commit v8 on v7

--- a/solution.py
+++ b/solution.py
@@ -127,8 +127,8 @@
             down_ref[128 * n : 128 * (n + 1), 256 * j : 256 * (j + 1)] = chunk[block, :]
 
 
-def mlp_middle_kernel(rows_ref, total_ref, a, b, out_ref, hidden_ref, down_ref):
-    mlp_chunks(rows_ref, (a, b), hidden_ref, down_ref)
+def mlp_middle_kernel(rows_ref, total_ref, a, b, c, d, out_ref, hidden_ref, down_ref):
+    mlp_chunks(rows_ref, (a, b, c, d), hidden_ref, down_ref)
     for j in range(3):
         cols = slice(512 * j, 512 * (j + 1))
         out_ref[:, cols] = total_ref[:, cols] + dot(hidden_ref[...], down_ref[:, cols])
@@ -182,11 +182,10 @@
         mlp_middle_kernel,
         [((RING * ROWS, D_VIT), F32)],
         rows,
-        scratch=[pltpu.VMEM((RING * ROWS, 256), BF16), pltpu.VMEM((256, D_VIT), BF16)],
+        scratch=[pltpu.VMEM((RING * ROWS, 512), BF16), pltpu.VMEM((512, D_VIT), BF16)],
         vmem=20,
     )
-    (total,) = middle(total, across, swap(across))
-    (total,) = middle(total, before, after)
+    (total,) = middle(total, across, swap(across), before, after)
     return call(
         mlp_last_kernel,
         [((ROWS, D_VIT), t) for t in (F32, BF16, BF16, BF16)],

time: 139 us -> 138 us (level)
    pallas_call x14 -> x13, Pallas kernels: 29.4 us -> 29.1 us  [call(): pl.pallas_call(kernel, out_shape=outs, in_specs=spaces or [VMEM] * len(ar...]
  transfers between devices with their start and end apart: 22 -> 22, of which waited for: 7 -> 7; matrix products, arithmetic and copies ran while one was open for 1% -> 1% of each run, Pallas kernels for 12% -> 11%
where the time goes in v8:
time: 138 us
  starting transfers between devices  42.6 us (31%)
  waiting for transfers between devices  33.1 us (24%)
  Pallas kernels  29.1 us (21%)
  blocking collectives  22 us (16%)
  local copies, waits for them, and re-layouts  10.4 us (8%)
    ppermute x19, starting transfers between devices, shift(): return lax.ppermute(value, AXES, pairs)  29.8 us
    pallas_call x13, Pallas kernels, call(): pl.pallas_call(kernel, out_shape=outs, in_specs=spaces or [VMEM] * len(ar...  29.1 us
    all_to_all x1, blocking collectives, body(): lax.all_to_all(payload, AXES, split_axis=1, concat_axis=1, tiled=True)  22 us
    ppermute x19, waiting for transfers between devices, shift(): return lax.ppermute(value, AXES, pairs)  21.7 us
    all_to_all x1, waiting for transfers between devices, along_y(): lax.all_to_all(value, 'tile', split_axis=0, concat_axis=0, axis_index_gro...  11.4 us
    unnamed x50, local copies, waits for them, and re-layouts  8.4 us
    all_to_all x1, starting transfers between devices, along_y(): lax.all_to_all(value, 'tile', split_axis=0, concat_axis=0, axis_index_gro...  4.31 us
    all_to_all x1, starting transfers between devices, body(): lax.all_to_all(far_parts, 'seq', split_axis=0, concat_axis=0, tiled=True)  4.23 us
  transfers between devices with their start and end apart: 22, of which 7 were waited for; matrix products, arithmetic and copies ran while one was open for 1% of the time, Pallas kernels for 11%

profile of v8, /device:TPU:1, one launch (start us, length us, event | category | flops | bytes accessed | tf_op | source)
XLA Modules:
  0.0 137.6 jit_solution(6454510080414809955)
XLA Ops:
  0.0 2.4 %shard_map.136 = (bf16[2304,256]{1,0:T(8,128)(2,1)}, bf16[576,256]{1,0:T(8,128)(2,1)}) custom-call(bf16[1536,256]{1,0:T(8,128)(2,1)} %gate_ref.3, bf16[1536,256]{1,0:T(8,128)(2,1)} %up_ref.3, bf16[256,1536]{1,0:T(8,128)(2,1)} %down_ref.3), custom_call_target="tpu_custom_call" | custom-call | flops 1024 | bytes 3833856 | tf_op jit(solution)/shard_map/pallas_call | solution.py:54
  2.5 4.5 %collective-permute-start = (bf16[576,256]{1,0:T(8,128)(2,1)}, bf16[576,256]{1,0:T(8,128)(2,1)S(1)}, u32[]{:S(2)}, u32[]{:S(2)}) collective-permute-start(bf16[576,256]{1,0:T(8,128)(2,1)} %get-tuple-element.51), channel_id=1, source_target_pairs={{0,64},{1,65},{2,66},{3,67},{4,68},{5,69},{6,70},{7,71},{8,72},{9,... | collective-permute-start | bytes 884744 | tf_op jit(solution)/shard_map/ppermute | solution.py:43
  8.5 1.5 %shard_map.137 = bf16[512,1536]{1,0:T(8,128)(2,1)} custom-call(bf16[128,1536]{1,0:T(8,128)(2,1)S(1)} %copy-done.6, f32[1,1536]{1,0:T(1,128)S(1)} %broadcast_in_dim.22.gain_ref), custom_call_target="tpu_custom_call" | custom-call | flops 1024 | bytes 1972224 | tf_op jit(solution)/shard_map/pallas_call | solution.py:54
  10.0 4.3 %all-to-all-start = ((bf16[4,128,1536]{2,1,0:T(8,128)(2,1)}), bf16[4,128,1536]{2,1,0:T(8,128)(2,1)S(1)}, u32[]{:S(2)}, u32[]{:S(2)}) async-start(bf16[4,128,1536]{2,1,0:T(8,128)(2,1)} %bitcast), calls=%async_computation | async-start | bytes 3145728 | tf_op jit(solution)/shard_map/all_to_all | solution.py:48
  15.1 1.9 %collective-permute-start.6 = (bf16[2304,256]{1,0:T(8,128)(2,1)}, bf16[2304,256]{1,0:T(8,128)(2,1)}, u32[]{:S(2)}, u32[]{:S(2)}) collective-permute-start(bf16[2304,256]{1,0:T(8,128)(2,1)} %get-tuple-element.58), channel_id=1, source_target_pairs={{0,96},{1,97},{2,98},{3,99},{4,100},{5,101},{6,102},{7,103},{8,104... | collective-permute-start | bytes 3538952 | tf_op jit(solution)/shard_map/ppermute | solution.py:43
  17.0 2.7 %collective-permute-start.1 = (bf16[576,256]{1,0:T(8,128)(2,1)S(1)}, bf16[576,256]{1,0:T(8,128)(2,1)}, u32[]{:S(2)}, u32[]{:S(2)}) collective-permute-start(bf16[576,256]{1,0:T(8,128)(2,1)S(1)} %collective-permute-done.q0), channel_id=1, source_target_pairs={{0,4},{1,5},{2,6},{3,7},{4,0},{5,1},{6,2},{7,3},{8,12},{9,13},{10,... | collective-permute-start | bytes 884744 | tf_op jit(solution)/shard_map/ppermute | solution.py:43
  20.1 2.4 %collective-permute-start.3 = (bf16[576,256]{1,0:T(8,128)(2,1)S(1)}, bf16[576,256]{1,0:T(8,128)(2,1)}, u32[]{:S(2)}, u32[]{:S(2)}) collective-permute-start(bf16[576,256]{1,0:T(8,128)(2,1)S(1)} %collective-permute-done.q0), channel_id=1, source_target_pairs={{0,6},{1,7},{2,0},{3,1},{4,2},{5,3},{6,4},{7,5},{8,14},{9,15},{10,... | collective-permute-start | bytes 884744 | tf_op jit(solution)/shard_map/ppermute | solution.py:43
  22.4 11.4 %all-to-all-done = bf16[4,128,1536]{2,1,0:T(8,128)(2,1)S(1)} async-done(((bf16[4,128,1536]{2,1,0:T(8,128)(2,1)}), bf16[4,128,1536]{2,1,0:T(8,128)(2,1)S(1)}, u32[]{:S(2)}, u32[]{:S(2)}) %all-to-all-start) | async-done | bytes 1572896 | tf_op jit(solution)/shard_map/all_to_all | solution.py:48
  35.0 1.4 %shard_map.138.total_ref = f32[512,1536]{1,0:T(8,128)S(1)} custom-call(bf16[512,1536]{1,0:T(8,128)(2,1)S(1)} %bitcast.9, bf16[1536,256]{1,0:T(8,128)(2,1)S(1)} %copy-done.1, bf16[1536,256]{1,0:T(8,128)(2,1)S(1)} %copy-done.2, bf16[256,1536]{1,0:T(8,128)(2,1)S(1)} %copy-done.3), custom_call_target="tpu_custom_call" | custom-call | flops 1024 | bytes 7077888 | tf_op jit(solution)/shard_map/pallas_call | solution.py:54
  37.6 2.2 %collective-permute-start.4 = (bf16[2304,256]{1,0:T(8,128)(2,1)S(1)}, bf16[2304,256]{1,0:T(8,128)(2,1)S(1)}, u32[]{:S(2)}, u32[]{:S(2)}) collective-permute-start(bf16[2304,256]{1,0:T(8,128)(2,1)S(1)} %shard_map.139.a), channel_id=1, source_target_pairs={{0,1},{1,0},{2,3},{3,2},{4,5},{5,4},{6,7},{7,6},{8,9},{9,8},{10,11... | collective-permute-start | bytes 3538952 | tf_op jit(solution)/shard_map/ppermute | solution.py:43
  39.9 2.2 %collective-permute-done.5.c = bf16[2304,256]{1,0:T(8,128)(2,1)} collective-permute-done((bf16[2304,256]{1,0:T(8,128)(2,1)}, bf16[2304,256]{1,0:T(8,128)(2,1)}, u32[]{:S(2)}, u32[]{:S(2)}) %collective-permute-start.5) | collective-permute-done | bytes 1179680 | tf_op jit(solution)/shard_map/ppermute | solution.py:43
  42.1 2.2 %collective-permute-start.7 = (bf16[2304,256]{1,0:T(8,128)(2,1)}, bf16[2304,256]{1,0:T(8,128)(2,1)S(1)}, u32[]{:S(2)}, u32[]{:S(2)}) collective-permute-start(bf16[2304,256]{1,0:T(8,128)(2,1)} %collective-permute-done.5.c), channel_id=1, source_target_pairs={{0,1},{1,0},{2,3},{3,2},{4,5},{5,4},{6,7},{7,6},{8,9},{9,8},{10,11... | collective-permute-start | bytes 3538952 | tf_op jit(solution)/shard_map/ppermute | solution.py:43
  44.2 4.3 %shard_map.140.total_ref = f32[512,1536]{1,0:T(8,128)S(1)} custom-call(bf16[512,1536]{1,0:T(8,128)(2,1)S(1)} %bitcast.10, f32[512,1536]{1,0:T(8,128)S(1)} %shard_map.138.total_ref, bf16[2304,256]{1,0:T(8,128)(2,1)S(1)} %shard_map.139.a, bf16[2304,256]{1,0:T(8,128)(2,1)S(1)} %collective-permute-done.4.b, bf16[2304,256]{1,0:T(8,128)(2,1)} %collective-permute-done.5.c, ...), custom_call_target="tpu_custom_call" | custom-call | flops 1024 | bytes 12582912 | tf_op jit(solution)/shard_map/pallas_call | solution.py:54
  48.6 1.8 %shard_map.141 = (f32[128,1536]{1,0:T(8,128)S(1)}, bf16[128,1536]{1,0:T(8,128)(2,1)S(1)}, bf16[128,1536]{1,0:T(8,128)(2,1)S(1)}, bf16[128,1536]{1,0:T(8,128)(2,1)S(1)}) custom-call(bf16[512,1536]{1,0:T(8,128)(2,1)S(1)} %bitcast.11, f32[512,1536]{1,0:T(8,128)S(1)} %shard_map.140.total_ref, bf16[2304,256]{1,0:T(8,128)(2,1)S(1)} %collective-permute-done.7.a, ...), custom_call_target="tpu_custom_call" | custom-call | flops 1024 | bytes 9043968 | tf_op jit(solution)/shard_map/pallas_call | solution.py:54
  50.4 3.0 %collective-permute-start.10 = (bf16[128,1536]{1,0:T(8,128)(2,1)S(1)}, bf16[128,1536]{1,0:T(8,128)(2,1)S(1)}, u32[]{:S(2)}, u32[]{:S(2)}) collective-permute-start(bf16[128,1536]{1,0:T(8,128)(2,1)S(1)} %get-tuple-element.62), channel_id=1, source_target_pairs={{0,16},{1,17},{2,18},{3,19},{4,20},{5,21},{6,22},{7,23},{8,24},{9,... | collective-permute-start | bytes 1179656 | tf_op jit(solution)/shard_map/ppermute | solution.py:43
  53.7 2.4 %collective-permute-start.9 = (bf16[128,1536]{1,0:T(8,128)(2,1)S(1)}, bf16[128,1536]{1,0:T(8,128)(2,1)S(1)}, u32[]{:S(2)}, u32[]{:S(2)}) collective-permute-start(bf16[128,1536]{1,0:T(8,128)(2,1)S(1)} %get-tuple-element.61), channel_id=1, source_target_pairs={{0,24},{1,25},{2,26},{3,27},{4,28},{5,29},{6,30},{7,31},{8,0},{9,1... | collective-permute-start | bytes 1179656 | tf_op jit(solution)/shard_map/ppermute | solution.py:43
  56.2 6.0 %collective-permute-done.10.b = bf16[128,1536]{1,0:T(8,128)(2,1)S(1)} collective-permute-done((bf16[128,1536]{1,0:T(8,128)(2,1)S(1)}, bf16[128,1536]{1,0:T(8,128)(2,1)S(1)}, u32[]{:S(2)}, u32[]{:S(2)}) %collective-permute-start.10) | collective-permute-done | bytes 393248 | tf_op jit(solution)/shard_map/ppermute | solution.py:43
  62.2 9.2 %collective-permute-done.11.c = bf16[128,1536]{1,0:T(8,128)(2,1)S(1)} collective-permute-done((bf16[128,1536]{1,0:T(8,128)(2,1)S(1)}, bf16[128,1536]{1,0:T(8,128)(2,1)S(1)}, u32[]{:S(2)}, u32[]{:S(2)}) %collective-permute-start.11) | collective-permute-done | bytes 393248 | tf_op jit(solution)/shard_map/ppermute | solution.py:43
  73.2 22.0 %all_to_all.38 = bf16[2,128,896]{2,0,1:T(2,128)(2,1)S(1)} all-to-all(bf16[2,128,896]{2,0,1:T(2,128)(2,1)S(1)} %copy.15), channel_id=1, replica_groups=mesh['tile'=16,'seq'=8] {'tile','seq'}, dimensions={1} | all-to-all | bytes 917504 | tf_op jit(solution)/shard_map/all_to_all | solution.py:429
  95.2 2.1 %shard_map.144 = (bf16[136,768]{1,0:T(8,128)(2,1)}, bf16[128,1536]{1,0:T(8,128)(2,1)S(1)}, f32[128,768]{1,0:T(8,128)S(1)}) custom-call(bf16[256,896]{1,0:T(8,128)(2,1)S(1)} %bitcast.13, f32[1,768]{1,0:T(1,128)S(1)} %copy-done.17, f32[1,768]{1,0:T(1,128)S(1)} %broadcast_in_dim.21.gain_ref, bf16[768,2304]{1,0:T(8,128)(2,1)S(1)} %copy-done, ...), custom_call_target="tpu_custom_call" | custom-call | flops 1024 | bytes 5002240 | tf_op jit(solution)/shard_map/pallas_call | solution.py:54
  100.4 2.2 %collective-permute-start.17 = (bf16[136,768]{1,0:T(8,128)(2,1)}, bf16[136,768]{1,0:T(8,128)(2,1)}, u32[]{:S(2)}, u32[]{:S(2)}) collective-permute-start(bf16[136,768]{1,0:T(8,128)(2,1)} %get-tuple-element.72.b0), channel_id=1, source_target_pairs={{0,6},{1,7},{2,0},{3,1},{4,2},{5,3},{6,4},{7,5},{8,14},{9,15},{10,... | collective-permute-start | bytes 626696 | tf_op jit(solution)/shard_map/ppermute | solution.py:43
  102.6 4.2 %all-to-all-start.2 = ((bf16[16,8,1536]{2,1,0:T(8,128)(2,1)}), bf16[16,8,1536]{2,1,0:T(8,128)(2,1)}, u32[]{:S(2)}, u32[]{:S(2)}) async-start(bf16[16,8,1536]{2,1,0:T(8,128)(2,1)} %bitcast.15), calls=%async_computation.2 | async-start | bytes 786432 | tf_op jit(solution)/shard_map/all_to_all | solution.py:440
  106.8 1.3 collective-permute-start.12
  108.1 1.5 %collective-permute-start.14 = (bf16[136,768]{1,0:T(8,128)(2,1)}, bf16[136,768]{1,0:T(8,128)(2,1)S(1)}, u32[]{:S(2)}, u32[]{:S(2)}) collective-permute-start(bf16[136,768]{1,0:T(8,128)(2,1)} %collective-permute-done.13.b2), channel_id=1, source_target_pairs={{0,1},{1,0},{2,3},{3,2},{4,5},{5,4},{6,7},{7,6},{8,9},{9,8},{10,11... | collective-permute-start | bytes 626696 | tf_op jit(solution)/shard_map/ppermute | solution.py:43
  109.6 2.6 %collective-permute-done.15.b4 = bf16[136,768]{1,0:T(8,128)(2,1)} collective-permute-done((bf16[136,768]{1,0:T(8,128)(2,1)}, bf16[136,768]{1,0:T(8,128)(2,1)}, u32[]{:S(2)}, u32[]{:S(2)}) %collective-permute-start.15) | collective-permute-done | bytes 208928 | tf_op jit(solution)/shard_map/ppermute | solution.py:43
  112.7 1.3 collective-permute-done.16.b5
  114.4 1.3 shard_map.145
  118.4 2.6 %shard_map.147 = f32[64,896]{1,0:T(8,128)S(1)} custom-call(bf16[64,768]{1,0:T(8,128)(2,1)S(1)} %copy-done.14, bf16[128,1536]{1,0:T(8,128)(2,1)} %bitcast.6.kv_ref), custom_call_target="tpu_custom_call" | custom-call | flops 1024 | bytes 720896 | tf_op jit(solution)/shard_map/pallas_call | solution.py:54
  121.7 4.2 %all-to-all-start.3 = ((f32[8,8,896]{2,1,0:T(8,128)}), f32[8,8,896]{2,1,0:T(8,128)}, u32[]{:S(2)}, u32[]{:S(2)}) async-start(f32[8,8,896]{2,1,0:T(8,128)} %bitcast.14), calls=%async_computation.3 | async-start | bytes 458752 | tf_op jit(solution)/shard_map/all_to_all | solution.py:449
  125.9 1.4 %copy-done.9 = bf16[1024,768]{1,0:T(8,128)(2,1)S(1)} copy-done((bf16[1024,768]{1,0:T(8,128)(2,1)S(1)}, bf16[1024,768]{1,0:T(8,128)(2,1)}, u32[]{:S(2)}) %copy-start.9) | copy-done | bytes 1572888
  127.3 5.7 %shard_map.146.near = f32[6,128,256]{2,1,0:T(8,128)S(1)} custom-call(bf16[1024,768]{1,0:T(8,128)(2,1)S(1)} %copy-done.9, bf16[768,2304]{1,0:T(8,128)(2,1)S(1)} %copy-done), custom_call_target="tpu_custom_call" | custom-call | flops 1024 | bytes 5898240 | tf_op jit(solution)/shard_map/pallas_call | solution.py:54
  134.0 3.5 %shard_map.148 = bf16[128,768]{1,0:T(8,128)(2,1)} custom-call(f32[6,128,256]{2,1,0:T(8,128)} %copy-done.4, f32[64,896]{1,0:T(8,128)} %bitcast.8.far, f32[128,768]{1,0:T(8,128)} %copy-done.12, s32[1,768]{1,0:T(1,128)} %copy-done.15, bf16[768,768]{1,0:T(8,128)(2,1)} %w.1), custom_call_target="tpu_custom_call" | custom-call | flops 1024 | bytes 2788352 | tf_op jit(solution)/shard_map/pallas_call | solution.py:54
  (87 shorter events, 15.4 us)
Async XLA Ops:
  0.0 7.8 %copy-start.23 = (f32[768]{0:T(1024)S(1)}, f32[768]{0:T(1024)}, u32[]{:S(2)}) copy-start(f32[768]{0:T(1024)} %param.24) | copy-start | bytes 9220
  0.0 8.5 %copy-start.6 = (bf16[128,1536]{1,0:T(8,128)(2,1)S(1)}, bf16[128,1536]{1,0:T(8,128)(2,1)}, u32[]{:S(2)}) copy-start(bf16[128,1536]{1,0:T(8,128)(2,1)} %tokens_ref) | copy-start | bytes 1179652
  2.5 11.8 %collective-permute-start = (bf16[576,256]{1,0:T(8,128)(2,1)}, bf16[576,256]{1,0:T(8,128)(2,1)S(1)}, u32[]{:S(2)}, u32[]{:S(2)}) collective-permute-start(bf16[576,256]{1,0:T(8,128)(2,1)} %get-tuple-element.51), channel_id=1, source_target_pairs={{0,64},{1,65},{2,66},{3,67},{4,68},{5,69},{6,70},{7,71},{8,72},{9,... | collective-permute-start | bytes 884744 | tf_op jit(solution)/shard_map/ppermute | solution.py:43
  7.2 88.0 %copy-start.15 = (s32[1,768]{1,0:T(1,128)}, s32[1,768]{1,0:T(1,128)S(1)}, u32[]{:S(2)}) copy-start(s32[1,768]{1,0:T(1,128)S(1)} %broadcast_in_dim_reshape.3.offsets_ref) | copy-start | bytes 9220
  10.0 23.8 %copy-start.1 = (bf16[1536,256]{1,0:T(8,128)(2,1)S(1)}, bf16[1536,256]{1,0:T(8,128)(2,1)}, u32[]{:S(2)}) copy-start(bf16[1536,256]{1,0:T(8,128)(2,1)} %gate_ref.3) | copy-start | bytes 2359300
  10.0 23.8 %copy-start.2 = (bf16[1536,256]{1,0:T(8,128)(2,1)S(1)}, bf16[1536,256]{1,0:T(8,128)(2,1)}, u32[]{:S(2)}) copy-start(bf16[1536,256]{1,0:T(8,128)(2,1)} %up_ref.3) | copy-start | bytes 2359300
  10.0 23.8 %all-to-all-start = ((bf16[4,128,1536]{2,1,0:T(8,128)(2,1)}), bf16[4,128,1536]{2,1,0:T(8,128)(2,1)S(1)}, u32[]{:S(2)}, u32[]{:S(2)}) async-start(bf16[4,128,1536]{2,1,0:T(8,128)(2,1)} %bitcast), calls=%async_computation | async-start | bytes 3145728 | tf_op jit(solution)/shard_map/all_to_all | solution.py:48
  14.3 27.7 %collective-permute-start.5 = (bf16[2304,256]{1,0:T(8,128)(2,1)}, bf16[2304,256]{1,0:T(8,128)(2,1)}, u32[]{:S(2)}, u32[]{:S(2)}) collective-permute-start(bf16[2304,256]{1,0:T(8,128)(2,1)} %get-tuple-element.58), channel_id=1, source_target_pairs={{0,32},{1,33},{2,34},{3,35},{4,36},{5,37},{6,38},{7,39},{8,40},{9,... | collective-permute-start | bytes 3538952 | tf_op jit(solution)/shard_map/ppermute | solution.py:43
  15.1 29.2 %collective-permute-start.6 = (bf16[2304,256]{1,0:T(8,128)(2,1)}, bf16[2304,256]{1,0:T(8,128)(2,1)}, u32[]{:S(2)}, u32[]{:S(2)}) collective-permute-start(bf16[2304,256]{1,0:T(8,128)(2,1)} %get-tuple-element.58), channel_id=1, source_target_pairs={{0,96},{1,97},{2,98},{3,99},{4,100},{5,101},{6,102},{7,103},{8,104... | collective-permute-start | bytes 3538952 | tf_op jit(solution)/shard_map/ppermute | solution.py:43
  17.0 19.4 %collective-permute-start.1 = (bf16[576,256]{1,0:T(8,128)(2,1)S(1)}, bf16[576,256]{1,0:T(8,128)(2,1)}, u32[]{:S(2)}, u32[]{:S(2)}) collective-permute-start(bf16[576,256]{1,0:T(8,128)(2,1)S(1)} %collective-permute-done.q0), channel_id=1, source_target_pairs={{0,4},{1,5},{2,6},{3,7},{4,0},{5,1},{6,2},{7,3},{8,12},{9,13},{10,... | collective-permute-start | bytes 884744 | tf_op jit(solution)/shard_map/ppermute | solution.py:43
  19.7 16.6 %collective-permute-start.2 = (bf16[576,256]{1,0:T(8,128)(2,1)S(1)}, bf16[576,256]{1,0:T(8,128)(2,1)}, u32[]{:S(2)}, u32[]{:S(2)}) collective-permute-start(bf16[576,256]{1,0:T(8,128)(2,1)S(1)} %collective-permute-done.q0), channel_id=1, source_target_pairs={{0,2},{1,3},{2,4},{3,5},{4,6},{5,7},{6,0},{7,1},{8,10},{9,11},{10,... | collective-permute-start | bytes 884744 | tf_op jit(solution)/shard_map/ppermute | solution.py:43
  20.1 16.3 %collective-permute-start.3 = (bf16[576,256]{1,0:T(8,128)(2,1)S(1)}, bf16[576,256]{1,0:T(8,128)(2,1)}, u32[]{:S(2)}, u32[]{:S(2)}) collective-permute-start(bf16[576,256]{1,0:T(8,128)(2,1)S(1)} %collective-permute-done.q0), channel_id=1, source_target_pairs={{0,6},{1,7},{2,0},{3,1},{4,2},{5,3},{6,4},{7,5},{8,14},{9,15},{10,... | collective-permute-start | bytes 884744 | tf_op jit(solution)/shard_map/ppermute | solution.py:43
  37.6 6.6 %collective-permute-start.4 = (bf16[2304,256]{1,0:T(8,128)(2,1)S(1)}, bf16[2304,256]{1,0:T(8,128)(2,1)S(1)}, u32[]{:S(2)}, u32[]{:S(2)}) collective-permute-start(bf16[2304,256]{1,0:T(8,128)(2,1)S(1)} %shard_map.139.a), channel_id=1, source_target_pairs={{0,1},{1,0},{2,3},{3,2},{4,5},{5,4},{6,7},{7,6},{8,9},{9,8},{10,11... | collective-permute-start | bytes 3538952 | tf_op jit(solution)/shard_map/ppermute | solution.py:43
  42.1 6.5 %collective-permute-start.7 = (bf16[2304,256]{1,0:T(8,128)(2,1)}, bf16[2304,256]{1,0:T(8,128)(2,1)S(1)}, u32[]{:S(2)}, u32[]{:S(2)}) collective-permute-start(bf16[2304,256]{1,0:T(8,128)(2,1)} %collective-permute-done.5.c), channel_id=1, source_target_pairs={{0,1},{1,0},{2,3},{3,2},{4,5},{5,4},{6,7},{7,6},{8,9},{9,8},{10,11... | collective-permute-start | bytes 3538952 | tf_op jit(solution)/shard_map/ppermute | solution.py:43
  44.2 4.4 %collective-permute-start.8 = (bf16[2304,256]{1,0:T(8,128)(2,1)}, bf16[2304,256]{1,0:T(8,128)(2,1)S(1)}, u32[]{:S(2)}, u32[]{:S(2)}) collective-permute-start(bf16[2304,256]{1,0:T(8,128)(2,1)} %collective-permute-done.6.d), channel_id=1, source_target_pairs={{0,1},{1,0},{2,3},{3,2},{4,5},{5,4},{6,7},{7,6},{8,9},{9,8},{10,11... | collective-permute-start | bytes 3538952 | tf_op jit(solution)/shard_map/ppermute | solution.py:43
  48.5 22.9 %copy-start.7 = (bf16[128,1536]{1,0:T(8,128)(2,1)S(1)}, bf16[128,1536]{1,0:T(8,128)(2,1)}, u32[]{:S(2)}) copy-start(bf16[128,1536]{1,0:T(8,128)(2,1)} %tokens_ref) | copy-start | bytes 1179652
  48.5 22.9 %copy-start.16 = (f32[1,1536]{1,0:T(1,128)S(1)}, f32[1,1536]{1,0:T(1,128)}, u32[]{:S(2)}) copy-start(f32[1,1536]{1,0:T(1,128)} %broadcast_in_dim.20.gain_ref) | copy-start | bytes 18436
  48.6 22.9 %copy-start.5 = (bf16[1536,768]{1,0:T(8,128)(2,1)S(1)}, bf16[1536,768]{1,0:T(8,128)(2,1)}, u32[]{:S(2)}) copy-start(bf16[1536,768]{1,0:T(8,128)(2,1)} %w_ref.3) | copy-start | bytes 7077892
  50.4 11.8 %collective-permute-start.10 = (bf16[128,1536]{1,0:T(8,128)(2,1)S(1)}, bf16[128,1536]{1,0:T(8,128)(2,1)S(1)}, u32[]{:S(2)}, u32[]{:S(2)}) collective-permute-start(bf16[128,1536]{1,0:T(8,128)(2,1)S(1)} %get-tuple-element.62), channel_id=1, source_target_pairs={{0,16},{1,17},{2,18},{3,19},{4,20},{5,21},{6,22},{7,23},{8,24},{9,... | collective-permute-start | bytes 1179656 | tf_op jit(solution)/shard_map/ppermute | solution.py:43
  53.4 18.0 %collective-permute-start.11 = (bf16[128,1536]{1,0:T(8,128)(2,1)S(1)}, bf16[128,1536]{1,0:T(8,128)(2,1)S(1)}, u32[]{:S(2)}, u32[]{:S(2)}) collective-permute-start(bf16[128,1536]{1,0:T(8,128)(2,1)S(1)} %get-tuple-element.63), channel_id=1, source_target_pairs={{0,8},{1,9},{2,10},{3,11},{4,12},{5,13},{6,14},{7,15},{8,16},{9,17... | collective-permute-start | bytes 1179656 | tf_op jit(solution)/shard_map/ppermute | solution.py:43
  53.7 17.7 %collective-permute-start.9 = (bf16[128,1536]{1,0:T(8,128)(2,1)S(1)}, bf16[128,1536]{1,0:T(8,128)(2,1)S(1)}, u32[]{:S(2)}, u32[]{:S(2)}) collective-permute-start(bf16[128,1536]{1,0:T(8,128)(2,1)S(1)} %get-tuple-element.61), channel_id=1, source_target_pairs={{0,24},{1,25},{2,26},{3,27},{4,28},{5,29},{6,30},{7,31},{8,0},{9,1... | collective-permute-start | bytes 1179656 | tf_op jit(solution)/shard_map/ppermute | solution.py:43
  71.5 23.7 %copy-start = (bf16[768,2304]{1,0:T(8,128)(2,1)S(1)}, bf16[768,2304]{1,0:T(8,128)(2,1)}, u32[]{:S(2)}) copy-start(bf16[768,2304]{1,0:T(8,128)(2,1)} %w_ref.5) | copy-start | bytes 10616836
  72.7 22.5 %copy-start.17 = (f32[1,768]{1,0:T(1,128)S(1)}, f32[1,768]{1,0:T(1,128)}, u32[]{:S(2)}) copy-start(f32[1,768]{1,0:T(1,128)} %broadcast_in_dim_tile.3.frequency_ref) | copy-start | bytes 9220
  98.8 9.3 %collective-permute-start.13 = (bf16[136,768]{1,0:T(8,128)(2,1)}, bf16[136,768]{1,0:T(8,128)(2,1)}, u32[]{:S(2)}, u32[]{:S(2)}) collective-permute-start(bf16[136,768]{1,0:T(8,128)(2,1)} %get-tuple-element.72.b0), channel_id=1, source_target_pairs={{0,4},{1,5},{2,6},{3,7},{4,0},{5,1},{6,2},{7,3},{8,12},{9,13},{10,... | collective-permute-start | bytes 626696 | tf_op jit(solution)/shard_map/ppermute | solution.py:43
  99.9 12.3 %collective-permute-start.15 = (bf16[136,768]{1,0:T(8,128)(2,1)}, bf16[136,768]{1,0:T(8,128)(2,1)}, u32[]{:S(2)}, u32[]{:S(2)}) collective-permute-start(bf16[136,768]{1,0:T(8,128)(2,1)} %get-tuple-element.72.b0), channel_id=1, source_target_pairs={{0,2},{1,3},{2,4},{3,5},{4,6},{5,7},{6,0},{7,1},{8,10},{9,11},{10,... | collective-permute-start | bytes 626696 | tf_op jit(solution)/shard_map/ppermute | solution.py:43
  100.4 12.3 %collective-permute-start.17 = (bf16[136,768]{1,0:T(8,128)(2,1)}, bf16[136,768]{1,0:T(8,128)(2,1)}, u32[]{:S(2)}, u32[]{:S(2)}) collective-permute-start(bf16[136,768]{1,0:T(8,128)(2,1)} %get-tuple-element.72.b0), channel_id=1, source_target_pairs={{0,6},{1,7},{2,0},{3,1},{4,2},{5,3},{6,4},{7,5},{8,14},{9,15},{10,... | collective-permute-start | bytes 626696 | tf_op jit(solution)/shard_map/ppermute | solution.py:43
  102.6 15.0 %all-to-all-start.2 = ((bf16[16,8,1536]{2,1,0:T(8,128)(2,1)}), bf16[16,8,1536]{2,1,0:T(8,128)(2,1)}, u32[]{:S(2)}, u32[]{:S(2)}) async-start(bf16[16,8,1536]{2,1,0:T(8,128)(2,1)} %bitcast.15), calls=%async_computation.2 | async-start | bytes 786432 | tf_op jit(solution)/shard_map/all_to_all | solution.py:440
  106.8 5.9 %collective-permute-start.12 = (bf16[136,768]{1,0:T(8,128)(2,1)}, bf16[136,768]{1,0:T(8,128)(2,1)S(1)}, u32[]{:S(2)}, u32[]{:S(2)}) collective-permute-start(bf16[136,768]{1,0:T(8,128)(2,1)} %get-tuple-element.72.b0), channel_id=1, source_target_pairs={{0,1},{1,0},{2,3},{3,2},{4,5},{5,4},{6,7},{7,6},{8,9},{9,8},{10,11... | collective-permute-start | bytes 626696 | tf_op jit(solution)/shard_map/ppermute | solution.py:43
  108.1 4.6 %collective-permute-start.14 = (bf16[136,768]{1,0:T(8,128)(2,1)}, bf16[136,768]{1,0:T(8,128)(2,1)S(1)}, u32[]{:S(2)}, u32[]{:S(2)}) collective-permute-start(bf16[136,768]{1,0:T(8,128)(2,1)} %collective-permute-done.13.b2), channel_id=1, source_target_pairs={{0,1},{1,0},{2,3},{3,2},{4,5},{5,4},{6,7},{7,6},{8,9},{9,8},{10,11... | collective-permute-start | bytes 626696 | tf_op jit(solution)/shard_map/ppermute | solution.py:43
  112.2 1.8 %collective-permute-start.16 = (bf16[136,768]{1,0:T(8,128)(2,1)}, bf16[136,768]{1,0:T(8,128)(2,1)S(1)}, u32[]{:S(2)}, u32[]{:S(2)}) collective-permute-start(bf16[136,768]{1,0:T(8,128)(2,1)} %collective-permute-done.15.b4), channel_id=1, source_target_pairs={{0,1},{1,0},{2,3},{3,2},{4,5},{5,4},{6,7},{7,6},{8,9},{9,8},{10,11... | collective-permute-start | bytes 626696 | tf_op jit(solution)/shard_map/ppermute | solution.py:43
  112.7 1.7 %collective-permute-start.18 = (bf16[136,768]{1,0:T(8,128)(2,1)}, bf16[136,768]{1,0:T(8,128)(2,1)S(1)}, u32[]{:S(2)}, u32[]{:S(2)}) collective-permute-start(bf16[136,768]{1,0:T(8,128)(2,1)} %collective-permute-done.17.b6), channel_id=1, source_target_pairs={{0,1},{1,0},{2,3},{3,2},{4,5},{5,4},{6,7},{7,6},{8,9},{9,8},{10,11... | collective-permute-start | bytes 626696 | tf_op jit(solution)/shard_map/ppermute | solution.py:43
  121.7 12.3 %all-to-all-start.3 = ((f32[8,8,896]{2,1,0:T(8,128)}), f32[8,8,896]{2,1,0:T(8,128)}, u32[]{:S(2)}, u32[]{:S(2)}) async-start(f32[8,8,896]{2,1,0:T(8,128)} %bitcast.14), calls=%async_computation.3 | async-start | bytes 458752 | tf_op jit(solution)/shard_map/all_to_all | solution.py:449
  (15 other events, 52.7 us)
